TPU v7x, 256 devices: a whole 4x4x8 slice. The times are simulated.
256 devices in a mesh: row: 8 (over y, x_hi), col: 8 (over z), rep: 4 (over x_lo, core).
Axes of the slice: x: 4 (x_hi: 2, x_lo: 2; x = x_hi * 2 + x_lo), y: 4, z: 8, core: 2. Of those that a mesh axis runs over, the one named last changes fastest.
Arguments:
- hidden: bfloat16 [2048, 28672], P('rep', 'col'), may hold values from -0.13183594 to 0.13183594
- grad_out: bfloat16 [2048, 8192], P('rep', 'row'), may hold values from -6 to 6
- weight: bfloat16 [28672, 8192], P('col', ('row', 'rep')), may hold values from -0.03125 to 0.03125
Outputs:
- grad_hidden: bfloat16 [2048, 28672], P('rep', 'col')
- grad_weight: bfloat16 [28672, 8192], P('col', ('row', 'rep'))
- left_stats: float32 [56, 512, 512], P('col', ('row', 'rep'))
- right_stats: float32 [8192, 512], P(('row', 'rep'), 'col')
All inputs are finite; a program needn't handle non-finite values.
Results may differ from a plain program's by a relative error of at most 0.017.
Values may be sent and summed in bfloat16 or wider, within the bound.
No kernel may reach another device: no remote copies, remote signals or barrier semaphores. Data moves between devices by JAX's collectives and lax.ppermute only.
A program may use at most 128 MiB of HBM per device.

v0:
```python
import jax
import jax.numpy as jnp
from jax import lax
from jax.sharding import PartitionSpec as P

D = 8192
FF = 28672
BLK = 512


def body(hidden, grad_out, weight):
    tile_rows = weight.shape[0]
    slab_width = weight.shape[1]
    num_blocks = tile_rows // BLK
    replica = lax.axis_index("rep")
    width_partial = lax.dot_general(
        grad_out,
        lax.all_gather(weight, "rep", axis=1, tiled=True),
        (((1,), (1,)), ((), ())),
        preferred_element_type=jnp.float32,
    )
    wgrad_term = lax.dot_general(
        hidden, grad_out, (((0,), (0,)), ((), ())), preferred_element_type=jnp.float32
    )
    grad_slab = lax.psum_scatter(
        wgrad_term.astype(jnp.bfloat16), "rep", scatter_dimension=1, tiled=True
    )
    grad_hidden = lax.psum(width_partial.astype(jnp.bfloat16), "row")
    full_tile = lax.all_gather(grad_slab, "rep", axis=1, tiled=True)
    block_start = replica * slab_width // BLK * BLK
    block_cols = lax.dynamic_slice_in_dim(full_tile, block_start, BLK, 1)
    right_partial = lax.dot_general(
        grad_slab, block_cols, (((0,), (0,)), ((), ())), preferred_element_type=jnp.float32
    )
    right_stats = lax.psum_scatter(
        (right_partial / FF).astype(jnp.bfloat16), "col", scatter_dimension=1, tiled=True
    ).astype(jnp.float32)
    slab_blocks = grad_slab.reshape(num_blocks, BLK, slab_width)
    left_partial = (
        jnp.einsum("abd,acd->abc", slab_blocks, slab_blocks, preferred_element_type=jnp.float32) / D
    )
    left_stats = lax.psum_scatter(
        left_partial.astype(jnp.bfloat16), ("row", "rep"), scatter_dimension=1, tiled=True
    ).astype(jnp.float32)
    return (grad_hidden, grad_slab, left_stats, right_stats)


def solution(mesh):
    return jax.shard_map(
        body,
        mesh=mesh,
        in_specs=(P("rep", "col"), P("rep", "row"), P("col", ("row", "rep"))),
        out_specs=(
            P("rep", "col"),
            P("col", ("row", "rep")),
            P("col", ("row", "rep"), None),
            P(("row", "rep"), "col"),
        ),
        check_vma=False,
    )
```

profile of v0, /device:TPU:32, one launch (start us, length us, event | category | flops | bytes accessed | tf_op | source)
XLA Modules:
  0.0 564.7 jit_solution(14728054595562930456)
XLA Ops:
  7.2 0.0 copy-start
  7.2 0.0 reduce-scatter.4.cloned.1.call-start
  7.2 1.2 copy-done
  8.4 8.2 %convolution_convert_fusion = bf16[3584,1024]{1,0:T(8,128)(2,1)} fusion(bf16[512,3584]{1,0:T(8,128)(2,1)} %param.3, bf16[512,1024]{1,0:T(8,128)(2,1)S(1)} %copy-done), kind=kOutput, calls=%fused_computation | convolution fusion | flops 3761766400 | bytes 12058624 | tf_op jit(solution)/shard_map/dot_general | solution.py:22
  16.6 0.0 reduce-scatter.4.cloned.1.call-update
  16.6 0.0 all-gather.5.cloned.1.call-start
  16.6 76.3 %reduce-scatter.4.cloned.1.call-done = bf16[3584,256]{1,0:T(8,128)(2,1)} async-done(((bf16[3584,1024]{1,0:T(8,128)(2,1)}), bf16[3584,256]{1,0:T(8,128)(2,1)}) %reduce-scatter.4.cloned.1.call-update) | async-done | bytes 1835024 | tf_op jit(solution)/shard_map/reduce_scatter | solution.py:25
  92.9 0.0 copy-start.1
  92.9 0.0 all-gather.5.cloned.1.call-update
  93.0 0.0 all-gather.3.cloned.1.call-start
  93.0 0.7 all-gather.3.cloned.1.call-update
  93.7 0.0 reduce-scatter.6.cloned.1.call-start
  93.7 0.7 copy-done.1
  94.4 2.9 multiply_convert_fusion
  97.4 0.0 reduce-scatter.6.cloned.1.call-update
  97.4 0.0 reduce-scatter.8.cloned.1.call-start
  97.5 72.9 %all-gather.5.cloned.1.call-done = bf16[3584,1024]{1,0:T(8,128)(2,1)} async-done(((bf16[3584,256]{1,0:T(8,128)(2,1)}), bf16[3584,1024]{1,0:T(8,128)(2,1)}) %all-gather.5.cloned.1.call-update) | async-done | bytes 7340048 | tf_op jit(solution)/shard_map/all_gather | solution.py:29
  170.4 4.3 fusion.5
  174.7 0.0 reduce-scatter.8.cloned.1.call-update
  174.7 0.0 all-reduce.2.cloned.1.call-start
  174.8 73.5 %all-gather.3.cloned.1.call-done = bf16[3584,1024]{1,0:T(8,128)(2,1)} async-done(((bf16[3584,256]{1,0:T(8,128)(2,1)}), bf16[3584,1024]{1,0:T(8,128)(2,1)}) %all-gather.3.cloned.1.call-update) | async-done | bytes 7340048 | tf_op jit(solution)/shard_map/all_gather | solution.py:18
  248.3 8.5 %convolution_convert_fusion.1 = bf16[512,3584]{1,0:T(8,128)(2,1)} fusion(bf16[512,1024]{1,0:T(8,128)(2,1)S(1)} %copy-done, bf16[3584,1024]{1,0:T(8,128)(2,1)} %all-gather.3.cloned.1.call-done), kind=kOutput, calls=%fused_computation.2 | convolution fusion | flops 3759931392 | bytes 12058624 | tf_op jit(solution)/shard_map/dot_general | solution.py:16
  256.8 0.0 all-reduce.2.cloned.1.call-update
  256.8 86.0 %reduce-scatter.6.cloned.1.call-done = bf16[7,16,512]{2,1,0:T(8,128)(2,1)} async-done(((bf16[7,512,512]{2,1,0:T(8,128)(2,1)}), bf16[7,16,512]{2,1,0:T(8,128)(2,1)}) %reduce-scatter.6.cloned.1.call-update) | async-done | bytes 114704 | tf_op jit(solution)/shard_map/reduce_scatter | solution.py:42
  342.8 1.6 convert_element_type.21
  344.4 36.3 %reduce-scatter.8.cloned.1.call-done = bf16[256,64]{0,1:T(8,128)(2,1)} async-done(((bf16[256,512]{0,1:T(8,128)(2,1)}), bf16[256,64]{0,1:T(8,128)(2,1)}) %reduce-scatter.8.cloned.1.call-update) | async-done | bytes 32784 | tf_op jit(solution)/shard_map/reduce_scatter | solution.py:35
  380.7 1.4 convert_element_type.23
  382.1 171.6 %all-reduce.2.cloned.1.call-done = bf16[512,3584]{1,0:T(8,128)(2,1)} async-done(((bf16[512,3584]{1,0:T(8,128)(2,1)}), bf16[512,3584]{1,0:T(8,128)(2,1)}) %all-reduce.2.cloned.1.call-update) | async-done | bytes 3670032 | tf_op jit(solution)/shard_map/psum | solution.py:28
  553.7 4.1 copy.8
Async XLA Ops:
  7.2 1.2 copy-start
  7.2 85.7 %reduce-scatter.4.cloned.1.call-start = ((), (), s32[]{:S(2)}) async-start(), calls=%async_computation.5 | async-start | bytes 9175040 | tf_op jit(solution)/shard_map/reduce_scatter | solution.py:25
  16.6 153.8 %all-gather.5.cloned.1.call-start = ((), (), s32[]{:S(2)}) async-start(), calls=%async_computation.7 | async-start | bytes 9175040 | tf_op jit(solution)/shard_map/all_gather | solution.py:29
  92.9 1.5 copy-start.1
  93.0 155.3 %all-gather.3.cloned.1.call-start = ((), (), s32[]{:S(2)}) async-start(), calls=%async_computation.3 | async-start | bytes 9175040 | tf_op jit(solution)/shard_map/all_gather | solution.py:18
  93.7 249.1 %reduce-scatter.6.cloned.1.call-start = ((), (), s32[]{:S(2)}) async-start(), calls=%async_computation.6 | async-start | bytes 3784704 | tf_op jit(solution)/shard_map/reduce_scatter | solution.py:42
  97.4 283.4 %reduce-scatter.8.cloned.1.call-start = ((), (), s32[]{:S(2)}) async-start(), calls=%async_computation.8 | async-start | bytes 294912 | tf_op jit(solution)/shard_map/reduce_scatter | solution.py:35
  174.7 379.0 %all-reduce.2.cloned.1.call-start = ((), (), s32[]{:S(2)}) async-start(), calls=%async_computation.4 | async-start | bytes 7340032 | tf_op jit(solution)/shard_map/psum | solution.py:28
Sparse Core Ops, SparseCore 0:
  16.7 76.1 reduce-scatter.3
  95.3 75.0 all-gather.4
  172.2 76.0 all-gather.2
  252.1 90.6 reduce-scatter.5
  345.3 35.3 reduce-scatter.7
  383.8 169.8 all-reduce.1
where the time goes:
time: 566 us; the launch traced here: 565 us
  waiting for transfers between devices  517 us (91%)
  matrix products  23.9 us (4%)
  between operations  14.1 us (2%)
  local copies, waits for them, and re-layouts  5.98 us (1%)
    psum x1, waiting for transfers between devices, body(): grad_hidden = lax.psum(width_partial.astype(jnp.bfloat16), 'row')  172 us
    reduce_scatter x1, waiting for transfers between devices, body(): lax.psum_scatter(left_partial.astype(jnp.bfloat16), ('row', 'rep'), scatt...  86 us
    reduce_scatter x1, waiting for transfers between devices, body(): lax.psum_scatter(wgrad_term.astype(jnp.bfloat16), 'rep', scatter_dimensio...  76.3 us
    all_gather x1, waiting for transfers between devices, body(): lax.all_gather(weight, 'rep', axis=1, tiled=True)  73.5 us
    all_gather x1, waiting for transfers between devices, body(): full_tile = lax.all_gather(grad_slab, 'rep', axis=1, tiled=True)  72.9 us
    reduce_scatter x1, waiting for transfers between devices, body(): lax.psum_scatter((right_partial / FF).astype(jnp.bfloat16), 'col', scatte...  36.3 us
  transfers between devices with their start and end apart: 6, of which 6 were waited for; matrix products, arithmetic and copies ran while one was open for 3% of the time, Pallas kernels for 0%

commit v1 on v0

v1 whole, which is shorter than its diff:
```python
import jax
import jax.numpy as jnp
from jax import lax
from jax.experimental import pallas as pl
from jax.experimental.pallas import tpu as pltpu
from jax.sharding import PartitionSpec as P

D = 8192
FF = 28672
BLK = 512
N_Y = 4
A_CHUNKS = 2
GATHERED_ROWS = 1280
TILE = 256
F32 = jnp.float32
BF16 = jnp.bfloat16

Y, SECOND, FIRST, FAR, SLAB, SLAB_C, SLAB_X, SLAB_XC, CORE_AT, X_LO_AT = range(10)


def plane_perm(move):
    pairs = []
    for at in range(32):
        y, x_hi, x_lo, core = at // 8, at // 4 % 2, at // 2 % 2, at % 2
        y, x_hi, x_lo, core = move(y, x_hi, x_lo, core)
        pairs.append((at, y * 8 + x_hi * 4 + x_lo * 2 + core))
    return pairs


CORE = plane_perm(lambda y, h, l, c: (y, h, l, 1 - c))
X_LO = plane_perm(lambda y, h, l, c: (y, h, 1 - l, c))
X_HI = plane_perm(lambda y, h, l, c: (y, 1 - h, l, c))
X_OUT = plane_perm(lambda y, h, l, c: (y, 1 - h, 1 - l, c))
X_OUT_CORE = plane_perm(lambda y, h, l, c: (y, 1 - h, 1 - l, 1 - c))
Y_FIRST = plane_perm(lambda y, h, l, c: (y ^ (3 if c else 1), h, l, c))
Y_SECOND = plane_perm(lambda y, h, l, c: (y ^ (1 if c else 3), h, l, c))


def send(x, perm):
    return lax.ppermute(x, ("row", "rep"), perm)


def shape(dims, dtype=BF16):
    return jax.ShapeDtypeStruct(dims, dtype)


ANY = pl.BlockSpec(memory_space=pl.ANY)


def call(kernel, at, arrays, in_specs, outs, out_specs, grid=(1,), scratch=(), after=(), aliases=None, vmem=12, cost=1):
    n, m = len(arrays), len(after)

    def run(at_ref, *refs):
        kernel(at_ref, *refs[:n], *refs[n + m:])

    return pl.pallas_call(
        run,
        grid_spec=pltpu.PrefetchScalarGridSpec(
            num_scalar_prefetch=1,
            grid=grid,
            in_specs=list(in_specs) + [ANY] * m,
            out_specs=list(out_specs),
            scratch_shapes=list(scratch),
        ),
        out_shape=list(outs),
        input_output_aliases=aliases or {},
        compiler_params=pltpu.CompilerParams(vmem_limit_bytes=vmem * 2**20),
        cost_estimate=pl.CostEstimate(flops=1, bytes_accessed=cost, transcendentals=0),
    )(at, *arrays, *after)


def copies(at, arrays, outs, plan, count, after=()):
    n = len(arrays)

    def kernel(at_ref, *refs):
        sems = refs[-1]
        moves = [
            pltpu.make_async_copy(src, dst, sems.at[i])
            for i, (src, dst) in enumerate(plan(at_ref, refs[:n], refs[n:-1]))
        ]
        for move in moves:
            move.start()
        for move in moves:
            move.wait()

    return call(
        kernel, at, arrays, [pl.BlockSpec(memory_space=pltpu.HBM)] * n, outs,
        [pl.BlockSpec(out.shape, lambda i, at: (0, 0)) for out in outs],
        scratch=[pltpu.SemaphoreType.DMA((count,))], after=after, vmem=58,
    )


def add(at, arrays, after=()):
    rows, width = arrays[0].shape
    spec = pl.BlockSpec((rows, width // 2), lambda i, at: (0, i))

    def kernel(at_ref, *refs):
        total = refs[0][...].astype(F32)
        for ref in refs[1:-1]:
            total = total + ref[...].astype(F32)
        refs[-1][...] = total.astype(BF16)

    return call(kernel, at, arrays, [spec] * len(arrays), [shape((rows, width))], [spec], (2,), after=after)[0]


def copy_of(at, x, rows=None, after=()):
    rows = rows or x.shape[0]
    spec = pl.BlockSpec((rows // 2, x.shape[1]), lambda i, at: (i, 0))

    def kernel(at_ref, x_ref, out_ref):
        out_ref[...] = x_ref[...]

    return call(kernel, at, [x], [spec], [shape((rows, x.shape[1]))], [spec], (2,), after=after)[0]


def dot(a, b, over_a, over_b):
    return lax.dot_general(a, b, (((over_a,), (over_b,)), ((), ())), preferred_element_type=F32)


def piece(x, at, axis):
    return lax.dynamic_index_in_dim(x, at, axis, keepdims=False)


def body(hidden, grad_out, weight):
    row, rep = lax.axis_index("row"), lax.axis_index("rep")
    y, x_hi = row // 2, row % 2
    x_lo, core = rep // 2, rep % 2
    first = y ^ (1 + 2 * core)
    second = y ^ (3 - 2 * core)
    at = jnp.stack([y, second, first, y ^ 2, rep, rep ^ 1, rep ^ 2, rep ^ 3, core, x_lo]).astype(jnp.int32)
    tokens, tile_rows = hidden.shape
    slab = weight.shape[1]
    half = tile_rows // 2
    pair = 2 * slab
    n = GATHERED_ROWS
    rest = half - n
    chunk = tile_rows // A_CHUNKS
    quarter = tokens // N_Y
    half_tiles, n_tiles, chunk_tiles = half // TILE, n // TILE, chunk // TILE

    hidden_from = grad_out.shape[1]
    weight_from = hidden_from + half
    weight_blocks = tile_rows // tokens

    def pack_plan(at, ins, outs):
        other = pl.multiple_of((1 - at[CORE_AT]) * half, TILE)
        moves = [
            (ins[0], outs[0].at[:, pl.ds(0, hidden_from)]),
            (ins[1].at[:, pl.ds(other, half)], outs[0].at[:, pl.ds(hidden_from, half)]),
        ]
        for i in range(weight_blocks):
            columns = pl.ds(weight_from + i * slab, slab)
            moves.append((ins[2].at[pl.ds(i * tokens, tokens)], outs[0].at[:, columns]))
        return moves

    def hidden_plan(at, ins, outs):
        sides = [pl.multiple_of(c * half, TILE) for c in (at[CORE_AT], 1 - at[CORE_AT])]
        return [
            (ins[0].at[:, pl.ds(sides[i // 2] + starts[i % 2], parts[i % 2])], outs[i]) for i in range(4)
        ]

    cuts = [(0, 0, 2 * TILE), (0, 2 * TILE, n - 2 * TILE), (1, 0, n - 2 * TILE), (1, n - 2 * TILE, 2 * TILE)]

    def hidden_cut(at, hidden_ref, i):
        side, start, size = cuts[i]
        start = pl.multiple_of((at[CORE_AT] if side == 0 else 1 - at[CORE_AT]) * half, TILE) + start
        return hidden_ref.at[:, pl.ds(start, size)]

    cut_shapes = [shape((tokens, size)) for _, _, size in cuts]
    weight_first, hidden_first = copies(
        at, [hidden, weight], [shape((chunk, slab)), cut_shapes[0]],
        lambda at, ins, outs: [(ins[1].at[pl.ds(0, chunk)], outs[0]), (hidden_cut(at, ins[0], 0), outs[1])], 2,
    )

    def late_plan(at, ins, outs):
        moves = [(hidden_cut(at, ins[1], i), outs[i - 1]) for i in (1, 2, 3)]
        moves.append((ins[2].at[pl.ds(chunk, chunk)], outs[3]))
        return moves + pack_plan(at, ins, outs[4:])

    *hidden_late, weight_late, packed = copies(
        at, [grad_out, hidden, weight],
        cut_shapes[1:] + [shape((chunk, slab)), shape((tokens, weight_from + half))],
        late_plan, 6 + weight_blocks, after=[weight_first],
    )
    weight_x = [send(weight_first, X_LO), send(weight_late, X_LO)]
    hidden_x = [
        send(h, p) for h, p in zip([hidden_first, *hidden_late], (X_OUT, X_OUT, X_OUT_CORE, X_OUT_CORE))
    ]
    pack = send(packed, CORE)

    def turn_plan(at, ins, outs):
        moves = []
        for i, p in enumerate((Y, SECOND, FIRST, FAR)):
            for j, s in enumerate((SLAB, SLAB_C, SLAB_X, SLAB_XC)):
                src = ins[0].at[
                    pl.ds(pl.multiple_of(at[p] * quarter, quarter), quarter),
                    pl.ds(pl.multiple_of(at[s] * slab, slab), slab),
                ]
                moves.append((src, outs[0].at[pl.ds(i * quarter, quarter), pl.ds(j * slab, slab)]))
        return moves

    turned = copies(at, [grad_out], [shape(grad_out.shape)], turn_plan, 16, after=[packed])[0]

    def sum_kernel(at, hidden_ref, hidden_c_ref, out_ref, out_c_ref, result_ref):
        result_ref[...] = dot(hidden_ref[...], out_ref[...], 0, 0) + dot(hidden_c_ref[...], out_c_ref[...], 0, 0)

    tile_spec = pl.BlockSpec((TILE, pair), lambda i, at: (i, 0))
    own_columns = pl.BlockSpec((tokens, pair), lambda i, at: (0, at[X_LO_AT]))
    own_sum = call(
        sum_kernel, at, [hidden, pack, grad_out, pack],
        [
            pl.BlockSpec((tokens, TILE), lambda i, at: (0, at[CORE_AT] * half_tiles + i)),
            pl.BlockSpec((tokens, TILE), lambda i, at: (0, hidden_from // TILE + i)),
            own_columns, own_columns,
        ],
        [shape((half, pair), F32)], [tile_spec], (half_tiles,), after=[turned],
    )[0]

    lead = tokens // TILE

    def away_kernel(at, hidden_ref, hidden_c_ref, out_ref, out_c_ref, result_ref):
        i = pl.program_id(0)

        @pl.when(i < lead)
        def _():
            result_ref[...] = out_ref[pl.ds(pl.multiple_of(i * TILE, TILE), TILE)]

        @pl.when(i >= lead)
        def _():
            total = dot(hidden_ref[...], out_ref[...], 0, 0) + dot(hidden_c_ref[...], out_c_ref[...], 0, 0)
            result_ref[...] = total.astype(BF16)

    def send_away(after):
        columns = pl.BlockSpec((tokens, pair), lambda i, at: (0, 1 - at[X_LO_AT]))
        tile = lambda i: n_tiles + jnp.maximum(i - lead, 0)
        away = call(
            away_kernel, at, [hidden, pack, grad_out, pack],
            [
                pl.BlockSpec((tokens, TILE), lambda i, at: (0, at[CORE_AT] * half_tiles + tile(i))),
                pl.BlockSpec((tokens, TILE), lambda i, at: (0, hidden_from // TILE + tile(i))),
                columns, columns,
            ],
            [shape((tokens + rest, pair))], [tile_spec], (lead + rest // TILE,), after=after,
        )[0]
        return away, send(away, X_LO)

    def width_kernel(at, turned_ref, *refs):
        total = 0.0
        for j in range(4):
            total = total + dot(turned_ref[:, j * slab:(j + 1) * slab], refs[j][...], 1, 1)
        for i in range(N_Y):
            refs[4 + i][...] = total[i * quarter:(i + 1) * quarter].astype(BF16)

    def scatter_sends(own, near, off, opposite):
        return own, near, send(opposite, Y_FIRST), send(off, Y_FIRST)

    last = own_sum
    mine = []
    for k in range(A_CHUNKS):
        whole = pl.BlockSpec((TILE, slab), lambda i, at, k=k: (k * chunk_tiles + i, 0))
        chunked = pl.BlockSpec((TILE, slab), lambda i, at: (i, 0))
        per_block = tokens // TILE
        packed_spec = pl.BlockSpec(
            (TILE, slab),
            lambda i, at, k=k: ((k * chunk_tiles + i) % per_block, weight_from // slab + (k * chunk_tiles + i) // per_block),
        )
        if k == 0:
            forward = copy_of(at, weight_x[0], after=[last, hidden_x[0]])
        if k == 1:
            last, came = send_away([last, forward])
        parts = call(
            width_kernel, at, [turned, weight, pack, weight_x[k], send(forward, CORE)],
            [pl.BlockSpec(turned.shape, lambda i, at: (0, 0)), whole, packed_spec, chunked, chunked],
            [shape((quarter, chunk))] * N_Y,
            [pl.BlockSpec((quarter, TILE), lambda i, at: (0, i))] * N_Y,
            (chunk_tiles,), after=[last],
        )
        own, near, came_near, came_own = scatter_sends(*parts)
        near = add(at, [near, came_near], after=[hidden_x[1]] if k == 0 else ())
        if k == 0:
            forward = copy_of(at, weight_x[1], after=[near])
            after = [forward]
        else:
            out_came = copy_of(at, came, tokens, after=[near, hidden_x[2]])
            after = [out_came]
        last = add(at, [own, came_own, send(near, Y_SECOND)], after=after)
        mine.append(last)
    beside = [send(m, X_HI) for m in mine]
    out_xc = send(out_came, CORE)

    def grad_kernel(at, sum_ref, a_low, a_high, b_low, b_high, out_x_ref, out_xc_ref, came_ref, result_ref):
        i = pl.program_id(0)

        def gathered(a_ref, b_ref):
            total = sum_ref[...] + dot(a_ref[...], out_x_ref[...], 0, 0)
            result_ref[...] = (total + dot(b_ref[...], out_xc_ref[...], 0, 0)).astype(BF16)

        splits = [cuts[1][1] // TILE, cuts[3][1] // TILE, n_tiles]
        low = 0
        for high, refs in zip(splits, ((a_low, b_low), (a_high, b_low), (a_high, b_high))):

            @pl.when((i >= low) & (i < high))
            def _():
                gathered(*refs)

            low = high

        @pl.when(i >= n_tiles)
        def _():
            result_ref[...] = (sum_ref[...] + came_ref[...].astype(F32)).astype(BF16)

    def cut_spec(start, size):
        return pl.BlockSpec(
            (tokens, TILE), lambda i, at: (0, jnp.clip(i - start // TILE, 0, size // TILE - 1))
        )

    all_out = pl.BlockSpec((tokens, pair), lambda i, at: (0, 0))
    own_half = call(
        grad_kernel, at, [own_sum, *hidden_x, came, out_xc, came],
        [
            tile_spec, *[cut_spec(start, size) for _, start, size in cuts], all_out, all_out,
            pl.BlockSpec((TILE, pair), lambda i, at: (lead + jnp.maximum(i - n_tiles, 0), 0)),
        ],
        [shape((half, pair))], [tile_spec], (half_tiles,), after=[last, beside[0]],
    )[0]
    other_half = send(own_half, CORE)

    def right_kernel(at, own_ref, other_ref, own_slab_ref, other_slab_ref, result_ref, total_ref):
        i = pl.program_id(0)
        value = dot(own_ref[...], own_slab_ref[...], 0, 0) + dot(other_ref[...], other_slab_ref[...], 0, 0)

        @pl.when(i == 0)
        def _():
            total_ref[...] = value

        @pl.when(i > 0)
        def _():
            total_ref[...] += value

        @pl.when(i == pl.num_programs(0) - 1)
        def _():
            result_ref[...] = (total_ref[...] / FF).astype(BF16)

    steps = 2
    rows_spec = pl.BlockSpec((half // steps, pair), lambda i, at: (i, 0))
    slab_spec = pl.BlockSpec((half // steps, slab), lambda i, at: (i, at[CORE_AT]))
    right_partial = call(
        right_kernel, at, [own_half, other_half, own_half, other_half],
        [rows_spec, rows_spec, slab_spec, slab_spec],
        [shape((pair, slab))], [pl.BlockSpec((pair, slab), lambda i, at: (0, 0))], (steps,),
        scratch=[pltpu.VMEM((pair, slab), F32)],
    )[0]
    z = lax.axis_index("col")
    cols = lax.axis_size("col")
    bits = [1 << i for i in range(cols.bit_length() - 1)]
    right = right_partial.reshape([2] * len(bits) + [pair // cols, slab])
    for i, bit in enumerate(bits):
        here = z // bit % 2
        axis = len(bits) - 1 - i
        came_z = lax.ppermute(
            piece(right, 1 - here, axis).astype(BF16), "col", [(j, j ^ bit) for j in range(cols)]
        )
        right = piece(right, here, axis)
        if i < len(bits) - 1:
            right = right.astype(F32) + came_z.astype(F32)

    def last_kernel(at, mine_ref, came_ref, result_ref):
        result_ref[...] = mine_ref[...].astype(F32) + came_ref[...].astype(F32)

    spec = pl.BlockSpec(right.shape, lambda i, at: (0, 0))
    right_stats = call(
        last_kernel, at, [right, came_z], [spec] * 2, [shape(right.shape, F32)], [spec],
    )[0].T

    num = tile_rows // BLK
    mine_rows = BLK // 2 // N_Y

    def left_kernel(at, own_low, own_high, other_low, other_high, *refs):
        outs, block, product = refs[:N_Y], refs[N_Y], refs[N_Y + 1]
        a = pl.program_id(0)
        for part, own_ref, other_ref in ((0, own_low, other_low), (1, own_high, other_high)):
            held = (2 * a + part) // half_tiles == at[CORE_AT]
            block[part * TILE:(part + 1) * TILE] = jnp.where(held, own_ref[...], other_ref[...])
        groups = block[...].reshape(16, 2, 16, pair)
        my_rows = jnp.where(at[CORE_AT] == 0, groups[:, 0], groups[:, 1]).reshape(BLK // 2, pair)
        product[...] = (dot(my_rows, block[...], 1, 1) / D).astype(BF16)
        for i, p in enumerate((Y, SECOND, FIRST, FAR)):
            outs[i][0] = product[pl.ds(pl.multiple_of(at[p] * mine_rows, mine_rows), mine_rows)]

    halves = [
        pl.BlockSpec((TILE, pair), lambda a, at, part=part: ((2 * a + part) % half_tiles, 0)) for part in (0, 1)
    ]
    left = left_parts = call(
        left_kernel, at, [own_half, own_half, other_half, other_half], halves + halves,
        [shape((num, mine_rows, BLK))] * N_Y,
        [pl.BlockSpec((1, mine_rows, BLK), lambda a, at: (a, 0, 0))] * N_Y,
        (num,), scratch=[pltpu.VMEM((BLK, pair), BF16), pltpu.VMEM((BLK // 2, BLK), BF16)],
        after=[right_partial, beside[1]],
    )
    own, near, came_near, came_own = scatter_sends(*left)
    near = (near.astype(F32) + came_near.astype(F32)).astype(BF16)
    left = own.astype(F32) + came_own.astype(F32) + send(near, Y_SECOND).astype(F32)
    left = left.reshape(num, 2, 2, 16, BLK)
    sent = send(piece(left, 1 - x_lo, 2).astype(BF16), X_LO)
    left = piece(left, x_lo, 2) + sent.astype(F32)
    sent = send(piece(left, 1 - x_hi, 1).astype(BF16), X_HI)
    left_stats = piece(left, x_hi, 1) + sent.astype(F32)

    def slab_kernel(at, own_ref, other_ref, result_ref):
        held = pl.program_id(0) == at[CORE_AT]
        result_ref[...] = jnp.where(held, own_ref[...], other_ref[...])

    slab_half = pl.BlockSpec((half, slab), lambda i, at: (0, at[CORE_AT]))
    grad_slab = call(
        slab_kernel, at, [own_half, other_half], [slab_half] * 2, [shape(weight.shape)],
        [pl.BlockSpec((half, slab), lambda i, at: (i, 0))], (2,), after=left_parts[:1],
    )[0]

    def place_kernel(at, *refs):
        for j in range(N_Y):

            @pl.when(pl.program_id(0) == j)
            def _():
                refs[-1][...] = refs[j][...]

    grad_hidden = None
    for k in range(A_CHUNKS):
        total = add(at, [mine[k], beside[k]], after=[grad_slab] if k > 0 else ())
        near = send(total, Y_SECOND)
        off = send(total, Y_FIRST)
        opposite = send(near, Y_FIRST)
        given, after = [total, near, off, opposite], []
        specs = [pl.BlockSpec(total.shape, lambda i, at: (0, 0))] * N_Y
        if k > 0:
            given, specs = given + [grad_hidden], specs + [ANY]
            after = [left_stats, right_stats]
        grad_hidden = call(
            place_kernel, at, given, specs, [shape(hidden.shape)],
            [pl.BlockSpec(total.shape, lambda i, at, k=k: (at[Y + i], k))], (N_Y,),
            aliases={N_Y + 1: 0} if k > 0 else None, after=after,
        )[0]
    return grad_hidden, grad_slab, left_stats, right_stats


def solution(mesh):
    return jax.shard_map(
        body,
        mesh=mesh,
        in_specs=(P("rep", "col"), P("rep", "row"), P("col", ("row", "rep"))),
        out_specs=(
            P("rep", "col"),
            P("col", ("row", "rep")),
            P("col", ("row", "rep"), None),
            P(("row", "rep"), "col"),
        ),
        check_vma=False,
    )
```

time: 566 us -> 200 us (0.35)
  waiting for transfers between devices: 517 us -> 66.1 us
  Pallas kernels: 0 us -> 58.7 us
  starting transfers between devices: 0.24 us -> 54.2 us
  matrix products: 23.9 us -> 0 us
  between operations: 14.1 us -> 1.18 us
  local copies, waits for them, and re-layouts: 5.98 us -> 14.5 us
    reduce_scatter x3 -> x0, waiting for transfers between devices: 199 us -> none  [the longest x1 86 us: body(): lax.psum_scatter(left_partial.astype(jnp.bfloat16), ('row', 'rep'), scatt...]
    psum x1 -> x0, waiting for transfers between devices: 172 us -> none  [body(): grad_hidden = lax.psum(width_partial.astype(jnp.bfloat16), 'row')]
    all_gather x2 -> x0, waiting for transfers between devices: 146 us -> none  [the longest x1 73.5 us: body(): lax.all_gather(weight, 'rep', axis=1, tiled=True)]
    ppermute x0 -> x34, waiting for transfers between devices: none -> 66.1 us  [the longest x31 63.9 us: send(): return lax.ppermute(x, ('row', 'rep'), perm)]
    pallas_call x0 -> x23, Pallas kernels: none -> 58.7 us  [call(): pl.pallas_call(run, grid_spec=pltpu.PrefetchScalarGridSpec(num_scalar_pre...]
    ppermute x0 -> x34, starting transfers between devices: none -> 54.2 us  [the longest x31 44.4 us: send(): return lax.ppermute(x, ('row', 'rep'), perm)]
    dot_general x4 -> x0, matrix products: 23.9 us -> none  [the longest x1 8.52 us: body(): lax.dot_general(grad_out, lax.all_gather(weight, 'rep', axis=1, tiled=Tru...]
    unnamed x5 -> x58, local copies, waits for them, and re-layouts: 5.98 us -> 11.5 us
  transfers between devices with their start and end apart: 6 -> 34, of which waited for: 6 -> 16; matrix products, arithmetic and copies ran while one was open for 3% -> 3% of each run, Pallas kernels for 0% -> 18%
where the time goes in v1:
time: 200 us; the launch traced here: 199 us
  waiting for transfers between devices  66.1 us (33%)
  Pallas kernels  58.7 us (29%)
  starting transfers between devices  54.2 us (27%)
  local copies, waits for them, and re-layouts  14.5 us (7%)
  other arithmetic  4.49 us (2%)
    ppermute x31, waiting for transfers between devices, send(): return lax.ppermute(x, ('row', 'rep'), perm)  63.9 us
    pallas_call x23, Pallas kernels, call(): pl.pallas_call(run, grid_spec=pltpu.PrefetchScalarGridSpec(num_scalar_pre...  58.7 us
    ppermute x31, starting transfers between devices, send(): return lax.ppermute(x, ('row', 'rep'), perm)  44.4 us
    unnamed x58, local copies, waits for them, and re-layouts  11.5 us
    ppermute x3, starting transfers between devices, body(): lax.ppermute(piece(right, 1 - here, axis).astype(BF16), 'col', [(j, j ^ b...  9.76 us
  transfers between devices with their start and end apart: 34, of which 16 were waited for; matrix products, arithmetic and copies ran while one was open for 3% of the time, Pallas kernels for 18%

profile of v1, /device:TPU:32, one launch (start us, length us, event | category | flops | bytes accessed | tf_op | source)
XLA Modules:
  0.0 199.2 jit_solution(1708736152115357282)
XLA Ops:
  1.3 3.1 %shard_map.66 = (bf16[1792,256]{1,0:T(8,128)(2,1)}, bf16[512,512]{1,0:T(8,128)(2,1)}) custom-call(s32[10]{0:T(128)} %stack.43.at_ref, bf16[512,3584]{1,0:T(8,128)(2,1)} %refs_0_.9, bf16[3584,256]{1,0:T(8,128)(2,1)} %refs_1_.7), custom_call_target="tpu_custom_call" | custom-call | flops 1 | bytes 1 | tf_op jit(solution)/shard_map/pallas_call | solution.py:56
  4.4 7.1 %shard_map.67 = (bf16[512,768]{1,0:T(8,128)(2,1)}, bf16[512,768]{1,0:T(8,128)(2,1)}, bf16[512,512]{1,0:T(8,128)(2,1)}, bf16[1792,256]{1,0:T(8,128)(2,1)}, bf16[512,4608]{1,0:T(8,128)(2,1)}) custom-call(s32[10]{0:T(128)} %stack.43.at_ref, bf16[512,1024]{1,0:T(8,128)(2,1)} %refs_2_.5, bf16[512,3584]{1,0:T(8,128)(2,1)} %refs_0_.9, bf16[3584,256]{1,0:T(8,128)(2,1)} %refs_1_.7, ...), custom_call_target="tpu_custom_call" | custom-call | flops 1 | bytes 1 | tf_op jit(solution)/shard_map/pallas_call | solution.py:56
  11.7 1.6 collective-permute-start.2
  13.2 2.1 %collective-permute-start.3 = (bf16[512,512]{1,0:T(8,128)(2,1)}, bf16[512,512]{1,0:T(8,128)(2,1)}, u32[]{:S(2)}, u32[]{:S(2)}) collective-permute-start(bf16[512,512]{1,0:T(8,128)(2,1)} %get-tuple-element.26), channel_id=1, source_target_pairs={{0,34},{1,35},{2,32},{3,33},{32,2},{33,3},{34,0},{35,1},{64,98},{6... | collective-permute-start | bytes 1572872 | tf_op jit(solution)/shard_map/ppermute | solution.py:40
  15.3 3.0 %shard_map.68.refs_4_.refs_0_ = bf16[512,1024]{1,0:T(8,128)(2,1)} custom-call(s32[10]{0:T(128)} %stack.43.at_ref, bf16[512,1024]{1,0:T(8,128)(2,1)} %refs_2_.5, bf16[512,4608]{1,0:T(8,128)(2,1)} %get-tuple-element.24.refs_1_), custom_call_target="tpu_custom_call" | custom-call | flops 1 | bytes 1 | tf_op jit(solution)/shard_map/pallas_call | solution.py:56
  19.8 2.0 %copy-done = bf16[512,3584]{1,0:T(8,128)(2,1)S(1)} copy-done((bf16[512,3584]{1,0:T(8,128)(2,1)S(1)}, bf16[512,3584]{1,0:T(8,128)(2,1)}, u32[]{:S(2)}) %copy-start) | copy-done | bytes 3670040
  23.0 4.4 %shard_map.69.refs_1_.refs_5_.refs_0_ = f32[1792,512]{1,0:T(8,128)S(1)} custom-call(s32[10]{0:T(128)S(1)} %copy-done.18, bf16[512,3584]{1,0:T(8,128)(2,1)S(1)} %copy-done, bf16[512,4608]{1,0:T(8,128)(2,1)S(1)} %collective-permute-done.refs_1_.refs_3_.refs_2_, bf16[512,1024]{1,0:T(8,128)(2,1)S(1)} %copy-done.5, ...), custom_call_target="tpu_custom_call" | custom-call | flops 1 | bytes 1 | tf_op jit(solution)/shard_map/pallas_call | solution.py:56
  28.7 6.0 %collective-permute-done.2.refs_0_.refs_3_ = bf16[1792,256]{1,0:T(8,128)(2,1)} collective-permute-done((bf16[1792,256]{1,0:T(8,128)(2,1)}, bf16[1792,256]{1,0:T(8,128)(2,1)}, u32[]{:S(2)}, u32[]{:S(2)}) %collective-permute-start.2) | collective-permute-done | bytes 917536 | tf_op jit(solution)/shard_map/ppermute | solution.py:40
  34.7 1.8 shard_map.70
  36.6 1.6 collective-permute-start.1
  38.2 2.1 %collective-permute-start.6 = (bf16[512,768]{1,0:T(8,128)(2,1)S(1)}, bf16[512,768]{1,0:T(8,128)(2,1)S(1)}, u32[]{:S(2)}, u32[]{:S(2)}) collective-permute-start(bf16[512,768]{1,0:T(8,128)(2,1)S(1)} %copy-done.27), channel_id=1, source_target_pairs={{0,34},{1,35},{2,32},{3,33},{32,2},{33,3},{34,0},{35,1},{64,98},{6... | collective-permute-start | bytes 2359304 | tf_op jit(solution)/shard_map/ppermute | solution.py:40
  40.3 6.3 %shard_map.71 = (bf16[128,1792]{1,0:T(8,128)(2,1)S(1)}, bf16[128,1792]{1,0:T(8,128)(2,1)S(1)}, bf16[128,1792]{1,0:T(8,128)(2,1)S(1)}, bf16[128,1792]{1,0:T(8,128)(2,1)S(1)}) custom-call(s32[10]{0:T(128)S(1)} %copy-done.18, bf16[512,1024]{1,0:T(8,128)(2,1)S(1)} %copy-done.7, bf16[3584,256]{1,0:T(8,128)(2,1)S(1)} %copy-done.4, ...), custom_call_target="tpu_custom_call" | custom-call | flops 1 | bytes 1 | tf_op jit(solution)/shard_map/pallas_call | solution.py:56
  46.7 1.7 collective-permute-start.5
  48.8 10.2 %collective-permute-done.6.refs_2_ = bf16[512,768]{1,0:T(8,128)(2,1)S(1)} collective-permute-done((bf16[512,768]{1,0:T(8,128)(2,1)S(1)}, bf16[512,768]{1,0:T(8,128)(2,1)S(1)}, u32[]{:S(2)}, u32[]{:S(2)}) %collective-permute-start.6) | collective-permute-done | bytes 786464 | tf_op jit(solution)/shard_map/ppermute | solution.py:40
  59.8 3.1 %collective-permute-start.9 = (bf16[128,1792]{1,0:T(8,128)(2,1)S(1)}, bf16[128,1792]{1,0:T(8,128)(2,1)S(1)}, u32[]{:S(2)}, u32[]{:S(2)}) collective-permute-start(bf16[128,1792]{1,0:T(8,128)(2,1)S(1)} %shard_map.72.refs_1_), channel_id=1, source_target_pairs={{0,192},{1,65},{2,194},{3,67},{32,224},{33,97},{34,226},{35,99},{6... | collective-permute-start | bytes 1376264 | tf_op jit(solution)/shard_map/ppermute | solution.py:40
  63.7 5.9 %collective-permute-done.9.refs_2_ = bf16[128,1792]{1,0:T(8,128)(2,1)S(1)} collective-permute-done((bf16[128,1792]{1,0:T(8,128)(2,1)S(1)}, bf16[128,1792]{1,0:T(8,128)(2,1)S(1)}, u32[]{:S(2)}, u32[]{:S(2)}) %collective-permute-start.9) | collective-permute-done | bytes 458784 | tf_op jit(solution)/shard_map/ppermute | solution.py:40
  70.6 1.9 shard_map.75.refs_5_
  72.7 4.3 %shard_map.76 = (bf16[128,1792]{1,0:T(8,128)(2,1)S(1)}, bf16[128,1792]{1,0:T(8,128)(2,1)S(1)}, bf16[128,1792]{1,0:T(8,128)(2,1)S(1)}, bf16[128,1792]{1,0:T(8,128)(2,1)S(1)}) custom-call(s32[10]{0:T(128)S(1)} %copy-done.19, bf16[512,1024]{1,0:T(8,128)(2,1)S(1)} %copy-done.7, bf16[3584,256]{1,0:T(8,128)(2,1)S(1)} %copy-done.4, ...), custom_call_target="tpu_custom_call" | custom-call | flops 1 | bytes 1 | tf_op jit(solution)/shard_map/pallas_call | solution.py:56
  77.6 5.2 %collective-permute-start.16 = (bf16[512,512]{1,0:T(8,128)(2,1)S(1)}, bf16[512,512]{1,0:T(8,128)(2,1)S(1)}, u32[]{:S(2)}, u32[]{:S(2)}) collective-permute-start(bf16[512,512]{1,0:T(8,128)(2,1)S(1)} %copy-done.28), channel_id=1, source_target_pairs={{0,35},{1,34},{2,33},{3,32},{32,3},{33,2},{34,1},{35,0},{64,99},{6... | collective-permute-start | bytes 1572872 | tf_op jit(solution)/shard_map/ppermute | solution.py:40
  82.8 2.8 %collective-permute-done.11.refs_1_ = bf16[128,1792]{1,0:T(8,128)(2,1)S(1)} collective-permute-done((bf16[128,1792]{1,0:T(8,128)(2,1)S(1)}, bf16[128,1792]{1,0:T(8,128)(2,1)S(1)}, u32[]{:S(2)}, u32[]{:S(2)}) %collective-permute-start.11) | collective-permute-done | bytes 458784 | tf_op jit(solution)/shard_map/ppermute | solution.py:40
  86.4 7.2 %collective-permute-done.14.refs_2_.refs_3_ = bf16[512,768]{1,0:T(8,128)(2,1)S(1)} collective-permute-done((bf16[512,768]{1,0:T(8,128)(2,1)S(1)}, bf16[512,768]{1,0:T(8,128)(2,1)S(1)}, u32[]{:S(2)}, u32[]{:S(2)}) %collective-permute-start.14) | collective-permute-done | bytes 786464 | tf_op jit(solution)/shard_map/ppermute | solution.py:40
  95.6 1.7 collective-permute-start.10
  97.2 2.2 %collective-permute-start.12 = (bf16[128,1792]{1,0:T(8,128)(2,1)S(1)}, bf16[128,1792]{1,0:T(8,128)(2,1)S(1)}, u32[]{:S(2)}, u32[]{:S(2)}) collective-permute-start(bf16[128,1792]{1,0:T(8,128)(2,1)S(1)} %shard_map.77.refs_1_), channel_id=1, source_target_pairs={{0,192},{1,65},{2,194},{3,67},{32,224},{33,97},{34,226},{35,99},{6... | collective-permute-start | bytes 1376264 | tf_op jit(solution)/shard_map/ppermute | solution.py:40
  99.4 1.8 collective-permute-start.18
  101.2 6.0 %collective-permute-done.10.refs_1_ = bf16[128,1792]{1,0:T(8,128)(2,1)S(1)} collective-permute-done((bf16[128,1792]{1,0:T(8,128)(2,1)S(1)}, bf16[128,1792]{1,0:T(8,128)(2,1)S(1)}, u32[]{:S(2)}, u32[]{:S(2)}) %collective-permute-start.10) | collective-permute-done | bytes 458784 | tf_op jit(solution)/shard_map/ppermute | solution.py:40
  107.3 2.5 %collective-permute-done.12.refs_2_ = bf16[128,1792]{1,0:T(8,128)(2,1)S(1)} collective-permute-done((bf16[128,1792]{1,0:T(8,128)(2,1)S(1)}, bf16[128,1792]{1,0:T(8,128)(2,1)S(1)}, u32[]{:S(2)}, u32[]{:S(2)}) %collective-permute-start.12) | collective-permute-done | bytes 458784 | tf_op jit(solution)/shard_map/ppermute | solution.py:40
  110.7 3.5 %collective-permute-done.16.refs_4_ = bf16[512,512]{1,0:T(8,128)(2,1)S(1)} collective-permute-done((bf16[512,512]{1,0:T(8,128)(2,1)S(1)}, bf16[512,512]{1,0:T(8,128)(2,1)S(1)}, u32[]{:S(2)}, u32[]{:S(2)}) %collective-permute-start.16) | collective-permute-done | bytes 524320 | tf_op jit(solution)/shard_map/ppermute | solution.py:40
  114.2 4.5 %shard_map.80.refs_0_.refs_2_.refs_1_ = bf16[1792,512]{1,0:T(8,128)(2,1)S(1)} custom-call(s32[10]{0:T(128)S(1)} %copy-done.19, f32[1792,512]{1,0:T(8,128)S(1)} %shard_map.69.refs_1_.refs_5_.refs_0_, bf16[512,512]{1,0:T(8,128)(2,1)} %collective-permute-done.3.refs_2_.refs_1_, bf16[512,768]{1,0:T(8,128)(2,1)S(1)} %collective-permute-done.6.refs_2_, ...), custom_call_target="tpu_custom_call" | custom-call | flops 1 | bytes 1 | tf_op jit(solution)/shard_map/pallas_call | solution.py:56
  119.5 1.9 collective-permute-start.15
  121.4 1.9 collective-permute-done.19.refs_1_.refs_3_.refs_2_
  123.3 2.4 %shard_map.81.refs_4_ = bf16[512,256]{1,0:T(8,128)(2,1)S(1)} custom-call(s32[10]{0:T(128)S(1)} %copy-done.19, bf16[1792,512]{1,0:T(8,128)(2,1)S(1)} %shard_map.80.refs_0_.refs_2_.refs_1_, bf16[1792,512]{1,0:T(8,128)(2,1)S(1)} %collective-permute-done.19.refs_1_.refs_3_.refs_2_, bf16[1792,512]{1,0:T(8,128)(2,1)S(1)} %shard_map.80.refs_0_.refs_2_.refs_1_, ...), custom_call_target="tpu_custom_call" | custom-call | flops 1 | bytes 1 | tf_op jit(solution)/shard_map/pallas_call | solution.py:56
  125.7 8.3 %collective-permute-done.15.refs_5_.refs_1_ = bf16[128,1792]{1,0:T(8,128)(2,1)S(1)} collective-permute-done((bf16[128,1792]{1,0:T(8,128)(2,1)S(1)}, bf16[128,1792]{1,0:T(8,128)(2,1)S(1)}, u32[]{:S(2)}, u32[]{:S(2)}) %collective-permute-start.15) | collective-permute-done | bytes 458784 | tf_op jit(solution)/shard_map/ppermute | solution.py:40
  134.0 4.7 %shard_map.82 = (bf16[7,64,512]{2,1,0:T(8,128)(2,1)S(1)}, bf16[7,64,512]{2,1,0:T(8,128)(2,1)S(1)}, bf16[7,64,512]{2,1,0:T(8,128)(2,1)S(1)}, bf16[7,64,512]{2,1,0:T(8,128)(2,1)}) custom-call(s32[10]{0:T(128)S(1)} %copy-done.19, bf16[1792,512]{1,0:T(8,128)(2,1)S(1)} %shard_map.80.refs_0_.refs_2_.refs_1_, ...), custom_call_target="tpu_custom_call" | custom-call | flops 1 | bytes 1 | tf_op jit(solution)/shard_map/pallas_call | solution.py:56
  142.6 2.7 %collective-permute-start.23 = (bf16[128,1792]{1,0:T(8,128)(2,1)S(1)}, bf16[128,1792]{1,0:T(8,128)(2,1)}, u32[]{:S(2)}, u32[]{:S(2)}) collective-permute-start(bf16[128,1792]{1,0:T(8,128)(2,1)S(1)} %shard_map.85.refs_0_), channel_id=1, source_target_pairs={{0,192},{1,65},{2,194},{3,67},{32,224},{33,97},{34,226},{35,99},{6... | collective-permute-start | bytes 1376264 | tf_op jit(solution)/shard_map/ppermute | solution.py:40
  148.2 2.6 %collective-permute-done.27 = bf16[7,64,512]{2,1,0:T(8,128)(2,1)} collective-permute-done((bf16[7,64,512]{2,1,0:T(8,128)(2,1)}, bf16[7,64,512]{2,1,0:T(8,128)(2,1)}, u32[]{:S(2)}, u32[]{:S(2)}) %collective-permute-start.27) | collective-permute-done | bytes 458784 | tf_op jit(solution)/shard_map/ppermute | solution.py:40
  150.8 2.1 %add_convert_fusion = bf16[7,64,512]{2,1,0:T(8,128)(2,1)} fusion(bf16[7,64,512]{2,1,0:T(8,128)(2,1)} %collective-permute-done.27, bf16[7,64,512]{2,1,0:T(8,128)(2,1)} %copy-done.17), kind=kLoop, calls=%fused_computation.1 | loop fusion | flops 917504 | bytes 1376256 | tf_op jit(solution)/shard_map/convert_element_type | solution.py:401
  152.9 5.9 %collective-permute-start.28 = (bf16[7,64,512]{2,1,0:T(8,128)(2,1)}, bf16[7,64,512]{2,1,0:T(8,128)(2,1)}, u32[]{:S(2)}, u32[]{:S(2)}) collective-permute-start(bf16[7,64,512]{2,1,0:T(8,128)(2,1)} %add_convert_fusion), channel_id=1, source_target_pairs={{0,192},{1,65},{2,194},{3,67},{32,224},{33,97},{34,226},{35,99},{6... | collective-permute-start | bytes 1376264 | tf_op jit(solution)/shard_map/ppermute | solution.py:40
  158.8 1.5 copy-done.3
  162.0 2.0 %shard_map.83.refs_2_ = bf16[3584,256]{1,0:T(8,128)(2,1)} custom-call(s32[10]{0:T(128)S(1)} %copy-done.21, bf16[1792,512]{1,0:T(8,128)(2,1)S(1)} %shard_map.80.refs_0_.refs_2_.refs_1_, bf16[1792,512]{1,0:T(8,128)(2,1)S(1)} %copy-done.3, bf16[7,64,512]{2,1,0:T(8,128)(2,1)S(1)} %copy-done.10), custom_call_target="tpu_custom_call" | custom-call | flops 1 | bytes 1 | tf_op jit(solution)/shard_map/pallas_call | solution.py:56
  164.0 2.0 %collective-permute-start.25 = (bf16[128,1792]{1,0:T(8,128)(2,1)}, bf16[128,1792]{1,0:T(8,128)(2,1)S(1)}, u32[]{:S(2)}, u32[]{:S(2)}) collective-permute-start(bf16[128,1792]{1,0:T(8,128)(2,1)} %collective-permute-done.23.refs_1_), channel_id=1, source_target_pairs={{0,64},{1,193},{2,66},{3,195},{32,96},{33,225},{34,98},{35,227},{6... | collective-permute-start | bytes 1376264 | tf_op jit(solution)/shard_map/ppermute | solution.py:40
  169.4 3.4 %collective-permute-start.32 = (bf16[2,64,256]{2,1,0:T(8,128)(2,1)S(1)}, bf16[2,64,256]{2,1,0:T(8,128)(2,1)S(1)}, u32[]{:S(2)}, u32[]{:S(2)}) collective-permute-start(bf16[2,64,256]{2,1,0:T(8,128)(2,1)S(1)} %fusion.2), channel_id=1, source_target_pairs={{0,8},{4,12},{8,0},{12,4},{16,24},{20,28},{24,16},{28,20},{1,9},{5... | collective-permute-start | bytes 196616 | tf_op jit(solution)/shard_map/ppermute | solution.py:360
  175.6 2.9 %collective-permute-done.25.refs_3_ = bf16[128,1792]{1,0:T(8,128)(2,1)S(1)} collective-permute-done((bf16[128,1792]{1,0:T(8,128)(2,1)}, bf16[128,1792]{1,0:T(8,128)(2,1)S(1)}, u32[]{:S(2)}, u32[]{:S(2)}) %collective-permute-start.25) | collective-permute-done | bytes 458784 | tf_op jit(solution)/shard_map/ppermute | solution.py:40
  178.6 3.3 %shard_map.86.refs_4_ = bf16[512,3584]{1,0:T(8,128)(2,1)} custom-call(s32[10]{0:T(128)S(1)} %copy-done.22, bf16[128,1792]{1,0:T(8,128)(2,1)S(1)} %shard_map.85.refs_0_, bf16[128,1792]{1,0:T(8,128)(2,1)} %collective-permute-done.23.refs_1_, bf16[128,1792]{1,0:T(8,128)(2,1)S(1)} %collective-permute-done.24.refs_2_, ...), custom_call_target="tpu_custom_call" | custom-call | flops 1 | bytes 1 | tf_op jit(solution)/shard_map/pallas_call | solution.py:56
  182.3 1.8 collective-permute-start.22
  184.2 1.9 collective-permute-start.30
  186.1 6.3 %collective-permute-start.33 = (bf16[64,256]{1,0:T(8,128)(2,1)S(1)}, bf16[64,256]{1,0:T(8,128)(2,1)S(1)}, u32[]{:S(2)}, u32[]{:S(2)}) collective-permute-start(bf16[64,256]{1,0:T(8,128)(2,1)S(1)} %fusion.3), channel_id=1, source_target_pairs={{0,16},{4,20},{8,24},{12,28},{16,0},{20,4},{24,8},{28,12},{1,17},{... | collective-permute-start | bytes 98312 | tf_op jit(solution)/shard_map/ppermute | solution.py:360
  192.4 2.2 %collective-permute-done.33.refs_1_ = bf16[64,256]{1,0:T(8,128)(2,1)S(1)} collective-permute-done((bf16[64,256]{1,0:T(8,128)(2,1)S(1)}, bf16[64,256]{1,0:T(8,128)(2,1)S(1)}, u32[]{:S(2)}, u32[]{:S(2)}) %collective-permute-start.33) | collective-permute-done | bytes 32800 | tf_op jit(solution)/shard_map/ppermute | solution.py:360
  196.8 2.3 %shard_map.88 = bf16[512,3584]{1,0:T(8,128)(2,1)} custom-call(s32[10]{0:T(128)S(1)} %copy-done.22, bf16[128,1792]{1,0:T(8,128)(2,1)S(1)} %shard_map.84.refs_0_, bf16[128,1792]{1,0:T(8,128)(2,1)S(1)} %collective-permute-done.20.refs_1_, bf16[128,1792]{1,0:T(8,128)(2,1)S(1)} %collective-permute-done.21.refs_2_, ...), custom_call_target="tpu_custom_call", output_to_operand_aliasing={{}: (5, {})} | custom-call | flops 1 | bytes 1 | tf_op jit(solution)/shard_map/pallas_call | solution.py:56
  (116 shorter events, 30.2 us)
Async XLA Ops:
  11.5 8.2 %copy-start.5 = (bf16[512,1024]{1,0:T(8,128)(2,1)S(1)}, bf16[512,1024]{1,0:T(8,128)(2,1)}, u32[]{:S(2)}) copy-start(bf16[512,1024]{1,0:T(8,128)(2,1)} %refs_2_.5) | copy-start | bytes 3145732
  11.5 8.2 %copy-start.18 = (s32[10]{0:T(128)S(1)}, s32[10]{0:T(128)}, u32[]{:S(2)}) copy-start(s32[10]{0:T(128)} %stack.43.at_ref) | copy-start | bytes 124
  11.6 8.2 %collective-permute-start = (bf16[512,4608]{1,0:T(8,128)(2,1)}, bf16[512,4608]{1,0:T(8,128)(2,1)S(1)}, u32[]{:S(2)}, u32[]{:S(2)}) collective-permute-start(bf16[512,4608]{1,0:T(8,128)(2,1)} %get-tuple-element.24.refs_1_), channel_id=1, source_target_pairs={{0,1},{1,0},{2,3},{3,2},{32,33},{33,32},{34,35},{35,34},{64,65},{6... | collective-permute-start | bytes 14155784 | tf_op jit(solution)/shard_map/ppermute | solution.py:40
  11.7 23.1 %collective-permute-start.2 = (bf16[1792,256]{1,0:T(8,128)(2,1)}, bf16[1792,256]{1,0:T(8,128)(2,1)}, u32[]{:S(2)}, u32[]{:S(2)}) collective-permute-start(bf16[1792,256]{1,0:T(8,128)(2,1)} %get-tuple-element.23.refs_3_), channel_id=1, source_target_pairs={{0,2},{1,3},{2,0},{3,1},{32,34},{33,35},{34,32},{35,33},{64,66},{6... | collective-permute-start | bytes 2752520 | tf_op jit(solution)/shard_map/ppermute | solution.py:40
  13.2 15.5 %collective-permute-start.3 = (bf16[512,512]{1,0:T(8,128)(2,1)}, bf16[512,512]{1,0:T(8,128)(2,1)}, u32[]{:S(2)}, u32[]{:S(2)}) collective-permute-start(bf16[512,512]{1,0:T(8,128)(2,1)} %get-tuple-element.26), channel_id=1, source_target_pairs={{0,34},{1,35},{2,32},{3,33},{32,2},{33,3},{34,0},{35,1},{64,98},{6... | collective-permute-start | bytes 1572872 | tf_op jit(solution)/shard_map/ppermute | solution.py:40
  27.4 9.2 %copy-start.25 = (bf16[1792,256]{1,0:T(8,128)(2,1)S(1)}, bf16[1792,256]{1,0:T(8,128)(2,1)}, u32[]{:S(2)}) copy-start(bf16[1792,256]{1,0:T(8,128)(2,1)} %get-tuple-element.25) | copy-start | bytes 2752516
  27.4 10.8 %copy-start.27 = (bf16[512,768]{1,0:T(8,128)(2,1)S(1)}, bf16[512,768]{1,0:T(8,128)(2,1)}, u32[]{:S(2)}) copy-start(bf16[512,768]{1,0:T(8,128)(2,1)} %get-tuple-element.29) | copy-start | bytes 2359300
  27.4 12.9 %copy-start.4 = (bf16[3584,256]{1,0:T(8,128)(2,1)S(1)}, bf16[3584,256]{1,0:T(8,128)(2,1)}, u32[]{:S(2)}) copy-start(bf16[3584,256]{1,0:T(8,128)(2,1)} %refs_1_.7) | copy-start | bytes 5505028
  27.4 12.9 %copy-start.7 = (bf16[512,1024]{1,0:T(8,128)(2,1)S(1)}, bf16[512,1024]{1,0:T(8,128)(2,1)}, u32[]{:S(2)}) copy-start(bf16[512,1024]{1,0:T(8,128)(2,1)} %shard_map.68.refs_4_.refs_0_) | copy-start | bytes 3145732
  36.5 3.8 %collective-permute-start.4 = (bf16[1792,256]{1,0:T(8,128)(2,1)S(1)}, bf16[1792,256]{1,0:T(8,128)(2,1)S(1)}, u32[]{:S(2)}, u32[]{:S(2)}) collective-permute-start(bf16[1792,256]{1,0:T(8,128)(2,1)S(1)} %shard_map.70), channel_id=1, source_target_pairs={{0,1},{1,0},{2,3},{3,2},{32,33},{33,32},{34,35},{35,34},{64,65},{6... | collective-permute-start | bytes 2752520 | tf_op jit(solution)/shard_map/ppermute | solution.py:40
  36.6 26.3 %collective-permute-start.1 = (bf16[1792,256]{1,0:T(8,128)(2,1)S(1)}, bf16[1792,256]{1,0:T(8,128)(2,1)S(1)}, u32[]{:S(2)}, u32[]{:S(2)}) collective-permute-start(bf16[1792,256]{1,0:T(8,128)(2,1)S(1)} %copy-done.25), channel_id=1, source_target_pairs={{0,2},{1,3},{2,0},{3,1},{32,34},{33,35},{34,32},{35,33},{64,66},{6... | collective-permute-start | bytes 2752520 | tf_op jit(solution)/shard_map/ppermute | solution.py:40
  38.2 20.8 %collective-permute-start.6 = (bf16[512,768]{1,0:T(8,128)(2,1)S(1)}, bf16[512,768]{1,0:T(8,128)(2,1)S(1)}, u32[]{:S(2)}, u32[]{:S(2)}) collective-permute-start(bf16[512,768]{1,0:T(8,128)(2,1)S(1)} %copy-done.27), channel_id=1, source_target_pairs={{0,34},{1,35},{2,32},{3,33},{32,2},{33,3},{34,0},{35,1},{64,98},{6... | collective-permute-start | bytes 2359304 | tf_op jit(solution)/shard_map/ppermute | solution.py:40
  46.6 23.0 %copy-start.19 = (s32[10]{0:T(128)S(1)}, s32[10]{0:T(128)}, u32[]{:S(2)}) copy-start(s32[10]{0:T(128)} %stack.43.at_ref) | copy-start | bytes 124
  46.6 23.9 %copy-start.1 = (bf16[512,3584]{1,0:T(8,128)(2,1)S(1)}, bf16[512,3584]{1,0:T(8,128)(2,1)}, u32[]{:S(2)}) copy-start(bf16[512,3584]{1,0:T(8,128)(2,1)} %refs_0_.9) | copy-start | bytes 11010052
  46.7 12.3 %collective-permute-start.5 = (bf16[128,1792]{1,0:T(8,128)(2,1)S(1)}, bf16[128,1792]{1,0:T(8,128)(2,1)S(1)}, u32[]{:S(2)}, u32[]{:S(2)}) collective-permute-start(bf16[128,1792]{1,0:T(8,128)(2,1)S(1)} %get-tuple-element.28), channel_id=1, source_target_pairs={{0,64},{1,193},{2,66},{3,195},{32,96},{33,225},{34,98},{35,227},{6... | collective-permute-start | bytes 1376264 | tf_op jit(solution)/shard_map/ppermute | solution.py:40
  48.3 15.4 %collective-permute-start.8 = (bf16[128,1792]{1,0:T(8,128)(2,1)S(1)}, bf16[128,1792]{1,0:T(8,128)(2,1)S(1)}, u32[]{:S(2)}, u32[]{:S(2)}) collective-permute-start(bf16[128,1792]{1,0:T(8,128)(2,1)S(1)} %get-tuple-element.31), channel_id=1, source_target_pairs={{0,64},{1,193},{2,66},{3,195},{32,96},{33,225},{34,98},{35,227},{6... | collective-permute-start | bytes 1376264 | tf_op jit(solution)/shard_map/ppermute | solution.py:40
  59.8 9.8 %collective-permute-start.9 = (bf16[128,1792]{1,0:T(8,128)(2,1)S(1)}, bf16[128,1792]{1,0:T(8,128)(2,1)S(1)}, u32[]{:S(2)}, u32[]{:S(2)}) collective-permute-start(bf16[128,1792]{1,0:T(8,128)(2,1)S(1)} %shard_map.72.refs_1_), channel_id=1, source_target_pairs={{0,192},{1,65},{2,194},{3,67},{32,224},{33,97},{34,226},{35,99},{6... | collective-permute-start | bytes 1376264 | tf_op jit(solution)/shard_map/ppermute | solution.py:40
  63.6 9.1 %collective-permute-start.7 = (bf16[1792,256]{1,0:T(8,128)(2,1)S(1)}, bf16[1792,256]{1,0:T(8,128)(2,1)S(1)}, u32[]{:S(2)}, u32[]{:S(2)}) collective-permute-start(bf16[1792,256]{1,0:T(8,128)(2,1)S(1)} %shard_map.73.refs_3_.refs_5_), channel_id=1, source_target_pairs={{0,1},{1,0},{2,3},{3,2},{32,33},{33,32},{34,35},{35,34},{64,65},{6... | collective-permute-start | bytes 2752520 | tf_op jit(solution)/shard_map/ppermute | solution.py:40
  72.4 22.4 %collective-permute-start.13 = (bf16[1024,512]{1,0:T(8,128)(2,1)S(1)}, bf16[1024,512]{1,0:T(8,128)(2,1)S(1)}, u32[]{:S(2)}, u32[]{:S(2)}) collective-permute-start(bf16[1024,512]{1,0:T(8,128)(2,1)S(1)} %shard_map.75.refs_5_), channel_id=1, source_target_pairs={{0,2},{1,3},{2,0},{3,1},{32,34},{33,35},{34,32},{35,33},{64,66},{6... | collective-permute-start | bytes 3145736 | tf_op jit(solution)/shard_map/ppermute | solution.py:40
  72.6 21.1 %collective-permute-start.14 = (bf16[512,768]{1,0:T(8,128)(2,1)S(1)}, bf16[512,768]{1,0:T(8,128)(2,1)S(1)}, u32[]{:S(2)}, u32[]{:S(2)}) collective-permute-start(bf16[512,768]{1,0:T(8,128)(2,1)S(1)} %copy-done.26), channel_id=1, source_target_pairs={{0,35},{1,34},{2,33},{3,32},{32,3},{33,2},{34,1},{35,0},{64,99},{6... | collective-permute-start | bytes 2359304 | tf_op jit(solution)/shard_map/ppermute | solution.py:40
  77.0 8.6 %collective-permute-start.11 = (bf16[128,1792]{1,0:T(8,128)(2,1)S(1)}, bf16[128,1792]{1,0:T(8,128)(2,1)S(1)}, u32[]{:S(2)}, u32[]{:S(2)}) collective-permute-start(bf16[128,1792]{1,0:T(8,128)(2,1)S(1)} %get-tuple-element.35), channel_id=1, source_target_pairs={{0,64},{1,193},{2,66},{3,195},{32,96},{33,225},{34,98},{35,227},{6... | collective-permute-start | bytes 1376264 | tf_op jit(solution)/shard_map/ppermute | solution.py:40
  77.6 36.6 %collective-permute-start.16 = (bf16[512,512]{1,0:T(8,128)(2,1)S(1)}, bf16[512,512]{1,0:T(8,128)(2,1)S(1)}, u32[]{:S(2)}, u32[]{:S(2)}) collective-permute-start(bf16[512,512]{1,0:T(8,128)(2,1)S(1)} %copy-done.28), channel_id=1, source_target_pairs={{0,35},{1,34},{2,33},{3,32},{32,3},{33,2},{34,1},{35,0},{64,99},{6... | collective-permute-start | bytes 1572872 | tf_op jit(solution)/shard_map/ppermute | solution.py:40
  95.5 18.7 %collective-permute-start.17 = (bf16[512,512]{1,0:T(8,128)(2,1)S(1)}, bf16[512,512]{1,0:T(8,128)(2,1)S(1)}, u32[]{:S(2)}, u32[]{:S(2)}) collective-permute-start(bf16[512,512]{1,0:T(8,128)(2,1)S(1)} %shard_map.78.refs_3_), channel_id=1, source_target_pairs={{0,1},{1,0},{2,3},{3,2},{32,33},{33,32},{34,35},{35,34},{64,65},{6... | collective-permute-start | bytes 1572872 | tf_op jit(solution)/shard_map/ppermute | solution.py:40
  95.6 11.7 %collective-permute-start.10 = (bf16[128,1792]{1,0:T(8,128)(2,1)S(1)}, bf16[128,1792]{1,0:T(8,128)(2,1)S(1)}, u32[]{:S(2)}, u32[]{:S(2)}) collective-permute-start(bf16[128,1792]{1,0:T(8,128)(2,1)S(1)} %get-tuple-element.33), channel_id=1, source_target_pairs={{0,64},{1,193},{2,66},{3,195},{32,96},{33,225},{34,98},{35,227},{6... | collective-permute-start | bytes 1376264 | tf_op jit(solution)/shard_map/ppermute | solution.py:40
  97.2 12.5 %collective-permute-start.12 = (bf16[128,1792]{1,0:T(8,128)(2,1)S(1)}, bf16[128,1792]{1,0:T(8,128)(2,1)S(1)}, u32[]{:S(2)}, u32[]{:S(2)}) collective-permute-start(bf16[128,1792]{1,0:T(8,128)(2,1)S(1)} %shard_map.77.refs_1_), channel_id=1, source_target_pairs={{0,192},{1,65},{2,194},{3,67},{32,224},{33,97},{34,226},{35,99},{6... | collective-permute-start | bytes 1376264 | tf_op jit(solution)/shard_map/ppermute | solution.py:40
  99.4 14.8 %collective-permute-start.18 = (bf16[128,1792]{1,0:T(8,128)(2,1)S(1)}, bf16[128,1792]{1,0:T(8,128)(2,1)S(1)}, u32[]{:S(2)}, u32[]{:S(2)}) collective-permute-start(bf16[128,1792]{1,0:T(8,128)(2,1)S(1)} %shard_map.74.refs_4_.refs_0_), channel_id=1, source_target_pairs={{0,32},{1,33},{2,34},{3,35},{32,0},{33,1},{34,2},{35,3},{64,96},{6... | collective-permute-start | bytes 1376264 | tf_op jit(solution)/shard_map/ppermute | solution.py:40
  119.5 3.8 %collective-permute-start.19 = (bf16[1792,512]{1,0:T(8,128)(2,1)S(1)}, bf16[1792,512]{1,0:T(8,128)(2,1)S(1)}, u32[]{:S(2)}, u32[]{:S(2)}) collective-permute-start(bf16[1792,512]{1,0:T(8,128)(2,1)S(1)} %shard_map.80.refs_0_.refs_2_.refs_1_), channel_id=1, source_target_pairs={{0,1},{1,0},{2,3},{3,2},{32,33},{33,32},{34,35},{35,34},{64,65},{6... | collective-permute-start | bytes 5505032 | tf_op jit(solution)/shard_map/ppermute | solution.py:40
  119.5 14.4 %collective-permute-start.15 = (bf16[128,1792]{1,0:T(8,128)(2,1)S(1)}, bf16[128,1792]{1,0:T(8,128)(2,1)S(1)}, u32[]{:S(2)}, u32[]{:S(2)}) collective-permute-start(bf16[128,1792]{1,0:T(8,128)(2,1)S(1)} %shard_map.79.refs_8_.refs_0_), channel_id=1, source_target_pairs={{0,32},{1,33},{2,34},{3,35},{32,0},{33,1},{34,2},{35,3},{64,96},{6... | collective-permute-start | bytes 1376264 | tf_op jit(solution)/shard_map/ppermute | solution.py:40
  123.3 10.7 %copy-start.2 = (bf16[1792,512]{1,0:T(8,128)(2,1)}, bf16[1792,512]{1,0:T(8,128)(2,1)S(1)}, u32[]{:S(2)}) copy-start(bf16[1792,512]{1,0:T(8,128)(2,1)S(1)} %collective-permute-done.19.refs_1_.refs_3_.refs_2_) | copy-start | bytes 5505028
  125.7 15.1 %copy-start.20 = (s32[10]{0:T(128)S(1)}, s32[10]{0:T(128)}, u32[]{:S(2)}) copy-start(s32[10]{0:T(128)} %stack.43.at_ref) | copy-start | bytes 124
  140.4 10.4 %collective-permute-start.27 = (bf16[7,64,512]{2,1,0:T(8,128)(2,1)}, bf16[7,64,512]{2,1,0:T(8,128)(2,1)}, u32[]{:S(2)}, u32[]{:S(2)}) collective-permute-start(bf16[7,64,512]{2,1,0:T(8,128)(2,1)} %get-tuple-element.41), channel_id=1, source_target_pairs={{0,64},{1,193},{2,66},{3,195},{32,96},{33,225},{34,98},{35,227},{6... | collective-permute-start | bytes 1376264 | tf_op jit(solution)/shard_map/ppermute | solution.py:40
  142.6 21.4 %collective-permute-start.23 = (bf16[128,1792]{1,0:T(8,128)(2,1)S(1)}, bf16[128,1792]{1,0:T(8,128)(2,1)}, u32[]{:S(2)}, u32[]{:S(2)}) collective-permute-start(bf16[128,1792]{1,0:T(8,128)(2,1)S(1)} %shard_map.85.refs_0_), channel_id=1, source_target_pairs={{0,192},{1,65},{2,194},{3,67},{32,224},{33,97},{34,226},{35,99},{6... | collective-permute-start | bytes 1376264 | tf_op jit(solution)/shard_map/ppermute | solution.py:40
  146.7 21.7 %collective-permute-start.31 = (bf16[2,2,64,256]{3,2,0,1:T(8,128)(2,1)}, bf16[2,2,64,256]{3,2,0,1:T(8,128)(2,1)}, u32[]{:S(2)}, u32[]{:S(2)}) collective-permute-start(bf16[2,2,64,256]{3,2,0,1:T(8,128)(2,1)} %bitcast.37), channel_id=1, source_target_pairs={{0,4},{4,0},{8,12},{12,8},{16,20},{20,16},{24,28},{28,24},{1,5},{5... | collective-permute-start | bytes 393224 | tf_op jit(solution)/shard_map/ppermute | solution.py:360
  146.8 22.6 %collective-permute-start.26 = (bf16[7,64,512]{2,1,0:T(8,128)(2,1)}, bf16[7,64,512]{2,1,0:T(8,128)(2,1)}, u32[]{:S(2)}, u32[]{:S(2)}) collective-permute-start(bf16[7,64,512]{2,1,0:T(8,128)(2,1)} %copy-done.23), channel_id=1, source_target_pairs={{0,64},{1,193},{2,66},{3,195},{32,96},{33,225},{34,98},{35,227},{6... | collective-permute-start | bytes 1376264 | tf_op jit(solution)/shard_map/ppermute | solution.py:40
  150.8 15.2 %copy-start.15 = (bf16[128,1792]{1,0:T(8,128)(2,1)S(1)}, bf16[128,1792]{1,0:T(8,128)(2,1)}, u32[]{:S(2)}) copy-start(bf16[128,1792]{1,0:T(8,128)(2,1)} %copy-done.14) | copy-start | bytes 1376260
  152.9 19.9 %collective-permute-start.28 = (bf16[7,64,512]{2,1,0:T(8,128)(2,1)}, bf16[7,64,512]{2,1,0:T(8,128)(2,1)}, u32[]{:S(2)}, u32[]{:S(2)}) collective-permute-start(bf16[7,64,512]{2,1,0:T(8,128)(2,1)} %add_convert_fusion), channel_id=1, source_target_pairs={{0,192},{1,65},{2,194},{3,67},{32,224},{33,97},{34,226},{35,99},{6... | collective-permute-start | bytes 1376264 | tf_op jit(solution)/shard_map/ppermute | solution.py:40
  158.8 16.8 %collective-permute-start.24 = (bf16[128,1792]{1,0:T(8,128)(2,1)S(1)}, bf16[128,1792]{1,0:T(8,128)(2,1)S(1)}, u32[]{:S(2)}, u32[]{:S(2)}) collective-permute-start(bf16[128,1792]{1,0:T(8,128)(2,1)S(1)} %shard_map.85.refs_0_), channel_id=1, source_target_pairs={{0,64},{1,193},{2,66},{3,195},{32,96},{33,225},{34,98},{35,227},{6... | collective-permute-start | bytes 1376264 | tf_op jit(solution)/shard_map/ppermute | solution.py:40
  162.0 6.5 %copy-start.24 = (bf16[2,2,1,64,256]{4,3,2,1,0:T(8,128)(2,1)S(1)}, bf16[2,2,1,64,256]{4,3,2,1,0:T(8,128)(2,1)}, u32[]{:S(2)}) copy-start(bf16[2,2,1,64,256]{4,3,2,1,0:T(8,128)(2,1)} %get-tuple-element.50) | copy-start | bytes 393220
  162.0 10.8 %copy-start.11 = (bf16[7,64,512]{2,1,0:T(8,128)(2,1)S(1)}, bf16[7,64,512]{2,1,0:T(8,128)(2,1)}, u32[]{:S(2)}) copy-start(bf16[7,64,512]{2,1,0:T(8,128)(2,1)} %copy-done.9) | copy-start | bytes 1376260
  162.0 16.6 %copy-start.22 = (s32[10]{0:T(128)S(1)}, s32[10]{0:T(128)}, u32[]{:S(2)}) copy-start(s32[10]{0:T(128)} %stack.43.at_ref) | copy-start | bytes 124
  164.0 14.6 %collective-permute-start.25 = (bf16[128,1792]{1,0:T(8,128)(2,1)}, bf16[128,1792]{1,0:T(8,128)(2,1)S(1)}, u32[]{:S(2)}, u32[]{:S(2)}) collective-permute-start(bf16[128,1792]{1,0:T(8,128)(2,1)} %collective-permute-done.23.refs_1_), channel_id=1, source_target_pairs={{0,64},{1,193},{2,66},{3,195},{32,96},{33,225},{34,98},{35,227},{6... | collective-permute-start | bytes 1376264 | tf_op jit(solution)/shard_map/ppermute | solution.py:40
  168.4 14.0 %collective-permute-start.20 = (bf16[128,1792]{1,0:T(8,128)(2,1)S(1)}, bf16[128,1792]{1,0:T(8,128)(2,1)S(1)}, u32[]{:S(2)}, u32[]{:S(2)}) collective-permute-start(bf16[128,1792]{1,0:T(8,128)(2,1)S(1)} %shard_map.84.refs_0_), channel_id=1, source_target_pairs={{0,192},{1,65},{2,194},{3,67},{32,224},{33,97},{34,226},{35,99},{6... | collective-permute-start | bytes 1376264 | tf_op jit(solution)/shard_map/ppermute | solution.py:40
  169.4 12.8 %collective-permute-start.32 = (bf16[2,64,256]{2,1,0:T(8,128)(2,1)S(1)}, bf16[2,64,256]{2,1,0:T(8,128)(2,1)S(1)}, u32[]{:S(2)}, u32[]{:S(2)}) collective-permute-start(bf16[2,64,256]{2,1,0:T(8,128)(2,1)S(1)} %fusion.2), channel_id=1, source_target_pairs={{0,8},{4,12},{8,0},{12,4},{16,24},{20,28},{24,16},{28,20},{1,9},{5... | collective-permute-start | bytes 196616 | tf_op jit(solution)/shard_map/ppermute | solution.py:360
  174.2 9.9 %collective-permute-start.29 = (bf16[7,2,16,512]{3,2,0,1:T(8,128)(2,1)S(1)}, bf16[7,2,16,512]{3,2,0,1:T(8,128)(2,1)S(1)}, u32[]{:S(2)}, u32[]{:S(2)}) collective-permute-start(bf16[7,2,16,512]{3,2,0,1:T(8,128)(2,1)S(1)} %fusion), channel_id=1, source_target_pairs={{0,2},{1,3},{2,0},{3,1},{32,34},{33,35},{34,32},{35,33},{64,66},{6... | collective-permute-start | bytes 688136 | tf_op jit(solution)/shard_map/ppermute | solution.py:40
  181.9 14.9 %collective-permute-start.21 = (bf16[128,1792]{1,0:T(8,128)(2,1)S(1)}, bf16[128,1792]{1,0:T(8,128)(2,1)S(1)}, u32[]{:S(2)}, u32[]{:S(2)}) collective-permute-start(bf16[128,1792]{1,0:T(8,128)(2,1)S(1)} %shard_map.84.refs_0_), channel_id=1, source_target_pairs={{0,64},{1,193},{2,66},{3,195},{32,96},{33,225},{34,98},{35,227},{6... | collective-permute-start | bytes 1376264 | tf_op jit(solution)/shard_map/ppermute | solution.py:40
  182.3 14.5 %collective-permute-start.22 = (bf16[128,1792]{1,0:T(8,128)(2,1)S(1)}, bf16[128,1792]{1,0:T(8,128)(2,1)S(1)}, u32[]{:S(2)}, u32[]{:S(2)}) collective-permute-start(bf16[128,1792]{1,0:T(8,128)(2,1)S(1)} %collective-permute-done.20.refs_1_), channel_id=1, source_target_pairs={{0,64},{1,193},{2,66},{3,195},{32,96},{33,225},{34,98},{35,227},{6... | collective-permute-start | bytes 1376264 | tf_op jit(solution)/shard_map/ppermute | solution.py:40
  184.2 12.6 %collective-permute-start.30 = (bf16[7,16,512]{2,1,0:T(8,128)(2,1)S(1)}, bf16[7,16,512]{2,1,0:T(8,128)(2,1)S(1)}, u32[]{:S(2)}, u32[]{:S(2)}) collective-permute-start(bf16[7,16,512]{2,1,0:T(8,128)(2,1)S(1)} %fusion.1), channel_id=1, source_target_pairs={{0,32},{1,33},{2,34},{3,35},{32,0},{33,1},{34,2},{35,3},{64,96},{6... | collective-permute-start | bytes 344072 | tf_op jit(solution)/shard_map/ppermute | solution.py:40
  186.1 8.5 %collective-permute-start.33 = (bf16[64,256]{1,0:T(8,128)(2,1)S(1)}, bf16[64,256]{1,0:T(8,128)(2,1)S(1)}, u32[]{:S(2)}, u32[]{:S(2)}) collective-permute-start(bf16[64,256]{1,0:T(8,128)(2,1)S(1)} %fusion.3), channel_id=1, source_target_pairs={{0,16},{4,20},{8,24},{12,28},{16,0},{20,4},{24,8},{28,12},{1,17},{... | collective-permute-start | bytes 98312 | tf_op jit(solution)/shard_map/ppermute | solution.py:360
  (15 other events, 26.3 us)

commit v2 on v1

v2 whole, which is shorter than its diff:
```python
import jax
import jax.numpy as jnp
from jax import lax
from jax.experimental import pallas as pl
from jax.experimental.pallas import tpu as pltpu
from jax.sharding import PartitionSpec as P

D = 8192
FF = 28672
BLK = 512
N_Y = 4
A_CHUNKS = 2
GATHERED_ROWS = 1280
TILE = 256
F32 = jnp.float32
BF16 = jnp.bfloat16

Y, SECOND, FIRST, FAR, SLAB, SLAB_C, SLAB_X, SLAB_XC, CORE_AT, X_LO_AT, X_HI_AT, Z_HIGH = range(12)


def plane_perm(move):
    pairs = []
    for at in range(32):
        y, x_hi, x_lo, core = at // 8, at // 4 % 2, at // 2 % 2, at % 2
        y, x_hi, x_lo, core = move(y, x_hi, x_lo, core)
        pairs.append((at, y * 8 + x_hi * 4 + x_lo * 2 + core))
    return pairs


CORE = plane_perm(lambda y, h, l, c: (y, h, l, 1 - c))
X_LO = plane_perm(lambda y, h, l, c: (y, h, 1 - l, c))
X_HI = plane_perm(lambda y, h, l, c: (y, 1 - h, l, c))
X_OUT = plane_perm(lambda y, h, l, c: (y, 1 - h, 1 - l, c))
X_OUT_CORE = plane_perm(lambda y, h, l, c: (y, 1 - h, 1 - l, 1 - c))
Y_FIRST = plane_perm(lambda y, h, l, c: (y ^ (3 if c else 1), h, l, c))
Y_SECOND = plane_perm(lambda y, h, l, c: (y ^ (1 if c else 3), h, l, c))


def send(x, perm):
    return lax.ppermute(x, ("row", "rep"), perm)


def shape(dims, dtype=BF16):
    return jax.ShapeDtypeStruct(dims, dtype)


ANY = pl.BlockSpec(memory_space=pl.ANY)


def call(kernel, at, arrays, in_specs, outs, out_specs, grid=(1,), scratch=(), after=(), aliases=None, vmem=10):
    n, m = len(arrays), len(after)

    def run(at_ref, *refs):
        kernel(at_ref, *refs[:n], *refs[n + m:])

    return pl.pallas_call(
        run,
        grid_spec=pltpu.PrefetchScalarGridSpec(
            num_scalar_prefetch=1,
            grid=grid,
            in_specs=list(in_specs) + [ANY] * m,
            out_specs=list(out_specs),
            scratch_shapes=list(scratch),
        ),
        out_shape=list(outs),
        input_output_aliases=aliases or {},
        compiler_params=pltpu.CompilerParams(vmem_limit_bytes=vmem * 2**20),
        cost_estimate=pl.CostEstimate(flops=1, bytes_accessed=1, transcendentals=0),
    )(at, *arrays, *after)


def copies(at, arrays, outs, plan, count, after=(), vmem=16):
    n = len(arrays)

    def kernel(at_ref, *refs):
        sems = refs[-1]
        moves = [
            pltpu.make_async_copy(src, dst, sems.at[i])
            for i, (src, dst) in enumerate(plan(at_ref, refs[:n], refs[n:-1]))
        ]
        for move in moves:
            move.start()
        for move in moves:
            move.wait()

    return call(
        kernel, at, arrays, [pl.BlockSpec(memory_space=pltpu.HBM)] * n, outs,
        [pl.BlockSpec(out.shape, lambda i, at: (0, 0)) for out in outs],
        scratch=[pltpu.SemaphoreType.DMA((count,))], after=after, vmem=vmem,
    )


def add(at, arrays, after=()):
    rows, width = arrays[0].shape
    spec = pl.BlockSpec((rows, width // 2), lambda i, at: (0, i))

    def kernel(at_ref, *refs):
        total = refs[0][...].astype(F32)
        for ref in refs[1:-1]:
            total = total + ref[...].astype(F32)
        refs[-1][...] = total.astype(BF16)

    return call(kernel, at, arrays, [spec] * len(arrays), [shape((rows, width))], [spec], (2,), after=after)[0]


def copy_of(at, x, rows=None, after=()):
    rows = rows or x.shape[0]
    spec = pl.BlockSpec((rows // 2, x.shape[1]), lambda i, at: (i, 0))

    def kernel(at_ref, x_ref, out_ref):
        out_ref[...] = x_ref[...]

    return call(kernel, at, [x], [spec], [shape((rows, x.shape[1]))], [spec], (2,), after=after)[0]


def dot(a, b, over_a, over_b):
    return lax.dot_general(a, b, (((over_a,), (over_b,)), ((), ())), preferred_element_type=F32)


def part_rows(x, at, rows):
    return lax.dynamic_slice_in_dim(x, at * rows, rows, 0)


def piece(x, at, axis):
    return lax.dynamic_index_in_dim(x, at, axis, keepdims=False)


def body(hidden, grad_out, weight):
    row, rep = lax.axis_index("row"), lax.axis_index("rep")
    y, x_hi = row // 2, row % 2
    x_lo, core = rep // 2, rep % 2
    first = y ^ (1 + 2 * core)
    second = y ^ (3 - 2 * core)
    z = lax.axis_index("col")
    cols = lax.axis_size("col")
    bits = [1 << i for i in reversed(range(cols.bit_length() - 1))]
    at = jnp.stack([y, second, first, y ^ 2, rep, rep ^ 1, rep ^ 2, rep ^ 3, core, x_lo, x_hi, *[z // bit % 2 for bit in bits]]).astype(jnp.int32)
    tokens, tile_rows = hidden.shape
    slab = weight.shape[1]
    half = tile_rows // 2
    pair = 2 * slab
    n = GATHERED_ROWS
    rest = half - n
    chunk = tile_rows // A_CHUNKS
    quarter = tokens // N_Y
    half_tiles, n_tiles, chunk_tiles = half // TILE, n // TILE, chunk // TILE

    hidden_c, grad_out_c, weight_c = (send(x, CORE) for x in (hidden, grad_out, weight))
    weight_x = [send(weight[:chunk], X_LO)]
    first_cut, low = (n_tiles - 1) * TILE, (n_tiles + 1) // 2 * TILE
    cuts = [(0, 0, first_cut), (0, first_cut, n - first_cut), (1, 0, low), (1, low, n - low)]

    def hidden_moves(at, hidden_ref, out, cut):
        other, start, size = cut
        start = pl.multiple_of((1 - at[CORE_AT] if other else at[CORE_AT]) * half, TILE) + start
        step = tokens // 4
        return [
            (hidden_ref.at[pl.ds(j * step, step), pl.ds(start, size)], out.at[pl.ds(j * step, step)])
            for j in range(4)
        ]

    cut_shapes = [shape((tokens, size)) for _, _, size in cuts]
    hidden_sent = copies(
        at, [hidden], cut_shapes[:1], lambda at, ins, outs: hidden_moves(at, ins[0], outs[0], cuts[0]), 4
    )
    hidden_x = [send(hidden_sent[0], X_OUT)]
    *hidden_late, weight_late = copies(
        at, [hidden, weight], cut_shapes[1:] + [shape((chunk, slab))],
        lambda at, ins, outs: [
            *hidden_moves(at, ins[0], outs[0], cuts[1]), *hidden_moves(at, ins[0], outs[1], cuts[2]),
            *hidden_moves(at, ins[0], outs[2], cuts[3]), (ins[1].at[pl.ds(chunk, chunk)], outs[3]),
        ], 13, after=hidden_sent,
    )
    weight_x.append(send(weight_late, X_LO))
    hidden_x += [send(h, p) for h, p in zip(hidden_late, (X_OUT, X_OUT_CORE, X_OUT_CORE))]

    def turn_plan(at, ins, outs):
        moves = []
        for i, p in enumerate((Y, SECOND, FIRST, FAR)):
            for j, s in enumerate((SLAB, SLAB_C, SLAB_X, SLAB_XC)):
                src = ins[0].at[
                    pl.ds(pl.multiple_of(at[p] * quarter, quarter), quarter),
                    pl.ds(pl.multiple_of(at[s] * slab, slab), slab),
                ]
                moves.append((src, outs[0].at[pl.ds(i * quarter, quarter), pl.ds(j * slab, slab)]))
        return moves

    turned = copies(at, [grad_out], [shape(grad_out.shape)], turn_plan, 16, after=[weight_late])[0]

    def sum_kernel(at, hidden_ref, hidden_c_ref, out_ref, out_c_ref, result_ref):
        result_ref[...] = dot(hidden_ref[...], out_ref[...], 0, 0) + dot(hidden_c_ref[...], out_c_ref[...], 0, 0)

    tile_spec = pl.BlockSpec((TILE, pair), lambda i, at: (i, 0))
    own_columns = pl.BlockSpec((tokens, pair), lambda i, at: (0, at[X_LO_AT]))
    own_sum = call(
        sum_kernel, at, [hidden, hidden_c, grad_out, grad_out_c],
        [
            pl.BlockSpec((tokens, TILE), lambda i, at: (0, at[CORE_AT] * half_tiles + i)),
            pl.BlockSpec((tokens, TILE), lambda i, at: (0, at[CORE_AT] * half_tiles + i)),
            own_columns, own_columns,
        ],
        [shape((half, pair), F32)], [tile_spec], (half_tiles,), after=[turned],
    )[0]

    lead = tokens // TILE

    def away_kernel(at, hidden_ref, hidden_c_ref, out_ref, out_c_ref, result_ref):
        i = pl.program_id(0)

        @pl.when(i < lead)
        def _():
            result_ref[...] = out_ref[pl.ds(pl.multiple_of(i * TILE, TILE), TILE)]

        @pl.when(i >= lead)
        def _():
            total = dot(hidden_ref[...], out_ref[...], 0, 0) + dot(hidden_c_ref[...], out_c_ref[...], 0, 0)
            result_ref[...] = total.astype(BF16)

    def send_away(after):
        columns = pl.BlockSpec((tokens, pair), lambda i, at: (0, 1 - at[X_LO_AT]))
        tile = lambda i: n_tiles + jnp.maximum(i - lead, 0)
        away = call(
            away_kernel, at, [hidden, hidden_c, grad_out, grad_out_c],
            [
                pl.BlockSpec((tokens, TILE), lambda i, at: (0, at[CORE_AT] * half_tiles + tile(i))),
                pl.BlockSpec((tokens, TILE), lambda i, at: (0, at[CORE_AT] * half_tiles + tile(i))),
                columns, columns,
            ],
            [shape((tokens + rest, pair))], [tile_spec], (lead + rest // TILE,), after=after,
        )[0]
        return away, send(away, X_LO)

    def width_kernel(at, turned_ref, *refs):
        total = 0.0
        for j in range(4):
            total = total + dot(turned_ref[:, j * slab:(j + 1) * slab], refs[j][...], 1, 1)
        for i in range(N_Y):
            refs[4 + i][...] = total[i * quarter:(i + 1) * quarter].astype(BF16)

    def scatter_sends(own, near, off, opposite):
        return own, near, send(opposite, Y_FIRST), send(off, Y_FIRST)

    def width_parts(k, after):
        forward = copy_of(at, weight_x[k], after=after)
        step = chunk // 2
        here = pl.BlockSpec((step, slab), lambda i, at: (2 * k + i, 0))
        there = pl.BlockSpec((step, slab), lambda i, at: (i, 0))
        return forward, lambda after: call(
            width_kernel, at, [turned, weight, weight_c, weight_x[k], send(forward, CORE)],
            [pl.BlockSpec(turned.shape, lambda i, at: (0, 0)), here, here, there, there],
            [shape((quarter, chunk))] * N_Y,
            [pl.BlockSpec((quarter, step), lambda i, at: (0, i))] * N_Y,
            (2,), after=after, vmem=16,
        )

    away, came_away = send_away([own_sum])
    forward, parts = width_parts(0, [away, hidden_x[0]])
    own, near, came_near, came_own = scatter_sends(*parts([forward]))
    near = add(at, [near, came_near])
    mine = [add(at, [own, came_own, send(near, Y_SECOND)])]
    forward, parts = width_parts(1, [mine[0], hidden_x[2]])
    own, near, came_near, came_own = scatter_sends(*parts([forward]))
    near = add(at, [near, came_near])
    mine.append(add(at, [own, came_own, send(near, Y_SECOND)]))
    beside = [send(m, X_HI) for m in mine]
    out_came = copy_of(at, came_away, tokens, after=[mine[1], hidden_x[1], hidden_x[3]])
    out_xc = send(out_came, CORE)

    def grad_kernel(at, sum_ref, a_low, a_high, b_low, b_high, out_x_ref, out_xc_ref, came_ref, result_ref):
        i = pl.program_id(0)

        def gathered(a_ref, b_ref):
            total = sum_ref[...] + dot(a_ref[...], out_x_ref[...], 0, 0)
            result_ref[...] = (total + dot(b_ref[...], out_xc_ref[...], 0, 0)).astype(BF16)

        bounds = [0, low // TILE, first_cut // TILE, n_tiles]
        for j, refs in enumerate(((a_low, b_low), (a_low, b_high), (a_high, b_high))):

            @pl.when((i >= bounds[j]) & (i < bounds[j + 1]))
            def _():
                gathered(*refs)

        @pl.when(i >= n_tiles)
        def _():
            result_ref[...] = (sum_ref[...] + came_ref[...].astype(F32)).astype(BF16)

    def cut_spec(start, size):
        return pl.BlockSpec(
            (tokens, TILE), lambda i, at: (0, jnp.clip(i - start // TILE, 0, size // TILE - 1))
        )

    all_out = pl.BlockSpec((tokens, pair), lambda i, at: (0, 0))
    own_half = call(
        grad_kernel, at, [own_sum, *hidden_x, came_away, out_xc, came_away],
        [
            tile_spec, *[cut_spec(start, size) for _, start, size in cuts], all_out, all_out,
            pl.BlockSpec((TILE, pair), lambda i, at: (lead + jnp.maximum(i - n_tiles, 0), 0)),
        ],
        [shape((half, pair))], [tile_spec], (half_tiles,), after=mine,
    )[0]
    other_half = send(own_half, CORE)

    num = tile_rows // BLK
    mine_rows = BLK // 2 // N_Y

    def left_kernel(at, own_low, own_high, other_low, other_high, *refs):
        outs, block, product = refs[:N_Y], refs[N_Y], refs[N_Y + 1]
        a = pl.program_id(0)
        for part, own_ref, other_ref in ((0, own_low, other_low), (1, own_high, other_high)):
            held = (2 * a + part) // half_tiles == at[CORE_AT]
            block[part * TILE:(part + 1) * TILE] = jnp.where(held, own_ref[...], other_ref[...])
        groups = block[...].reshape(16, 2, 16, pair)
        my_rows = jnp.where(at[CORE_AT] == 0, groups[:, 0], groups[:, 1]).reshape(BLK // 2, pair)
        product[...] = (dot(my_rows, block[...], 1, 1) / D).astype(BF16)
        for i, p in enumerate((Y, SECOND, FIRST, FAR)):
            outs[i][0] = product[pl.ds(pl.multiple_of(at[p] * mine_rows, mine_rows), mine_rows)]

    halves = [
        pl.BlockSpec((TILE, pair), lambda a, at, part=part: ((2 * a + part) % half_tiles, 0)) for part in (0, 1)
    ]
    left = left_parts = call(
        left_kernel, at, [own_half, own_half, other_half, other_half], halves + halves,
        [shape((num, mine_rows, BLK))] * N_Y,
        [pl.BlockSpec((1, mine_rows, BLK), lambda a, at: (a, 0, 0))] * N_Y,
        (num,), scratch=[pltpu.VMEM((BLK, pair), BF16), pltpu.VMEM((BLK // 2, BLK), BF16)],
        after=[own_half],
    )
    totals = [add(at, [mine[0], beside[0]], after=left_parts[:1])]
    def slab_kernel(at, own_ref, other_ref, result_ref, token_ref):
        token_ref[...] = jnp.zeros_like(token_ref)
        held = pl.program_id(0) == at[CORE_AT]
        result_ref[...] = jnp.where(held, own_ref[...], other_ref[...])

    slab_half = pl.BlockSpec((half, slab), lambda i, at: (0, at[CORE_AT]))
    grad_slab, slab_done = call(
        slab_kernel, at, [own_half, other_half], [slab_half] * 2, [shape(weight.shape), shape((8, 128), F32)],
        [pl.BlockSpec((half, slab), lambda i, at: (i, 0)), pl.BlockSpec((8, 128), lambda i, at: (0, 0))],
        (2,), after=totals,
    )

    own, near, came_near, came_own = scatter_sends(*left)

    def place_kernel(at, *refs):
        refs[-1][...] = jnp.zeros_like(refs[-1])
        for j in range(N_Y):

            @pl.when(pl.program_id(0) == j)
            def _():
                refs[-2][...] = refs[j][...]

    def go_round(k, total, grad_hidden, after):
        near = send(total, Y_SECOND)
        off = send(total, Y_FIRST)
        opposite = send(near, Y_FIRST)
        given = [total, near, off, opposite]
        specs = [pl.BlockSpec(total.shape, lambda i, at: (0, 0))] * N_Y
        if k > 0:
            given, specs = given + [grad_hidden], specs + [ANY]
        return call(
            place_kernel, at, given, specs, [shape(hidden.shape), shape((8, 128), F32)],
            [
                pl.BlockSpec(total.shape, lambda i, at: (at[Y + i], k)),
                pl.BlockSpec((8, 128), lambda i, at: (0, 0)),
            ],
            (N_Y,), aliases={N_Y + 1: 0} if k > 0 else None, after=after,
        )

    blocks = (num * mine_rows, BLK)
    near = add(at, [near.reshape(blocks), came_near.reshape(blocks)], after=[slab_done, came_own, beside[1]])
    totals.append(add(at, [mine[1], beside[1]], after=[near]))
    grad_hidden, placed = go_round(0, totals[0], None, [totals[1]])
    upper = pair // 2

    def right_kernel(at, own_ref, other_ref, own_slab_ref, other_slab_ref, keep_ref, send_ref, total_ref):
        i = pl.program_id(0)
        value = dot(own_ref[...], own_slab_ref[...], 0, 0) + dot(other_ref[...], other_slab_ref[...], 0, 0)

        @pl.when(i == 0)
        def _():
            total_ref[...] = value

        @pl.when(i > 0)
        def _():
            total_ref[...] += value

        @pl.when(i == pl.num_programs(0) - 1)
        def _():
            here = at[Z_HIGH] * upper
            there = (1 - at[Z_HIGH]) * upper
            keep_ref[...] = total_ref[pl.ds(pl.multiple_of(here, upper), upper)] / FF
            send_ref[...] = (total_ref[pl.ds(pl.multiple_of(there, upper), upper)] / FF).astype(BF16)

    steps = 2
    rows_spec = pl.BlockSpec((half // steps, pair), lambda i, at: (i, 0))
    slab_spec = pl.BlockSpec((half // steps, slab), lambda i, at: (i, at[CORE_AT]))
    upper_spec = pl.BlockSpec((upper, slab), lambda i, at: (0, 0))

    stay, go = call(
        right_kernel, at, [own_half, other_half, own_half, other_half],
        [rows_spec, rows_spec, slab_spec, slab_spec],
        [shape((upper, slab), F32), shape((upper, slab))], [upper_spec] * 2, (steps,),
        scratch=[pltpu.VMEM((pair, slab), F32)], after=totals[1:],
    )

    def right_sum(stay, came, bit):
        rows = stay.shape[0] // 2

        def kernel(at_ref, stay_ref, came_ref, keep_ref, send_ref):
            total = stay_ref[...] + came_ref[...].astype(F32)
            here = at_ref[bit] == 0
            keep_ref[...] = jnp.where(here, total[:rows], total[rows:])
            send_ref[...] = jnp.where(here, total[rows:], total[:rows]).astype(BF16)

        whole = pl.BlockSpec(stay.shape, lambda i, at: (0, 0))
        half_of = pl.BlockSpec((rows, slab), lambda i, at: (0, 0))
        return call(
            kernel, at, [stay, came], [whole] * 2, [shape((rows, slab), F32), shape((rows, slab))], [half_of] * 2
        )

    right_steps = []
    for i, bit in enumerate(bits):
        came_z = lax.ppermute(go, "col", [(j, j ^ bit) for j in range(cols)])
        if i < len(bits) - 1:
            stay, go = right_sum(stay, came_z, Z_HIGH + 1 + i)
            right_steps.append(stay)

    near = near.reshape(own.shape)
    def left_sum(parts, groups, bit, after=()):
        def kernel(at_ref, *refs):
            total = refs[0][...].astype(F32)
            for ref in refs[1:-2]:
                total = total + ref[...].astype(F32)
            total = total.reshape((num * groups // 2, 2, 16, BLK))
            stays = at_ref[bit] == 0
            rows = (num, groups * 8, BLK)
            refs[-2][...] = jnp.where(stays, total[:, 0], total[:, 1]).reshape(rows)
            refs[-1][...] = jnp.where(stays, total[:, 1], total[:, 0]).reshape(rows).astype(BF16)

        whole = pl.BlockSpec((num, groups * 16, BLK), lambda a, at: (0, 0, 0))
        half_of = pl.BlockSpec((num, groups * 8, BLK), lambda a, at: (0, 0, 0))
        return call(
            kernel, at, parts, [whole] * len(parts),
            [shape((num, groups * 8, BLK), F32), shape((num, groups * 8, BLK))], [half_of] * 2, after=after,
        )

    stays, goes = left_sum([own, came_own, send(near, Y_SECOND)], 4, X_LO_AT)
    stays, goes = left_sum([stays, send(goes, X_LO)], 2, X_HI_AT)
    left_stats = stays + send(goes, X_HI).astype(F32)

    def last_kernel(at, mine_ref, came_ref, result_ref):
        result_ref[...] = mine_ref[...] + came_ref[...].astype(F32)

    spec = pl.BlockSpec(stay.shape, lambda i, at: (0, 0))
    right_stats = call(
        last_kernel, at, [stay, came_z], [spec] * 2, [shape(stay.shape, F32)], [spec], after=[placed]
    )[0].T

    grad_hidden, _ = go_round(1, totals[1], grad_hidden, [left_stats, right_stats])
    return grad_hidden, grad_slab, left_stats, right_stats


def solution(mesh):
    return jax.shard_map(
        body,
        mesh=mesh,
        in_specs=(P("rep", "col"), P("rep", "row"), P("col", ("row", "rep"))),
        out_specs=(
            P("rep", "col"),
            P("col", ("row", "rep")),
            P("col", ("row", "rep"), None),
            P(("row", "rep"), "col"),
        ),
        check_vma=False,
    )
```

time: 200 us -> 171 us (0.85)
  Pallas kernels: 58.7 us -> 46.3 us
  local copies, waits for them, and re-layouts: 14.5 us -> 3.17 us
  other arithmetic: 4.49 us -> 0.03 us
  starting transfers between devices: 54.2 us -> 51.9 us
    pallas_call x23 -> x28, Pallas kernels: 58.7 us -> 46.3 us  [call(): pl.pallas_call(run, grid_spec=pltpu.PrefetchScalarGridSpec(num_scalar_pre...]
    unnamed x58 -> x10, local copies, waits for them, and re-layouts: 11.5 us -> 2.1 us
    ppermute x31 -> x33, starting transfers between devices: 44.4 us -> 40.1 us  [send(): return lax.ppermute(x, ('row', 'rep'), perm)]
    ppermute x3, waiting for transfers between devices: 2.19 us -> 4.73 us  [body(): came_z = lax.ppermute(go, 'col', [(j, j ^ bit) for j in range(cols)])]
    add x5 -> x1, other arithmetic: 2.36 us -> 0.03 us  [body(): left_stats = stays + send(goes, X_HI).astype(F32)]
    convert_element_type x1 -> x0, other arithmetic: 2.13 us -> none  [body(): near = (near.astype(F32) + came_near.astype(F32)).astype(BF16)]
    ppermute x3, starting transfers between devices: 9.76 us -> 11.8 us  [body(): came_z = lax.ppermute(go, 'col', [(j, j ^ bit) for j in range(cols)])]
    ppermute x31 -> x33, waiting for transfers between devices: 63.9 us -> 62.7 us  [send(): return lax.ppermute(x, ('row', 'rep'), perm)]
  transfers between devices with their start and end apart: 34 -> 36, of which waited for: 16 -> 20; matrix products, arithmetic and copies ran while one was open for 3% -> 1% of each run, Pallas kernels for 18% -> 21%
where the time goes in v2:
time: 171 us; the launch traced here: 170 us
  waiting for transfers between devices  67.4 us (39%)
  starting transfers between devices  51.9 us (30%)
  Pallas kernels  46.3 us (27%)
  local copies, waits for them, and re-layouts  3.17 us (2%)
    ppermute x33, waiting for transfers between devices, send(): return lax.ppermute(x, ('row', 'rep'), perm)  62.7 us
    pallas_call x28, Pallas kernels, call(): pl.pallas_call(run, grid_spec=pltpu.PrefetchScalarGridSpec(num_scalar_pre...  46.3 us
    ppermute x33, starting transfers between devices, send(): return lax.ppermute(x, ('row', 'rep'), perm)  40.1 us
    ppermute x3, starting transfers between devices, body(): came_z = lax.ppermute(go, 'col', [(j, j ^ bit) for j in range(cols)])  11.8 us
    ppermute x3, waiting for transfers between devices, body(): came_z = lax.ppermute(go, 'col', [(j, j ^ bit) for j in range(cols)])  4.73 us
  transfers between devices with their start and end apart: 36, of which 20 were waited for; matrix products, arithmetic and copies ran while one was open for 1% of the time, Pallas kernels for 21%

profile of v2, /device:TPU:32, one launch (start us, length us, event | category | flops | bytes accessed | tf_op | source)
XLA Modules:
  0.0 169.8 jit_solution(13386541817078637135)
XLA Ops:
  1.3 2.0 %copy-done = bf16[512,3584]{1,0:T(8,128)(2,1)S(1)} copy-done((bf16[512,3584]{1,0:T(8,128)(2,1)S(1)}, bf16[512,3584]{1,0:T(8,128)(2,1)}, u32[]{:S(2)}) %copy-start) | copy-done | bytes 3670040
  4.0 2.8 %collective-permute-start.5 = (bf16[512,1024]{1,0:T(8,128)(2,1)S(1)}, bf16[512,1024]{1,0:T(8,128)(2,1)S(1)}, u32[]{:S(2)}, u32[]{:S(2)}) collective-permute-start(bf16[512,1024]{1,0:T(8,128)(2,1)S(1)} %shard_map.66.refs_2_), channel_id=1, source_target_pairs={{0,34},{1,35},{2,32},{3,33},{32,2},{33,3},{34,0},{35,1},{64,98},{6... | collective-permute-start | bytes 3145736 | tf_op jit(solution)/shard_map/ppermute | solution.py:40
  9.3 6.4 %shard_map.69.refs_4_.refs_0_ = f32[1792,512]{1,0:T(8,128)S(1)} custom-call(s32[14]{0:T(128)S(1)} %stack.59.at_ref, bf16[512,3584]{1,0:T(8,128)(2,1)S(1)} %copy-done.1, bf16[512,3584]{1,0:T(8,128)(2,1)} %collective-permute-done.3.refs_1_, bf16[512,1024]{1,0:T(8,128)(2,1)S(1)} %copy-done.3, bf16[512,1024]{1,0:T(8,128)(2,1)S(1)} %collective-permute-done.4.refs_3_, ...), custom_call_target="tpu_custom_call" | custom-call | flops 1 | bytes 1 | tf_op jit(solution)/shard_map/pallas_call | solution.py:56
  15.7 3.1 %shard_map.70.refs_1_ = bf16[1024,512]{1,0:T(8,128)(2,1)S(1)} custom-call(s32[14]{0:T(128)S(1)} %stack.59.at_ref, bf16[512,3584]{1,0:T(8,128)(2,1)S(1)} %copy-done.1, bf16[512,3584]{1,0:T(8,128)(2,1)} %collective-permute-done.3.refs_1_, bf16[512,1024]{1,0:T(8,128)(2,1)S(1)} %copy-done.3, bf16[512,1024]{1,0:T(8,128)(2,1)S(1)} %collective-permute-done.4.refs_3_, ...), custom_call_target="tpu_custom_call" | custom-call | flops 1 | bytes 1 | tf_op jit(solution)/shard_map/pallas_call | solution.py:56
  18.9 10.3 %collective-permute-done.2.refs_0_.refs_3_ = bf16[1792,256]{1,0:T(8,128)(2,1)S(1)} collective-permute-done((bf16[1792,256]{1,0:T(8,128)(2,1)S(1)}, bf16[1792,256]{1,0:T(8,128)(2,1)S(1)}, u32[]{:S(2)}, u32[]{:S(2)}) %collective-permute-start.2) | collective-permute-done | bytes 917536 | tf_op jit(solution)/shard_map/ppermute | solution.py:40
  29.1 1.4 collective-permute-done.5.refs_2_.refs_1_
  31.3 2.4 %collective-permute-done.6.refs_4_ = bf16[1792,256]{1,0:T(8,128)(2,1)S(1)} collective-permute-done((bf16[1792,256]{1,0:T(8,128)(2,1)S(1)}, bf16[1792,256]{1,0:T(8,128)(2,1)S(1)}, u32[]{:S(2)}, u32[]{:S(2)}) %collective-permute-start.6) | collective-permute-done | bytes 917536 | tf_op jit(solution)/shard_map/ppermute | solution.py:40
  33.7 3.3 %shard_map.72 = (bf16[128,1792]{1,0:T(8,128)(2,1)S(1)}, bf16[128,1792]{1,0:T(8,128)(2,1)S(1)}, bf16[128,1792]{1,0:T(8,128)(2,1)S(1)}, bf16[128,1792]{1,0:T(8,128)(2,1)S(1)}) custom-call(s32[14]{0:T(128)S(1)} %stack.59.at_ref, bf16[512,1024]{1,0:T(8,128)(2,1)S(1)} %shard_map.68.refs_4_.refs_0_, bf16[3584,256]{1,0:T(8,128)(2,1)S(1)} %copy-done.2, ...), custom_call_target="tpu_custom_call" | custom-call | flops 1 | bytes 1 | tf_op jit(solution)/shard_map/pallas_call | solution.py:56
  37.0 1.7 collective-permute-start.8
  38.9 3.4 %collective-permute-start.10 = (bf16[512,768]{1,0:T(8,128)(2,1)S(1)}, bf16[512,768]{1,0:T(8,128)(2,1)S(1)}, u32[]{:S(2)}, u32[]{:S(2)}) collective-permute-start(bf16[512,768]{1,0:T(8,128)(2,1)S(1)} %get-tuple-element.40), channel_id=1, source_target_pairs={{0,35},{1,34},{2,33},{3,32},{32,3},{33,2},{34,1},{35,0},{64,99},{6... | collective-permute-start | bytes 2359304 | tf_op jit(solution)/shard_map/ppermute | solution.py:40
  42.4 3.1 %collective-permute-done.8.refs_1_ = bf16[128,1792]{1,0:T(8,128)(2,1)S(1)} collective-permute-done((bf16[128,1792]{1,0:T(8,128)(2,1)S(1)}, bf16[128,1792]{1,0:T(8,128)(2,1)S(1)}, u32[]{:S(2)}, u32[]{:S(2)}) %collective-permute-start.8) | collective-permute-done | bytes 458784 | tf_op jit(solution)/shard_map/ppermute | solution.py:40
  46.4 3.1 %collective-permute-start.9 = (bf16[128,1792]{1,0:T(8,128)(2,1)S(1)}, bf16[128,1792]{1,0:T(8,128)(2,1)S(1)}, u32[]{:S(2)}, u32[]{:S(2)}) collective-permute-start(bf16[128,1792]{1,0:T(8,128)(2,1)S(1)} %shard_map.73), channel_id=1, source_target_pairs={{0,192},{1,65},{2,194},{3,67},{32,224},{33,97},{34,226},{35,99},{6... | collective-permute-start | bytes 1376264 | tf_op jit(solution)/shard_map/ppermute | solution.py:40
  49.5 2.4 %collective-permute-done.7.refs_1_ = bf16[128,1792]{1,0:T(8,128)(2,1)S(1)} collective-permute-done((bf16[128,1792]{1,0:T(8,128)(2,1)S(1)}, bf16[128,1792]{1,0:T(8,128)(2,1)S(1)}, u32[]{:S(2)}, u32[]{:S(2)}) %collective-permute-start.7) | collective-permute-done | bytes 458784 | tf_op jit(solution)/shard_map/ppermute | solution.py:40
  51.9 4.3 %collective-permute-done.9.refs_2_ = bf16[128,1792]{1,0:T(8,128)(2,1)S(1)} collective-permute-done((bf16[128,1792]{1,0:T(8,128)(2,1)S(1)}, bf16[128,1792]{1,0:T(8,128)(2,1)S(1)}, u32[]{:S(2)}, u32[]{:S(2)}) %collective-permute-start.9) | collective-permute-done | bytes 458784 | tf_op jit(solution)/shard_map/ppermute | solution.py:40
  57.1 2.6 %collective-permute-done.10.refs_2_.refs_3_ = bf16[512,768]{1,0:T(8,128)(2,1)S(1)} collective-permute-done((bf16[512,768]{1,0:T(8,128)(2,1)S(1)}, bf16[512,768]{1,0:T(8,128)(2,1)S(1)}, u32[]{:S(2)}, u32[]{:S(2)}) %collective-permute-start.10) | collective-permute-done | bytes 786464 | tf_op jit(solution)/shard_map/ppermute | solution.py:40
  59.7 1.9 %collective-permute-done.1.refs_0_.refs_3_ = bf16[1792,256]{1,0:T(8,128)(2,1)S(1)} collective-permute-done((bf16[1792,256]{1,0:T(8,128)(2,1)S(1)}, bf16[1792,256]{1,0:T(8,128)(2,1)S(1)}, u32[]{:S(2)}, u32[]{:S(2)}) %collective-permute-start.1) | collective-permute-done | bytes 917536 | tf_op jit(solution)/shard_map/ppermute | solution.py:40
  62.7 2.0 %collective-permute-done.11.refs_4_ = bf16[1792,256]{1,0:T(8,128)(2,1)S(1)} collective-permute-done((bf16[1792,256]{1,0:T(8,128)(2,1)S(1)}, bf16[1792,256]{1,0:T(8,128)(2,1)S(1)}, u32[]{:S(2)}, u32[]{:S(2)}) %collective-permute-start.11) | collective-permute-done | bytes 917536 | tf_op jit(solution)/shard_map/ppermute | solution.py:40
  64.8 3.3 %shard_map.76 = (bf16[128,1792]{1,0:T(8,128)(2,1)S(1)}, bf16[128,1792]{1,0:T(8,128)(2,1)S(1)}, bf16[128,1792]{1,0:T(8,128)(2,1)S(1)}, bf16[128,1792]{1,0:T(8,128)(2,1)S(1)}) custom-call(s32[14]{0:T(128)S(1)} %stack.59.at_ref, bf16[512,1024]{1,0:T(8,128)(2,1)S(1)} %shard_map.68.refs_4_.refs_0_, bf16[3584,256]{1,0:T(8,128)(2,1)S(1)} %copy-done.2, ...), custom_call_target="tpu_custom_call" | custom-call | flops 1 | bytes 1 | tf_op jit(solution)/shard_map/pallas_call | solution.py:56
  68.9 2.5 %collective-permute-start.17 = (bf16[512,512]{1,0:T(8,128)(2,1)S(1)}, bf16[512,512]{1,0:T(8,128)(2,1)S(1)}, u32[]{:S(2)}, u32[]{:S(2)}) collective-permute-start(bf16[512,512]{1,0:T(8,128)(2,1)S(1)} %get-tuple-element.46), channel_id=1, source_target_pairs={{0,35},{1,34},{2,33},{3,32},{32,3},{33,2},{34,1},{35,0},{64,99},{6... | collective-permute-start | bytes 1572872 | tf_op jit(solution)/shard_map/ppermute | solution.py:40
  71.7 4.9 %collective-permute-done.13.refs_1_ = bf16[128,1792]{1,0:T(8,128)(2,1)S(1)} collective-permute-done((bf16[128,1792]{1,0:T(8,128)(2,1)S(1)}, bf16[128,1792]{1,0:T(8,128)(2,1)S(1)}, u32[]{:S(2)}, u32[]{:S(2)}) %collective-permute-start.13) | collective-permute-done | bytes 458784 | tf_op jit(solution)/shard_map/ppermute | solution.py:40
  77.4 1.1 collective-permute-start.14
  78.6 2.8 %collective-permute-start.16 = (bf16[512,256]{1,0:T(8,128)(2,1)S(1)}, bf16[512,256]{1,0:T(8,128)(2,1)S(1)}, u32[]{:S(2)}, u32[]{:S(2)}) collective-permute-start(bf16[512,256]{1,0:T(8,128)(2,1)S(1)} %get-tuple-element.45), channel_id=1, source_target_pairs={{0,34},{1,35},{2,32},{3,33},{32,2},{33,3},{34,0},{35,1},{64,98},{6... | collective-permute-start | bytes 786440 | tf_op jit(solution)/shard_map/ppermute | solution.py:40
  82.3 4.9 %collective-permute-done.14.refs_2_ = bf16[128,1792]{1,0:T(8,128)(2,1)S(1)} collective-permute-done((bf16[128,1792]{1,0:T(8,128)(2,1)S(1)}, bf16[128,1792]{1,0:T(8,128)(2,1)S(1)}, u32[]{:S(2)}, u32[]{:S(2)}) %collective-permute-start.14) | collective-permute-done | bytes 458784 | tf_op jit(solution)/shard_map/ppermute | solution.py:40
  88.1 1.8 %collective-permute-done.16.refs_2_ = bf16[512,256]{1,0:T(8,128)(2,1)S(1)} collective-permute-done((bf16[512,256]{1,0:T(8,128)(2,1)S(1)}, bf16[512,256]{1,0:T(8,128)(2,1)S(1)}, u32[]{:S(2)}, u32[]{:S(2)}) %collective-permute-start.16) | collective-permute-done | bytes 262176 | tf_op jit(solution)/shard_map/ppermute | solution.py:40
  90.7 1.9 %collective-permute-done.19.refs_6_ = bf16[512,512]{1,0:T(8,128)(2,1)S(1)} collective-permute-done((bf16[512,512]{1,0:T(8,128)(2,1)S(1)}, bf16[512,512]{1,0:T(8,128)(2,1)S(1)}, u32[]{:S(2)}, u32[]{:S(2)}) %collective-permute-start.19) | collective-permute-done | bytes 524320 | tf_op jit(solution)/shard_map/ppermute | solution.py:40
  92.6 3.6 %shard_map.80.refs_0_.refs_1_.refs_4_.refs_2_ = bf16[1792,512]{1,0:T(8,128)(2,1)S(1)} custom-call(s32[14]{0:T(128)S(1)} %stack.59.at_ref, f32[1792,512]{1,0:T(8,128)S(1)} %shard_map.69.refs_4_.refs_0_, bf16[512,1024]{1,0:T(8,128)(2,1)S(1)} %collective-permute-done.5.refs_2_.refs_1_, bf16[512,256]{1,0:T(8,128)(2,1)S(1)} %collective-permute-done.16.refs_2_, ...), custom_call_target="tpu_custom_call" | custom-call | flops 1 | bytes 1 | tf_op jit(solution)/shard_map/pallas_call | solution.py:56
  97.1 2.8 %collective-permute-start.15 = (bf16[128,1792]{1,0:T(8,128)(2,1)S(1)}, bf16[128,1792]{1,0:T(8,128)(2,1)S(1)}, u32[]{:S(2)}, u32[]{:S(2)}) collective-permute-start(bf16[128,1792]{1,0:T(8,128)(2,1)S(1)} %shard_map.78.refs_1_.refs_9_.refs_0_), channel_id=1, source_target_pairs={{0,32},{1,33},{2,34},{3,35},{32,0},{33,1},{34,2},{35,3},{64,96},{6... | collective-permute-start | bytes 1376264 | tf_op jit(solution)/shard_map/ppermute | solution.py:40
  100.1 3.4 %shard_map.81 = (bf16[7,64,512]{2,1,0:T(8,128)(2,1)S(1)}, bf16[7,64,512]{2,1,0:T(8,128)(2,1)S(1)}, bf16[7,64,512]{2,1,0:T(8,128)(2,1)S(1)}, bf16[7,64,512]{2,1,0:T(8,128)(2,1)S(1)}) custom-call(s32[14]{0:T(128)S(1)} %stack.59.at_ref, bf16[1792,512]{1,0:T(8,128)(2,1)S(1)} %shard_map.80.refs_0_.refs_1_.refs_4_.refs_2_, ...), custom_call_target="tpu_custom_call" | custom-call | flops 1 | bytes 1 | tf_op jit(solution)/shard_map/pallas_call | solution.py:56
  103.5 1.3 collective-permute-start.21
  105.6 5.7 %collective-permute-done.22.refs_1_ = bf16[128,1792]{1,0:T(8,128)(2,1)S(1)} collective-permute-done((bf16[128,1792]{1,0:T(8,128)(2,1)S(1)}, bf16[128,1792]{1,0:T(8,128)(2,1)S(1)}, u32[]{:S(2)}, u32[]{:S(2)}) %collective-permute-start.22) | collective-permute-done | bytes 458784 | tf_op jit(solution)/shard_map/ppermute | solution.py:40
  112.1 1.8 %collective-permute-start.27 = (bf16[128,1792]{1,0:T(8,128)(2,1)S(1)}, bf16[128,1792]{1,0:T(8,128)(2,1)S(1)}, u32[]{:S(2)}, u32[]{:S(2)}) collective-permute-start(bf16[128,1792]{1,0:T(8,128)(2,1)S(1)} %shard_map.82.refs_2_.refs_0_), channel_id=1, source_target_pairs={{0,192},{1,65},{2,194},{3,67},{32,224},{33,97},{34,226},{35,99},{6... | collective-permute-start | bytes 1376264 | tf_op jit(solution)/shard_map/ppermute | solution.py:40
  113.9 2.0 %shard_map.83 = (bf16[3584,256]{1,0:T(8,128)(2,1)}, f32[8,128]{1,0:T(8,128)S(1)}) custom-call(s32[14]{0:T(128)S(1)} %stack.59.at_ref, bf16[1792,512]{1,0:T(8,128)(2,1)S(1)} %shard_map.80.refs_0_.refs_1_.refs_4_.refs_2_, bf16[1792,512]{1,0:T(8,128)(2,1)S(1)} %collective-permute-done.20.refs_2_.refs_3_.refs_1_, bf16[128,1792]{1,0:T(8,128)(2,1)S(1)} %shard_map.82.refs_2_.refs_0_), custom_call_target="tpu_custom_call" | custom-call | flops 1 | bytes 1 | tf_op jit(solution)/shard_map/pallas_call | solution.py:56
  116.0 4.6 %collective-permute-done.15.refs_4_.refs_1_ = bf16[128,1792]{1,0:T(8,128)(2,1)S(1)} collective-permute-done((bf16[128,1792]{1,0:T(8,128)(2,1)S(1)}, bf16[128,1792]{1,0:T(8,128)(2,1)S(1)}, u32[]{:S(2)}, u32[]{:S(2)}) %collective-permute-start.15) | collective-permute-done | bytes 458784 | tf_op jit(solution)/shard_map/ppermute | solution.py:40
  121.4 1.8 %collective-permute-start.30 = (bf16[7,64,512]{2,1,0:T(8,128)(2,1)S(1)}, bf16[7,64,512]{2,1,0:T(8,128)(2,1)S(1)}, u32[]{:S(2)}, u32[]{:S(2)}) collective-permute-start(bf16[7,64,512]{2,1,0:T(8,128)(2,1)S(1)} %bitcast.19), channel_id=1, source_target_pairs={{0,192},{1,65},{2,194},{3,67},{32,224},{33,97},{34,226},{35,99},{6... | collective-permute-start | bytes 1376264 | tf_op jit(solution)/shard_map/ppermute | solution.py:40
  124.0 1.6 collective-permute-start.24
  125.7 2.0 %collective-permute-start.29 = (bf16[128,1792]{1,0:T(8,128)(2,1)S(1)}, bf16[128,1792]{1,0:T(8,128)(2,1)S(1)}, u32[]{:S(2)}, u32[]{:S(2)}) collective-permute-start(bf16[128,1792]{1,0:T(8,128)(2,1)S(1)} %collective-permute-done.27.refs_1_), channel_id=1, source_target_pairs={{0,64},{1,193},{2,66},{3,195},{32,96},{33,225},{34,98},{35,227},{6... | collective-permute-start | bytes 1376264 | tf_op jit(solution)/shard_map/ppermute | solution.py:40
  127.6 7.5 %collective-permute-done.30.refs_2_ = bf16[7,64,512]{2,1,0:T(8,128)(2,1)S(1)} collective-permute-done((bf16[7,64,512]{2,1,0:T(8,128)(2,1)S(1)}, bf16[7,64,512]{2,1,0:T(8,128)(2,1)S(1)}, u32[]{:S(2)}, u32[]{:S(2)}) %collective-permute-start.30) | collective-permute-done | bytes 458784 | tf_op jit(solution)/shard_map/ppermute | solution.py:40
  136.0 2.4 %shard_map.89 = (f32[256,256]{1,0:T(8,128)S(1)}, bf16[256,256]{1,0:T(8,128)(2,1)S(1)}) custom-call(s32[14]{0:T(128)S(1)} %stack.59.at_ref, bf16[1792,512]{1,0:T(8,128)(2,1)S(1)} %shard_map.80.refs_0_.refs_1_.refs_4_.refs_2_, bf16[1792,512]{1,0:T(8,128)(2,1)S(1)} %collective-permute-done.20.refs_2_.refs_3_.refs_1_, ...), custom_call_target="tpu_custom_call" | custom-call | flops 1 | bytes 1 | tf_op jit(solution)/shard_map/pallas_call | solution.py:56
  138.4 6.6 %collective-permute-start.33 = (bf16[256,256]{1,0:T(8,128)(2,1)S(1)}, bf16[256,256]{1,0:T(8,128)(2,1)S(1)}, u32[]{:S(2)}, u32[]{:S(2)}) collective-permute-start(bf16[256,256]{1,0:T(8,128)(2,1)S(1)} %get-tuple-element.58), channel_id=1, source_target_pairs={{0,16},{4,20},{8,24},{12,28},{16,0},{20,4},{24,8},{28,12},{1,17},{... | collective-permute-start | bytes 393224 | tf_op jit(solution)/shard_map/ppermute | solution.py:422
  145.0 3.0 %collective-permute-done.33.refs_1_ = bf16[256,256]{1,0:T(8,128)(2,1)S(1)} collective-permute-done((bf16[256,256]{1,0:T(8,128)(2,1)S(1)}, bf16[256,256]{1,0:T(8,128)(2,1)S(1)}, u32[]{:S(2)}, u32[]{:S(2)}) %collective-permute-start.33) | collective-permute-done | bytes 131104 | tf_op jit(solution)/shard_map/ppermute | solution.py:422
  148.0 2.0 %collective-permute-start.26 = (bf16[128,1792]{1,0:T(8,128)(2,1)S(1)}, bf16[128,1792]{1,0:T(8,128)(2,1)S(1)}, u32[]{:S(2)}, u32[]{:S(2)}) collective-permute-start(bf16[128,1792]{1,0:T(8,128)(2,1)S(1)} %collective-permute-done.24.refs_1_), channel_id=1, source_target_pairs={{0,64},{1,193},{2,66},{3,195},{32,96},{33,225},{34,98},{35,227},{6... | collective-permute-start | bytes 1376264 | tf_op jit(solution)/shard_map/ppermute | solution.py:40
  150.6 2.9 %collective-permute-start.34 = (bf16[128,256]{1,0:T(8,128)(2,1)S(1)}, bf16[128,256]{1,0:T(8,128)(2,1)S(1)}, u32[]{:S(2)}, u32[]{:S(2)}) collective-permute-start(bf16[128,256]{1,0:T(8,128)(2,1)S(1)} %get-tuple-element.60), channel_id=1, source_target_pairs={{0,8},{4,12},{8,0},{12,4},{16,24},{20,28},{24,16},{28,20},{1,9},{5... | collective-permute-start | bytes 196616 | tf_op jit(solution)/shard_map/ppermute | solution.py:422
  154.1 1.7 %collective-permute-done.34.refs_1_ = bf16[128,256]{1,0:T(8,128)(2,1)S(1)} collective-permute-done((bf16[128,256]{1,0:T(8,128)(2,1)S(1)}, bf16[128,256]{1,0:T(8,128)(2,1)S(1)}, u32[]{:S(2)}, u32[]{:S(2)}) %collective-permute-start.34) | collective-permute-done | bytes 65568 | tf_op jit(solution)/shard_map/ppermute | solution.py:422
  155.9 4.2 %collective-permute-start.32 = (bf16[7,16,512]{2,1,0:T(8,128)(2,1)S(1)}, bf16[7,16,512]{2,1,0:T(8,128)(2,1)S(1)}, u32[]{:S(2)}, u32[]{:S(2)}) collective-permute-start(bf16[7,16,512]{2,1,0:T(8,128)(2,1)S(1)} %get-tuple-element.56), channel_id=1, source_target_pairs={{0,32},{1,33},{2,34},{3,35},{32,0},{33,1},{34,2},{35,3},{64,96},{6... | collective-permute-start | bytes 344072 | tf_op jit(solution)/shard_map/ppermute | solution.py:40
  160.7 2.2 %collective-permute-start.35 = (bf16[64,256]{1,0:T(8,128)(2,1)S(1)}, bf16[64,256]{1,0:T(8,128)(2,1)S(1)}, u32[]{:S(2)}, u32[]{:S(2)}) collective-permute-start(bf16[64,256]{1,0:T(8,128)(2,1)S(1)} %get-tuple-element.62), channel_id=1, source_target_pairs={{0,4},{4,0},{8,12},{12,8},{16,20},{20,16},{24,28},{28,24},{1,5},{5... | collective-permute-start | bytes 98312 | tf_op jit(solution)/shard_map/ppermute | solution.py:422
  162.9 2.3 %shard_map.86 = (bf16[512,3584]{1,0:T(8,128)(2,1)}, f32[8,128]{1,0:T(8,128)S(1)}) custom-call(s32[14]{0:T(128)S(1)} %stack.59.at_ref, bf16[128,1792]{1,0:T(8,128)(2,1)S(1)} %shard_map.82.refs_2_.refs_0_, bf16[128,1792]{1,0:T(8,128)(2,1)S(1)} %collective-permute-done.27.refs_1_, bf16[128,1792]{1,0:T(8,128)(2,1)S(1)} %collective-permute-done.28.refs_2_, ...), custom_call_target="tpu_custom_call" | custom-call | flops 1 | bytes 1 | tf_op jit(solution)/shard_map/pallas_call | solution.py:56
  165.3 1.2 shard_map.92
  167.5 2.4 %shard_map.93 = (bf16[512,3584]{1,0:T(8,128)(2,1)}, f32[8,128]{1,0:T(8,128)}) custom-call(s32[14]{0:T(128)S(1)} %stack.59.at_ref, bf16[128,1792]{1,0:T(8,128)(2,1)S(1)} %shard_map.85.refs_4_.refs_0_, bf16[128,1792]{1,0:T(8,128)(2,1)S(1)} %collective-permute-done.24.refs_1_, ...), custom_call_target="tpu_custom_call", output_to_operand_aliasing={{0}: (5, {})} | custom-call | flops 1 | bytes 1 | tf_op jit(solution)/shard_map/pallas_call | solution.py:56
  (66 shorter events, 20.4 us)
Async XLA Ops:
  0.6 8.6 %collective-permute-start.3 = (bf16[512,3584]{1,0:T(8,128)(2,1)}, bf16[512,3584]{1,0:T(8,128)(2,1)}, u32[]{:S(2)}, u32[]{:S(2)}) collective-permute-start(bf16[512,3584]{1,0:T(8,128)(2,1)} %refs_0_.9), channel_id=1, source_target_pairs={{0,1},{1,0},{2,3},{3,2},{32,33},{33,32},{34,35},{35,34},{64,65},{6... | collective-permute-start | bytes 11010056 | tf_op jit(solution)/shard_map/ppermute | solution.py:40
  0.7 8.5 %collective-permute-start.4 = (bf16[512,1024]{1,0:T(8,128)(2,1)}, bf16[512,1024]{1,0:T(8,128)(2,1)S(1)}, u32[]{:S(2)}, u32[]{:S(2)}) collective-permute-start(bf16[512,1024]{1,0:T(8,128)(2,1)} %refs_2_.3), channel_id=1, source_target_pairs={{0,1},{1,0},{2,3},{3,2},{32,33},{33,32},{34,35},{35,34},{64,65},{6... | collective-permute-start | bytes 3145736 | tf_op jit(solution)/shard_map/ppermute | solution.py:40
  1.3 2.0 %copy-start = (bf16[512,3584]{1,0:T(8,128)(2,1)S(1)}, bf16[512,3584]{1,0:T(8,128)(2,1)}, u32[]{:S(2)}) copy-start(bf16[512,3584]{1,0:T(8,128)(2,1)} %refs_0_.9) | copy-start | bytes 11010052
  3.4 3.5 %copy-start.2 = (bf16[3584,256]{1,0:T(8,128)(2,1)S(1)}, bf16[3584,256]{1,0:T(8,128)(2,1)}, u32[]{:S(2)}) copy-start(bf16[3584,256]{1,0:T(8,128)(2,1)} %refs_1_.5) | copy-start | bytes 5505028
  4.0 26.5 %collective-permute-start.5 = (bf16[512,1024]{1,0:T(8,128)(2,1)S(1)}, bf16[512,1024]{1,0:T(8,128)(2,1)S(1)}, u32[]{:S(2)}, u32[]{:S(2)}) collective-permute-start(bf16[512,1024]{1,0:T(8,128)(2,1)S(1)} %shard_map.66.refs_2_), channel_id=1, source_target_pairs={{0,34},{1,35},{2,32},{3,33},{32,2},{33,3},{34,0},{35,1},{64,98},{6... | collective-permute-start | bytes 3145736 | tf_op jit(solution)/shard_map/ppermute | solution.py:40
  6.9 1.4 copy-start.3
  7.0 2.4 %copy-start.1 = (bf16[512,3584]{1,0:T(8,128)(2,1)S(1)}, bf16[512,3584]{1,0:T(8,128)(2,1)}, u32[]{:S(2)}) copy-start(bf16[512,3584]{1,0:T(8,128)(2,1)} %refs_0_.9) | copy-start | bytes 11010052
  7.0 22.2 %collective-permute-start.2 = (bf16[1792,256]{1,0:T(8,128)(2,1)S(1)}, bf16[1792,256]{1,0:T(8,128)(2,1)S(1)}, u32[]{:S(2)}, u32[]{:S(2)}) collective-permute-start(bf16[1792,256]{1,0:T(8,128)(2,1)S(1)} %slice.3), channel_id=1, source_target_pairs={{0,2},{1,3},{2,0},{3,1},{32,34},{33,35},{34,32},{35,33},{64,66},{6... | collective-permute-start | bytes 2752520 | tf_op jit(solution)/shard_map/ppermute | solution.py:40
  7.3 24.0 %collective-permute-start = (bf16[3584,256]{1,0:T(8,128)(2,1)S(1)}, bf16[3584,256]{1,0:T(8,128)(2,1)S(1)}, u32[]{:S(2)}, u32[]{:S(2)}) collective-permute-start(bf16[3584,256]{1,0:T(8,128)(2,1)S(1)} %copy-done.2), channel_id=1, source_target_pairs={{0,1},{1,0},{2,3},{3,2},{32,33},{33,32},{34,35},{35,34},{64,65},{6... | collective-permute-start | bytes 5505032 | tf_op jit(solution)/shard_map/ppermute | solution.py:40
  31.1 2.6 %collective-permute-start.6 = (bf16[1792,256]{1,0:T(8,128)(2,1)S(1)}, bf16[1792,256]{1,0:T(8,128)(2,1)S(1)}, u32[]{:S(2)}, u32[]{:S(2)}) collective-permute-start(bf16[1792,256]{1,0:T(8,128)(2,1)S(1)} %shard_map.71.refs_5_), channel_id=1, source_target_pairs={{0,1},{1,0},{2,3},{3,2},{32,33},{33,32},{34,35},{35,34},{64,65},{6... | collective-permute-start | bytes 2752520 | tf_op jit(solution)/shard_map/ppermute | solution.py:40
  37.0 8.6 %collective-permute-start.8 = (bf16[128,1792]{1,0:T(8,128)(2,1)S(1)}, bf16[128,1792]{1,0:T(8,128)(2,1)S(1)}, u32[]{:S(2)}, u32[]{:S(2)}) collective-permute-start(bf16[128,1792]{1,0:T(8,128)(2,1)S(1)} %get-tuple-element.39), channel_id=1, source_target_pairs={{0,64},{1,193},{2,66},{3,195},{32,96},{33,225},{34,98},{35,227},{6... | collective-permute-start | bytes 1376264 | tf_op jit(solution)/shard_map/ppermute | solution.py:40
  38.6 22.9 %collective-permute-start.1 = (bf16[1792,256]{1,0:T(8,128)(2,1)S(1)}, bf16[1792,256]{1,0:T(8,128)(2,1)S(1)}, u32[]{:S(2)}, u32[]{:S(2)}) collective-permute-start(bf16[1792,256]{1,0:T(8,128)(2,1)S(1)} %get-tuple-element.35.refs_1_), channel_id=1, source_target_pairs={{0,2},{1,3},{2,0},{3,1},{32,34},{33,35},{34,32},{35,33},{64,66},{6... | collective-permute-start | bytes 2752520 | tf_op jit(solution)/shard_map/ppermute | solution.py:40
  38.9 20.7 %collective-permute-start.10 = (bf16[512,768]{1,0:T(8,128)(2,1)S(1)}, bf16[512,768]{1,0:T(8,128)(2,1)S(1)}, u32[]{:S(2)}, u32[]{:S(2)}) collective-permute-start(bf16[512,768]{1,0:T(8,128)(2,1)S(1)} %get-tuple-element.40), channel_id=1, source_target_pairs={{0,35},{1,34},{2,33},{3,32},{32,3},{33,2},{34,1},{35,0},{64,99},{6... | collective-permute-start | bytes 2359304 | tf_op jit(solution)/shard_map/ppermute | solution.py:40
  42.3 9.6 %collective-permute-start.7 = (bf16[128,1792]{1,0:T(8,128)(2,1)S(1)}, bf16[128,1792]{1,0:T(8,128)(2,1)S(1)}, u32[]{:S(2)}, u32[]{:S(2)}) collective-permute-start(bf16[128,1792]{1,0:T(8,128)(2,1)S(1)} %get-tuple-element.37), channel_id=1, source_target_pairs={{0,64},{1,193},{2,66},{3,195},{32,96},{33,225},{34,98},{35,227},{6... | collective-permute-start | bytes 1376264 | tf_op jit(solution)/shard_map/ppermute | solution.py:40
  46.4 9.8 %collective-permute-start.9 = (bf16[128,1792]{1,0:T(8,128)(2,1)S(1)}, bf16[128,1792]{1,0:T(8,128)(2,1)S(1)}, u32[]{:S(2)}, u32[]{:S(2)}) collective-permute-start(bf16[128,1792]{1,0:T(8,128)(2,1)S(1)} %shard_map.73), channel_id=1, source_target_pairs={{0,192},{1,65},{2,194},{3,67},{32,224},{33,97},{34,226},{35,99},{6... | collective-permute-start | bytes 1376264 | tf_op jit(solution)/shard_map/ppermute | solution.py:40
  62.2 2.6 %collective-permute-start.11 = (bf16[1792,256]{1,0:T(8,128)(2,1)S(1)}, bf16[1792,256]{1,0:T(8,128)(2,1)S(1)}, u32[]{:S(2)}, u32[]{:S(2)}) collective-permute-start(bf16[1792,256]{1,0:T(8,128)(2,1)S(1)} %shard_map.75.refs_5_), channel_id=1, source_target_pairs={{0,1},{1,0},{2,3},{3,2},{32,33},{33,32},{34,35},{35,34},{64,65},{6... | collective-permute-start | bytes 2752520 | tf_op jit(solution)/shard_map/ppermute | solution.py:40
  62.4 27.5 %collective-permute-start.18 = (bf16[1024,512]{1,0:T(8,128)(2,1)S(1)}, bf16[1024,512]{1,0:T(8,128)(2,1)S(1)}, u32[]{:S(2)}, u32[]{:S(2)}) collective-permute-start(bf16[1024,512]{1,0:T(8,128)(2,1)S(1)} %shard_map.70.refs_1_), channel_id=1, source_target_pairs={{0,2},{1,3},{2,0},{3,1},{32,34},{33,35},{34,32},{35,33},{64,66},{6... | collective-permute-start | bytes 3145736 | tf_op jit(solution)/shard_map/ppermute | solution.py:40
  68.0 8.6 %collective-permute-start.13 = (bf16[128,1792]{1,0:T(8,128)(2,1)S(1)}, bf16[128,1792]{1,0:T(8,128)(2,1)S(1)}, u32[]{:S(2)}, u32[]{:S(2)}) collective-permute-start(bf16[128,1792]{1,0:T(8,128)(2,1)S(1)} %get-tuple-element.44), channel_id=1, source_target_pairs={{0,64},{1,193},{2,66},{3,195},{32,96},{33,225},{34,98},{35,227},{6... | collective-permute-start | bytes 1376264 | tf_op jit(solution)/shard_map/ppermute | solution.py:40
  68.9 21.1 %collective-permute-start.17 = (bf16[512,512]{1,0:T(8,128)(2,1)S(1)}, bf16[512,512]{1,0:T(8,128)(2,1)S(1)}, u32[]{:S(2)}, u32[]{:S(2)}) collective-permute-start(bf16[512,512]{1,0:T(8,128)(2,1)S(1)} %get-tuple-element.46), channel_id=1, source_target_pairs={{0,35},{1,34},{2,33},{3,32},{32,3},{33,2},{34,1},{35,0},{64,99},{6... | collective-permute-start | bytes 1572872 | tf_op jit(solution)/shard_map/ppermute | solution.py:40
  71.4 11.0 %collective-permute-start.12 = (bf16[128,1792]{1,0:T(8,128)(2,1)S(1)}, bf16[128,1792]{1,0:T(8,128)(2,1)S(1)}, u32[]{:S(2)}, u32[]{:S(2)}) collective-permute-start(bf16[128,1792]{1,0:T(8,128)(2,1)S(1)} %get-tuple-element.42), channel_id=1, source_target_pairs={{0,64},{1,193},{2,66},{3,195},{32,96},{33,225},{34,98},{35,227},{6... | collective-permute-start | bytes 1376264 | tf_op jit(solution)/shard_map/ppermute | solution.py:40
  77.4 9.8 %collective-permute-start.14 = (bf16[128,1792]{1,0:T(8,128)(2,1)S(1)}, bf16[128,1792]{1,0:T(8,128)(2,1)S(1)}, u32[]{:S(2)}, u32[]{:S(2)}) collective-permute-start(bf16[128,1792]{1,0:T(8,128)(2,1)S(1)} %shard_map.77), channel_id=1, source_target_pairs={{0,192},{1,65},{2,194},{3,67},{32,224},{33,97},{34,226},{35,99},{6... | collective-permute-start | bytes 1376264 | tf_op jit(solution)/shard_map/ppermute | solution.py:40
  78.6 11.4 %collective-permute-start.16 = (bf16[512,256]{1,0:T(8,128)(2,1)S(1)}, bf16[512,256]{1,0:T(8,128)(2,1)S(1)}, u32[]{:S(2)}, u32[]{:S(2)}) collective-permute-start(bf16[512,256]{1,0:T(8,128)(2,1)S(1)} %get-tuple-element.45), channel_id=1, source_target_pairs={{0,34},{1,35},{2,32},{3,33},{32,2},{33,3},{34,0},{35,1},{64,98},{6... | collective-permute-start | bytes 786440 | tf_op jit(solution)/shard_map/ppermute | solution.py:40
  90.6 2.0 %collective-permute-start.19 = (bf16[512,512]{1,0:T(8,128)(2,1)S(1)}, bf16[512,512]{1,0:T(8,128)(2,1)S(1)}, u32[]{:S(2)}, u32[]{:S(2)}) collective-permute-start(bf16[512,512]{1,0:T(8,128)(2,1)S(1)} %shard_map.79), channel_id=1, source_target_pairs={{0,1},{1,0},{2,3},{3,2},{32,33},{33,32},{34,35},{35,34},{64,65},{6... | collective-permute-start | bytes 1572872 | tf_op jit(solution)/shard_map/ppermute | solution.py:40
  96.2 3.9 %collective-permute-start.20 = (bf16[1792,512]{1,0:T(8,128)(2,1)S(1)}, bf16[1792,512]{1,0:T(8,128)(2,1)S(1)}, u32[]{:S(2)}, u32[]{:S(2)}) collective-permute-start(bf16[1792,512]{1,0:T(8,128)(2,1)S(1)} %shard_map.80.refs_0_.refs_1_.refs_4_.refs_2_), channel_id=1, source_target_pairs={{0,1},{1,0},{2,3},{3,2},{32,33},{33,32},{34,35},{35,34},{64,65},{6... | collective-permute-start | bytes 5505032 | tf_op jit(solution)/shard_map/ppermute | solution.py:40
  96.4 14.9 %collective-permute-start.22 = (bf16[128,1792]{1,0:T(8,128)(2,1)S(1)}, bf16[128,1792]{1,0:T(8,128)(2,1)S(1)}, u32[]{:S(2)}, u32[]{:S(2)}) collective-permute-start(bf16[128,1792]{1,0:T(8,128)(2,1)S(1)} %shard_map.74.refs_1_.refs_8_.refs_0_), channel_id=1, source_target_pairs={{0,32},{1,33},{2,34},{3,35},{32,0},{33,1},{34,2},{35,3},{64,96},{6... | collective-permute-start | bytes 1376264 | tf_op jit(solution)/shard_map/ppermute | solution.py:40
  97.1 23.4 %collective-permute-start.15 = (bf16[128,1792]{1,0:T(8,128)(2,1)S(1)}, bf16[128,1792]{1,0:T(8,128)(2,1)S(1)}, u32[]{:S(2)}, u32[]{:S(2)}) collective-permute-start(bf16[128,1792]{1,0:T(8,128)(2,1)S(1)} %shard_map.78.refs_1_.refs_9_.refs_0_), channel_id=1, source_target_pairs={{0,32},{1,33},{2,34},{3,35},{32,0},{33,1},{34,2},{35,3},{64,96},{6... | collective-permute-start | bytes 1376264 | tf_op jit(solution)/shard_map/ppermute | solution.py:40
  103.5 17.1 %collective-permute-start.21 = (bf16[7,64,512]{2,1,0:T(8,128)(2,1)S(1)}, bf16[7,64,512]{2,1,0:T(8,128)(2,1)S(1)}, u32[]{:S(2)}, u32[]{:S(2)}) collective-permute-start(bf16[7,64,512]{2,1,0:T(8,128)(2,1)S(1)} %get-tuple-element.48), channel_id=1, source_target_pairs={{0,64},{1,193},{2,66},{3,195},{32,96},{33,225},{34,98},{35,227},{6... | collective-permute-start | bytes 1376264 | tf_op jit(solution)/shard_map/ppermute | solution.py:40
  104.8 15.7 %collective-permute-start.23 = (bf16[7,64,512]{2,1,0:T(8,128)(2,1)S(1)}, bf16[7,64,512]{2,1,0:T(8,128)(2,1)S(1)}, u32[]{:S(2)}, u32[]{:S(2)}) collective-permute-start(bf16[7,64,512]{2,1,0:T(8,128)(2,1)S(1)} %get-tuple-element.51), channel_id=1, source_target_pairs={{0,64},{1,193},{2,66},{3,195},{32,96},{33,225},{34,98},{35,227},{6... | collective-permute-start | bytes 1376264 | tf_op jit(solution)/shard_map/ppermute | solution.py:40
  112.1 13.5 %collective-permute-start.27 = (bf16[128,1792]{1,0:T(8,128)(2,1)S(1)}, bf16[128,1792]{1,0:T(8,128)(2,1)S(1)}, u32[]{:S(2)}, u32[]{:S(2)}) collective-permute-start(bf16[128,1792]{1,0:T(8,128)(2,1)S(1)} %shard_map.82.refs_2_.refs_0_), channel_id=1, source_target_pairs={{0,192},{1,65},{2,194},{3,67},{32,224},{33,97},{34,226},{35,99},{6... | collective-permute-start | bytes 1376264 | tf_op jit(solution)/shard_map/ppermute | solution.py:40
  121.4 13.7 %collective-permute-start.30 = (bf16[7,64,512]{2,1,0:T(8,128)(2,1)S(1)}, bf16[7,64,512]{2,1,0:T(8,128)(2,1)S(1)}, u32[]{:S(2)}, u32[]{:S(2)}) collective-permute-start(bf16[7,64,512]{2,1,0:T(8,128)(2,1)S(1)} %bitcast.19), channel_id=1, source_target_pairs={{0,192},{1,65},{2,194},{3,67},{32,224},{33,97},{34,226},{35,99},{6... | collective-permute-start | bytes 1376264 | tf_op jit(solution)/shard_map/ppermute | solution.py:40
  124.0 23.9 %collective-permute-start.24 = (bf16[128,1792]{1,0:T(8,128)(2,1)S(1)}, bf16[128,1792]{1,0:T(8,128)(2,1)S(1)}, u32[]{:S(2)}, u32[]{:S(2)}) collective-permute-start(bf16[128,1792]{1,0:T(8,128)(2,1)S(1)} %shard_map.85.refs_4_.refs_0_), channel_id=1, source_target_pairs={{0,192},{1,65},{2,194},{3,67},{32,224},{33,97},{34,226},{35,99},{6... | collective-permute-start | bytes 1376264 | tf_op jit(solution)/shard_map/ppermute | solution.py:40
  125.6 35.1 %collective-permute-start.28 = (bf16[128,1792]{1,0:T(8,128)(2,1)S(1)}, bf16[128,1792]{1,0:T(8,128)(2,1)S(1)}, u32[]{:S(2)}, u32[]{:S(2)}) collective-permute-start(bf16[128,1792]{1,0:T(8,128)(2,1)S(1)} %shard_map.82.refs_2_.refs_0_), channel_id=1, source_target_pairs={{0,64},{1,193},{2,66},{3,195},{32,96},{33,225},{34,98},{35,227},{6... | collective-permute-start | bytes 1376264 | tf_op jit(solution)/shard_map/ppermute | solution.py:40
  125.7 37.3 %collective-permute-start.29 = (bf16[128,1792]{1,0:T(8,128)(2,1)S(1)}, bf16[128,1792]{1,0:T(8,128)(2,1)S(1)}, u32[]{:S(2)}, u32[]{:S(2)}) collective-permute-start(bf16[128,1792]{1,0:T(8,128)(2,1)S(1)} %collective-permute-done.27.refs_1_), channel_id=1, source_target_pairs={{0,64},{1,193},{2,66},{3,195},{32,96},{33,225},{34,98},{35,227},{6... | collective-permute-start | bytes 1376264 | tf_op jit(solution)/shard_map/ppermute | solution.py:40
  135.8 14.7 %collective-permute-start.31 = (bf16[7,32,512]{2,1,0:T(8,128)(2,1)S(1)}, bf16[7,32,512]{2,1,0:T(8,128)(2,1)S(1)}, u32[]{:S(2)}, u32[]{:S(2)}) collective-permute-start(bf16[7,32,512]{2,1,0:T(8,128)(2,1)S(1)} %get-tuple-element.54), channel_id=1, source_target_pairs={{0,2},{1,3},{2,0},{3,1},{32,34},{33,35},{34,32},{35,33},{64,66},{6... | collective-permute-start | bytes 688136 | tf_op jit(solution)/shard_map/ppermute | solution.py:40
  138.4 9.6 %collective-permute-start.33 = (bf16[256,256]{1,0:T(8,128)(2,1)S(1)}, bf16[256,256]{1,0:T(8,128)(2,1)S(1)}, u32[]{:S(2)}, u32[]{:S(2)}) collective-permute-start(bf16[256,256]{1,0:T(8,128)(2,1)S(1)} %get-tuple-element.58), channel_id=1, source_target_pairs={{0,16},{4,20},{8,24},{12,28},{16,0},{20,4},{24,8},{28,12},{1,17},{... | collective-permute-start | bytes 393224 | tf_op jit(solution)/shard_map/ppermute | solution.py:422
  148.0 19.5 %collective-permute-start.25 = (bf16[128,1792]{1,0:T(8,128)(2,1)S(1)}, bf16[128,1792]{1,0:T(8,128)(2,1)S(1)}, u32[]{:S(2)}, u32[]{:S(2)}) collective-permute-start(bf16[128,1792]{1,0:T(8,128)(2,1)S(1)} %shard_map.85.refs_4_.refs_0_), channel_id=1, source_target_pairs={{0,64},{1,193},{2,66},{3,195},{32,96},{33,225},{34,98},{35,227},{6... | collective-permute-start | bytes 1376264 | tf_op jit(solution)/shard_map/ppermute | solution.py:40
  148.0 19.5 %collective-permute-start.26 = (bf16[128,1792]{1,0:T(8,128)(2,1)S(1)}, bf16[128,1792]{1,0:T(8,128)(2,1)S(1)}, u32[]{:S(2)}, u32[]{:S(2)}) collective-permute-start(bf16[128,1792]{1,0:T(8,128)(2,1)S(1)} %collective-permute-done.24.refs_1_), channel_id=1, source_target_pairs={{0,64},{1,193},{2,66},{3,195},{32,96},{33,225},{34,98},{35,227},{6... | collective-permute-start | bytes 1376264 | tf_op jit(solution)/shard_map/ppermute | solution.py:40
  150.6 5.3 %collective-permute-start.34 = (bf16[128,256]{1,0:T(8,128)(2,1)S(1)}, bf16[128,256]{1,0:T(8,128)(2,1)S(1)}, u32[]{:S(2)}, u32[]{:S(2)}) collective-permute-start(bf16[128,256]{1,0:T(8,128)(2,1)S(1)} %get-tuple-element.60), channel_id=1, source_target_pairs={{0,8},{4,12},{8,0},{12,4},{16,24},{20,28},{24,16},{28,20},{1,9},{5... | collective-permute-start | bytes 196616 | tf_op jit(solution)/shard_map/ppermute | solution.py:422
  155.9 11.5 %collective-permute-start.32 = (bf16[7,16,512]{2,1,0:T(8,128)(2,1)S(1)}, bf16[7,16,512]{2,1,0:T(8,128)(2,1)S(1)}, u32[]{:S(2)}, u32[]{:S(2)}) collective-permute-start(bf16[7,16,512]{2,1,0:T(8,128)(2,1)S(1)} %get-tuple-element.56), channel_id=1, source_target_pairs={{0,32},{1,33},{2,34},{3,35},{32,0},{33,1},{34,2},{35,3},{64,96},{6... | collective-permute-start | bytes 344072 | tf_op jit(solution)/shard_map/ppermute | solution.py:40
  160.7 4.6 %collective-permute-start.35 = (bf16[64,256]{1,0:T(8,128)(2,1)S(1)}, bf16[64,256]{1,0:T(8,128)(2,1)S(1)}, u32[]{:S(2)}, u32[]{:S(2)}) collective-permute-start(bf16[64,256]{1,0:T(8,128)(2,1)S(1)} %get-tuple-element.62), channel_id=1, source_target_pairs={{0,4},{4,0},{8,12},{12,8},{16,20},{20,16},{24,28},{28,24},{1,5},{5... | collective-permute-start | bytes 98312 | tf_op jit(solution)/shard_map/ppermute | solution.py:422
  167.4 2.4 %copy-start.4 = (f32[7,16,512]{2,1,0:T(8,128)}, f32[7,16,512]{2,1,0:T(8,128)S(1)}, u32[]{:S(2)}) copy-start(f32[7,16,512]{2,1,0:T(8,128)S(1)} %convert_add_fusion.refs_5_) | copy-start | bytes 688132

commit v3 on v2

--- a/solution.py
+++ b/solution.py
@@ -325,7 +325,14 @@
         (num,), scratch=[pltpu.VMEM((BLK, pair), BF16), pltpu.VMEM((BLK // 2, BLK), BF16)],
         after=[own_half],
     )
-    totals = [add(at, [mine[0], beside[0]], after=left_parts[:1])]
+    own, near, came_near, came_own = scatter_sends(*left)
+    def go_round(total):
+        near = send(total, Y_SECOND)
+        off = send(total, Y_FIRST)
+        return [total, near, off, send(near, Y_FIRST)]
+
+    totals = [add(at, [mine[0], beside[0]], after=[came_near])]
+    rounds = [go_round(totals[0])]
     def slab_kernel(at, own_ref, other_ref, result_ref, token_ref):
         token_ref[...] = jnp.zeros_like(token_ref)
         held = pl.program_id(0) == at[CORE_AT]
@@ -338,7 +345,6 @@
         (2,), after=totals,
     )
 
-    own, near, came_near, came_own = scatter_sends(*left)
 
     def place_kernel(at, *refs):
         refs[-1][...] = jnp.zeros_like(refs[-1])
@@ -348,11 +354,8 @@
             def _():
                 refs[-2][...] = refs[j][...]
 
-    def go_round(k, total, grad_hidden, after):
-        near = send(total, Y_SECOND)
-        off = send(total, Y_FIRST)
-        opposite = send(near, Y_FIRST)
-        given = [total, near, off, opposite]
+    def place(k, given, grad_hidden, after):
+        total = given[0]
         specs = [pl.BlockSpec(total.shape, lambda i, at: (0, 0))] * N_Y
         if k > 0:
             given, specs = given + [grad_hidden], specs + [ANY]
@@ -367,8 +370,9 @@
 
     blocks = (num * mine_rows, BLK)
     near = add(at, [near.reshape(blocks), came_near.reshape(blocks)], after=[slab_done, came_own, beside[1]])
-    totals.append(add(at, [mine[1], beside[1]], after=[near]))
-    grad_hidden, placed = go_round(0, totals[0], None, [totals[1]])
+    totals.append(add(at, [mine[1], beside[1]], after=[near, rounds[0][2]]))
+    rounds.append(go_round(totals[1]))
+    grad_hidden, placed = place(0, rounds[0], None, [totals[1]])
     upper = pair // 2
 
     def right_kernel(at, own_ref, other_ref, own_slab_ref, other_slab_ref, keep_ref, send_ref, total_ref):
@@ -443,8 +447,8 @@
             [shape((num, groups * 8, BLK), F32), shape((num, groups * 8, BLK))], [half_of] * 2, after=after,
         )
 
-    stays, goes = left_sum([own, came_own, send(near, Y_SECOND)], 4, X_LO_AT)
-    stays, goes = left_sum([stays, send(goes, X_LO)], 2, X_HI_AT)
+    stays, goes = left_sum([own, came_own, send(near, Y_SECOND)], 4, X_LO_AT, right_steps[:1])
+    stays, goes = left_sum([stays, send(goes, X_LO)], 2, X_HI_AT, [*right_steps[1:], rounds[1][2]])
     left_stats = stays + send(goes, X_HI).astype(F32)
 
     def last_kernel(at, mine_ref, came_ref, result_ref):
@@ -455,7 +459,7 @@
         last_kernel, at, [stay, came_z], [spec] * 2, [shape(stay.shape, F32)], [spec], after=[placed]
     )[0].T
 
-    grad_hidden, _ = go_round(1, totals[1], grad_hidden, [left_stats, right_stats])
+    grad_hidden, _ = place(1, rounds[1], grad_hidden, [left_stats, right_stats])
     return grad_hidden, grad_slab, left_stats, right_stats
 
 

time: 171 us -> 166 us (0.971)
  starting transfers between devices: 51.9 us -> 45.8 us
    ppermute x3, waiting for transfers between devices: 4.73 us -> 9.04 us  [body(): came_z = lax.ppermute(go, 'col', [(j, j ^ bit) for j in range(cols)])]
    ppermute x3, starting transfers between devices: 11.8 us -> 8.18 us  [body(): came_z = lax.ppermute(go, 'col', [(j, j ^ bit) for j in range(cols)])]
    ppermute x33, waiting for transfers between devices: 62.7 us -> 59.8 us  [send(): return lax.ppermute(x, ('row', 'rep'), perm)]
    ppermute x33, starting transfers between devices: 40.1 us -> 37.6 us  [send(): return lax.ppermute(x, ('row', 'rep'), perm)]
  transfers between devices with their start and end apart: 36 -> 36, of which waited for: 20 -> 22; matrix products, arithmetic and copies ran while one was open for 1% -> 1% of each run, Pallas kernels for 21% -> 22%
where the time goes in v3:
time: 166 us; the launch traced here: 165 us
  waiting for transfers between devices  68.9 us (42%)
  Pallas kernels  46.3 us (28%)
  starting transfers between devices  45.8 us (28%)
  local copies, waits for them, and re-layouts  3.17 us (2%)
    ppermute x33, waiting for transfers between devices, send(): return lax.ppermute(x, ('row', 'rep'), perm)  59.8 us
    pallas_call x28, Pallas kernels, call(): pl.pallas_call(run, grid_spec=pltpu.PrefetchScalarGridSpec(num_scalar_pre...  46.3 us
    ppermute x33, starting transfers between devices, send(): return lax.ppermute(x, ('row', 'rep'), perm)  37.6 us
    ppermute x3, waiting for transfers between devices, body(): came_z = lax.ppermute(go, 'col', [(j, j ^ bit) for j in range(cols)])  9.04 us
    ppermute x3, starting transfers between devices, body(): came_z = lax.ppermute(go, 'col', [(j, j ^ bit) for j in range(cols)])  8.18 us
  transfers between devices with their start and end apart: 36, of which 22 were waited for; matrix products, arithmetic and copies ran while one was open for 1% of the time, Pallas kernels for 22%

profile of v3, /device:TPU:32, one launch (start us, length us, event | category | flops | bytes accessed | tf_op | source)
XLA Modules:
  0.0 165.2 jit_solution(9447094740209467969)
XLA Ops:
  1.3 2.0 %copy-done = bf16[512,3584]{1,0:T(8,128)(2,1)S(1)} copy-done((bf16[512,3584]{1,0:T(8,128)(2,1)S(1)}, bf16[512,3584]{1,0:T(8,128)(2,1)}, u32[]{:S(2)}) %copy-start) | copy-done | bytes 3670040
  4.0 2.8 %collective-permute-start.5 = (bf16[512,1024]{1,0:T(8,128)(2,1)S(1)}, bf16[512,1024]{1,0:T(8,128)(2,1)S(1)}, u32[]{:S(2)}, u32[]{:S(2)}) collective-permute-start(bf16[512,1024]{1,0:T(8,128)(2,1)S(1)} %shard_map.66.refs_2_), channel_id=1, source_target_pairs={{0,34},{1,35},{2,32},{3,33},{32,2},{33,3},{34,0},{35,1},{64,98},{6... | collective-permute-start | bytes 3145736 | tf_op jit(solution)/shard_map/ppermute | solution.py:40
  9.3 6.4 %shard_map.69.refs_4_.refs_0_ = f32[1792,512]{1,0:T(8,128)S(1)} custom-call(s32[14]{0:T(128)S(1)} %stack.59.at_ref, bf16[512,3584]{1,0:T(8,128)(2,1)S(1)} %copy-done.1, bf16[512,3584]{1,0:T(8,128)(2,1)} %collective-permute-done.3.refs_1_, bf16[512,1024]{1,0:T(8,128)(2,1)S(1)} %copy-done.3, bf16[512,1024]{1,0:T(8,128)(2,1)S(1)} %collective-permute-done.4.refs_3_, ...), custom_call_target="tpu_custom_call" | custom-call | flops 1 | bytes 1 | tf_op jit(solution)/shard_map/pallas_call | solution.py:56
  15.7 3.1 %shard_map.70.refs_1_ = bf16[1024,512]{1,0:T(8,128)(2,1)S(1)} custom-call(s32[14]{0:T(128)S(1)} %stack.59.at_ref, bf16[512,3584]{1,0:T(8,128)(2,1)S(1)} %copy-done.1, bf16[512,3584]{1,0:T(8,128)(2,1)} %collective-permute-done.3.refs_1_, bf16[512,1024]{1,0:T(8,128)(2,1)S(1)} %copy-done.3, bf16[512,1024]{1,0:T(8,128)(2,1)S(1)} %collective-permute-done.4.refs_3_, ...), custom_call_target="tpu_custom_call" | custom-call | flops 1 | bytes 1 | tf_op jit(solution)/shard_map/pallas_call | solution.py:56
  18.9 10.3 %collective-permute-done.2.refs_0_.refs_3_ = bf16[1792,256]{1,0:T(8,128)(2,1)S(1)} collective-permute-done((bf16[1792,256]{1,0:T(8,128)(2,1)S(1)}, bf16[1792,256]{1,0:T(8,128)(2,1)S(1)}, u32[]{:S(2)}, u32[]{:S(2)}) %collective-permute-start.2) | collective-permute-done | bytes 917536 | tf_op jit(solution)/shard_map/ppermute | solution.py:40
  29.1 1.4 collective-permute-done.5.refs_2_.refs_1_
  31.3 2.4 %collective-permute-done.6.refs_4_ = bf16[1792,256]{1,0:T(8,128)(2,1)S(1)} collective-permute-done((bf16[1792,256]{1,0:T(8,128)(2,1)S(1)}, bf16[1792,256]{1,0:T(8,128)(2,1)S(1)}, u32[]{:S(2)}, u32[]{:S(2)}) %collective-permute-start.6) | collective-permute-done | bytes 917536 | tf_op jit(solution)/shard_map/ppermute | solution.py:40
  33.7 3.3 %shard_map.72 = (bf16[128,1792]{1,0:T(8,128)(2,1)S(1)}, bf16[128,1792]{1,0:T(8,128)(2,1)S(1)}, bf16[128,1792]{1,0:T(8,128)(2,1)S(1)}, bf16[128,1792]{1,0:T(8,128)(2,1)S(1)}) custom-call(s32[14]{0:T(128)S(1)} %stack.59.at_ref, bf16[512,1024]{1,0:T(8,128)(2,1)S(1)} %shard_map.68.refs_4_.refs_0_, bf16[3584,256]{1,0:T(8,128)(2,1)S(1)} %copy-done.2, ...), custom_call_target="tpu_custom_call" | custom-call | flops 1 | bytes 1 | tf_op jit(solution)/shard_map/pallas_call | solution.py:56
  37.0 1.7 %collective-permute-start.8 = (bf16[128,1792]{1,0:T(8,128)(2,1)S(1)}, bf16[128,1792]{1,0:T(8,128)(2,1)S(1)}, u32[]{:S(2)}, u32[]{:S(2)}) collective-permute-start(bf16[128,1792]{1,0:T(8,128)(2,1)S(1)} %get-tuple-element.39), channel_id=1, source_target_pairs={{0,64},{1,193},{2,66},{3,195},{32,96},{33,225},{34,98},{35,227},{6... | collective-permute-start | bytes 1376264 | tf_op jit(solution)/shard_map/ppermute | solution.py:40
  38.9 3.4 %collective-permute-start.10 = (bf16[512,768]{1,0:T(8,128)(2,1)S(1)}, bf16[512,768]{1,0:T(8,128)(2,1)S(1)}, u32[]{:S(2)}, u32[]{:S(2)}) collective-permute-start(bf16[512,768]{1,0:T(8,128)(2,1)S(1)} %get-tuple-element.40), channel_id=1, source_target_pairs={{0,35},{1,34},{2,33},{3,32},{32,3},{33,2},{34,1},{35,0},{64,99},{6... | collective-permute-start | bytes 2359304 | tf_op jit(solution)/shard_map/ppermute | solution.py:40
  42.4 3.1 %collective-permute-done.8.refs_1_ = bf16[128,1792]{1,0:T(8,128)(2,1)S(1)} collective-permute-done((bf16[128,1792]{1,0:T(8,128)(2,1)S(1)}, bf16[128,1792]{1,0:T(8,128)(2,1)S(1)}, u32[]{:S(2)}, u32[]{:S(2)}) %collective-permute-start.8) | collective-permute-done | bytes 458784 | tf_op jit(solution)/shard_map/ppermute | solution.py:40
  46.4 3.1 %collective-permute-start.9 = (bf16[128,1792]{1,0:T(8,128)(2,1)S(1)}, bf16[128,1792]{1,0:T(8,128)(2,1)S(1)}, u32[]{:S(2)}, u32[]{:S(2)}) collective-permute-start(bf16[128,1792]{1,0:T(8,128)(2,1)S(1)} %shard_map.73), channel_id=1, source_target_pairs={{0,192},{1,65},{2,194},{3,67},{32,224},{33,97},{34,226},{35,99},{6... | collective-permute-start | bytes 1376264 | tf_op jit(solution)/shard_map/ppermute | solution.py:40
  49.5 2.4 %collective-permute-done.7.refs_1_ = bf16[128,1792]{1,0:T(8,128)(2,1)S(1)} collective-permute-done((bf16[128,1792]{1,0:T(8,128)(2,1)S(1)}, bf16[128,1792]{1,0:T(8,128)(2,1)S(1)}, u32[]{:S(2)}, u32[]{:S(2)}) %collective-permute-start.7) | collective-permute-done | bytes 458784 | tf_op jit(solution)/shard_map/ppermute | solution.py:40
  51.9 4.3 %collective-permute-done.9.refs_2_ = bf16[128,1792]{1,0:T(8,128)(2,1)S(1)} collective-permute-done((bf16[128,1792]{1,0:T(8,128)(2,1)S(1)}, bf16[128,1792]{1,0:T(8,128)(2,1)S(1)}, u32[]{:S(2)}, u32[]{:S(2)}) %collective-permute-start.9) | collective-permute-done | bytes 458784 | tf_op jit(solution)/shard_map/ppermute | solution.py:40
  57.1 2.6 %collective-permute-done.10.refs_2_.refs_3_ = bf16[512,768]{1,0:T(8,128)(2,1)S(1)} collective-permute-done((bf16[512,768]{1,0:T(8,128)(2,1)S(1)}, bf16[512,768]{1,0:T(8,128)(2,1)S(1)}, u32[]{:S(2)}, u32[]{:S(2)}) %collective-permute-start.10) | collective-permute-done | bytes 786464 | tf_op jit(solution)/shard_map/ppermute | solution.py:40
  59.7 1.9 %collective-permute-done.1.refs_0_.refs_3_ = bf16[1792,256]{1,0:T(8,128)(2,1)S(1)} collective-permute-done((bf16[1792,256]{1,0:T(8,128)(2,1)S(1)}, bf16[1792,256]{1,0:T(8,128)(2,1)S(1)}, u32[]{:S(2)}, u32[]{:S(2)}) %collective-permute-start.1) | collective-permute-done | bytes 917536 | tf_op jit(solution)/shard_map/ppermute | solution.py:40
  62.7 2.0 %collective-permute-done.11.refs_4_ = bf16[1792,256]{1,0:T(8,128)(2,1)S(1)} collective-permute-done((bf16[1792,256]{1,0:T(8,128)(2,1)S(1)}, bf16[1792,256]{1,0:T(8,128)(2,1)S(1)}, u32[]{:S(2)}, u32[]{:S(2)}) %collective-permute-start.11) | collective-permute-done | bytes 917536 | tf_op jit(solution)/shard_map/ppermute | solution.py:40
  64.8 3.3 %shard_map.76 = (bf16[128,1792]{1,0:T(8,128)(2,1)S(1)}, bf16[128,1792]{1,0:T(8,128)(2,1)S(1)}, bf16[128,1792]{1,0:T(8,128)(2,1)S(1)}, bf16[128,1792]{1,0:T(8,128)(2,1)S(1)}) custom-call(s32[14]{0:T(128)S(1)} %stack.59.at_ref, bf16[512,1024]{1,0:T(8,128)(2,1)S(1)} %shard_map.68.refs_4_.refs_0_, bf16[3584,256]{1,0:T(8,128)(2,1)S(1)} %copy-done.2, ...), custom_call_target="tpu_custom_call" | custom-call | flops 1 | bytes 1 | tf_op jit(solution)/shard_map/pallas_call | solution.py:56
  68.9 2.5 %collective-permute-start.17 = (bf16[512,512]{1,0:T(8,128)(2,1)S(1)}, bf16[512,512]{1,0:T(8,128)(2,1)S(1)}, u32[]{:S(2)}, u32[]{:S(2)}) collective-permute-start(bf16[512,512]{1,0:T(8,128)(2,1)S(1)} %get-tuple-element.46), channel_id=1, source_target_pairs={{0,35},{1,34},{2,33},{3,32},{32,3},{33,2},{34,1},{35,0},{64,99},{6... | collective-permute-start | bytes 1572872 | tf_op jit(solution)/shard_map/ppermute | solution.py:40
  71.7 4.9 %collective-permute-done.13.refs_1_ = bf16[128,1792]{1,0:T(8,128)(2,1)S(1)} collective-permute-done((bf16[128,1792]{1,0:T(8,128)(2,1)S(1)}, bf16[128,1792]{1,0:T(8,128)(2,1)S(1)}, u32[]{:S(2)}, u32[]{:S(2)}) %collective-permute-start.13) | collective-permute-done | bytes 458784 | tf_op jit(solution)/shard_map/ppermute | solution.py:40
  78.6 2.8 %collective-permute-start.16 = (bf16[512,256]{1,0:T(8,128)(2,1)S(1)}, bf16[512,256]{1,0:T(8,128)(2,1)S(1)}, u32[]{:S(2)}, u32[]{:S(2)}) collective-permute-start(bf16[512,256]{1,0:T(8,128)(2,1)S(1)} %get-tuple-element.45), channel_id=1, source_target_pairs={{0,34},{1,35},{2,32},{3,33},{32,2},{33,3},{34,0},{35,1},{64,98},{6... | collective-permute-start | bytes 786440 | tf_op jit(solution)/shard_map/ppermute | solution.py:40
  82.3 4.9 %collective-permute-done.14.refs_2_ = bf16[128,1792]{1,0:T(8,128)(2,1)S(1)} collective-permute-done((bf16[128,1792]{1,0:T(8,128)(2,1)S(1)}, bf16[128,1792]{1,0:T(8,128)(2,1)S(1)}, u32[]{:S(2)}, u32[]{:S(2)}) %collective-permute-start.14) | collective-permute-done | bytes 458784 | tf_op jit(solution)/shard_map/ppermute | solution.py:40
  88.1 1.8 %collective-permute-done.16.refs_2_ = bf16[512,256]{1,0:T(8,128)(2,1)S(1)} collective-permute-done((bf16[512,256]{1,0:T(8,128)(2,1)S(1)}, bf16[512,256]{1,0:T(8,128)(2,1)S(1)}, u32[]{:S(2)}, u32[]{:S(2)}) %collective-permute-start.16) | collective-permute-done | bytes 262176 | tf_op jit(solution)/shard_map/ppermute | solution.py:40
  90.7 1.9 %collective-permute-done.19.refs_6_ = bf16[512,512]{1,0:T(8,128)(2,1)S(1)} collective-permute-done((bf16[512,512]{1,0:T(8,128)(2,1)S(1)}, bf16[512,512]{1,0:T(8,128)(2,1)S(1)}, u32[]{:S(2)}, u32[]{:S(2)}) %collective-permute-start.19) | collective-permute-done | bytes 524320 | tf_op jit(solution)/shard_map/ppermute | solution.py:40
  92.6 3.6 %shard_map.80.refs_0_.refs_1_.refs_4_.refs_2_ = bf16[1792,512]{1,0:T(8,128)(2,1)S(1)} custom-call(s32[14]{0:T(128)S(1)} %stack.59.at_ref, f32[1792,512]{1,0:T(8,128)S(1)} %shard_map.69.refs_4_.refs_0_, bf16[512,1024]{1,0:T(8,128)(2,1)S(1)} %collective-permute-done.5.refs_2_.refs_1_, bf16[512,256]{1,0:T(8,128)(2,1)S(1)} %collective-permute-done.16.refs_2_, ...), custom_call_target="tpu_custom_call" | custom-call | flops 1 | bytes 1 | tf_op jit(solution)/shard_map/pallas_call | solution.py:56
  97.1 2.9 %collective-permute-done.20.refs_2_.refs_3_.refs_1_ = bf16[1792,512]{1,0:T(8,128)(2,1)S(1)} collective-permute-done((bf16[1792,512]{1,0:T(8,128)(2,1)S(1)}, bf16[1792,512]{1,0:T(8,128)(2,1)S(1)}, u32[]{:S(2)}, u32[]{:S(2)}) %collective-permute-start.20) | collective-permute-done | bytes 1835040 | tf_op jit(solution)/shard_map/ppermute | solution.py:40
  100.1 3.4 %shard_map.81 = (bf16[7,64,512]{2,1,0:T(8,128)(2,1)S(1)}, bf16[7,64,512]{2,1,0:T(8,128)(2,1)S(1)}, bf16[7,64,512]{2,1,0:T(8,128)(2,1)S(1)}, bf16[7,64,512]{2,1,0:T(8,128)(2,1)S(1)}) custom-call(s32[14]{0:T(128)S(1)} %stack.59.at_ref, bf16[1792,512]{1,0:T(8,128)(2,1)S(1)} %shard_map.80.refs_0_.refs_1_.refs_4_.refs_2_, ...), custom_call_target="tpu_custom_call" | custom-call | flops 1 | bytes 1 | tf_op jit(solution)/shard_map/pallas_call | solution.py:56
  103.5 1.3 collective-permute-start.21
  105.1 1.2 collective-permute-start.23
  106.3 5.0 %collective-permute-done.22.refs_1_ = bf16[128,1792]{1,0:T(8,128)(2,1)S(1)} collective-permute-done((bf16[128,1792]{1,0:T(8,128)(2,1)S(1)}, bf16[128,1792]{1,0:T(8,128)(2,1)S(1)}, u32[]{:S(2)}, u32[]{:S(2)}) %collective-permute-start.22) | collective-permute-done | bytes 458784 | tf_op jit(solution)/shard_map/ppermute | solution.py:40
  112.9 1.3 collective-permute-start.24
  115.3 2.0 %shard_map.83 = (bf16[3584,256]{1,0:T(8,128)(2,1)}, f32[8,128]{1,0:T(8,128)S(1)}) custom-call(s32[14]{0:T(128)S(1)} %stack.59.at_ref, bf16[1792,512]{1,0:T(8,128)(2,1)S(1)} %shard_map.80.refs_0_.refs_1_.refs_4_.refs_2_, bf16[1792,512]{1,0:T(8,128)(2,1)S(1)} %collective-permute-done.20.refs_2_.refs_3_.refs_1_, bf16[128,1792]{1,0:T(8,128)(2,1)S(1)} %shard_map.82.refs_2_.refs_0_), custom_call_target="tpu_custom_call" | custom-call | flops 1 | bytes 1 | tf_op jit(solution)/shard_map/pallas_call | solution.py:56
  117.3 3.3 %collective-permute-done.15.refs_4_.refs_1_ = bf16[128,1792]{1,0:T(8,128)(2,1)S(1)} collective-permute-done((bf16[128,1792]{1,0:T(8,128)(2,1)S(1)}, bf16[128,1792]{1,0:T(8,128)(2,1)S(1)}, u32[]{:S(2)}, u32[]{:S(2)}) %collective-permute-start.15) | collective-permute-done | bytes 458784 | tf_op jit(solution)/shard_map/ppermute | solution.py:40
  121.4 1.8 %collective-permute-start.30 = (bf16[7,64,512]{2,1,0:T(8,128)(2,1)S(1)}, bf16[7,64,512]{2,1,0:T(8,128)(2,1)S(1)}, u32[]{:S(2)}, u32[]{:S(2)}) collective-permute-start(bf16[7,64,512]{2,1,0:T(8,128)(2,1)S(1)} %bitcast.19), channel_id=1, source_target_pairs={{0,192},{1,65},{2,194},{3,67},{32,224},{33,97},{34,226},{35,99},{6... | collective-permute-start | bytes 1376264 | tf_op jit(solution)/shard_map/ppermute | solution.py:40
  123.2 3.0 %collective-permute-done.24.refs_3_.refs_2_ = bf16[128,1792]{1,0:T(8,128)(2,1)S(1)} collective-permute-done((bf16[128,1792]{1,0:T(8,128)(2,1)S(1)}, bf16[128,1792]{1,0:T(8,128)(2,1)S(1)}, u32[]{:S(2)}, u32[]{:S(2)}) %collective-permute-start.24) | collective-permute-done | bytes 458784 | tf_op jit(solution)/shard_map/ppermute | solution.py:40
  127.0 2.1 %collective-permute-start.25 = (bf16[128,1792]{1,0:T(8,128)(2,1)S(1)}, bf16[128,1792]{1,0:T(8,128)(2,1)S(1)}, u32[]{:S(2)}, u32[]{:S(2)}) collective-permute-start(bf16[128,1792]{1,0:T(8,128)(2,1)S(1)} %shard_map.85.refs_4_.refs_0_), channel_id=1, source_target_pairs={{0,192},{1,65},{2,194},{3,67},{32,224},{33,97},{34,226},{35,99},{6... | collective-permute-start | bytes 1376264 | tf_op jit(solution)/shard_map/ppermute | solution.py:40
  129.4 2.4 %shard_map.87 = (f32[256,256]{1,0:T(8,128)S(1)}, bf16[256,256]{1,0:T(8,128)(2,1)S(1)}) custom-call(s32[14]{0:T(128)S(1)} %stack.59.at_ref, bf16[1792,512]{1,0:T(8,128)(2,1)S(1)} %shard_map.80.refs_0_.refs_1_.refs_4_.refs_2_, bf16[1792,512]{1,0:T(8,128)(2,1)S(1)} %collective-permute-done.20.refs_2_.refs_3_.refs_1_, ...), custom_call_target="tpu_custom_call" | custom-call | flops 1 | bytes 1 | tf_op jit(solution)/shard_map/pallas_call | solution.py:56
  131.8 6.4 %collective-permute-start.31 = (bf16[256,256]{1,0:T(8,128)(2,1)S(1)}, bf16[256,256]{1,0:T(8,128)(2,1)S(1)}, u32[]{:S(2)}, u32[]{:S(2)}) collective-permute-start(bf16[256,256]{1,0:T(8,128)(2,1)S(1)} %get-tuple-element.54), channel_id=1, source_target_pairs={{0,16},{4,20},{8,24},{12,28},{16,0},{20,4},{24,8},{28,12},{1,17},{... | collective-permute-start | bytes 393224 | tf_op jit(solution)/shard_map/ppermute | solution.py:426
  138.2 1.8 %collective-permute-start.29 = (bf16[128,1792]{1,0:T(8,128)(2,1)S(1)}, bf16[128,1792]{1,0:T(8,128)(2,1)S(1)}, u32[]{:S(2)}, u32[]{:S(2)}) collective-permute-start(bf16[128,1792]{1,0:T(8,128)(2,1)S(1)} %collective-permute-done.28.refs_1_), channel_id=1, source_target_pairs={{0,64},{1,193},{2,66},{3,195},{32,96},{33,225},{34,98},{35,227},{6... | collective-permute-start | bytes 1376264 | tf_op jit(solution)/shard_map/ppermute | solution.py:40
  139.9 4.1 %collective-permute-done.31.refs_1_ = bf16[256,256]{1,0:T(8,128)(2,1)S(1)} collective-permute-done((bf16[256,256]{1,0:T(8,128)(2,1)S(1)}, bf16[256,256]{1,0:T(8,128)(2,1)S(1)}, u32[]{:S(2)}, u32[]{:S(2)}) %collective-permute-start.31) | collective-permute-done | bytes 131104 | tf_op jit(solution)/shard_map/ppermute | solution.py:426
  145.5 1.2 collective-permute-start.27
  146.7 1.8 %collective-permute-start.33 = (bf16[128,256]{1,0:T(8,128)(2,1)S(1)}, bf16[128,256]{1,0:T(8,128)(2,1)S(1)}, u32[]{:S(2)}, u32[]{:S(2)}) collective-permute-start(bf16[128,256]{1,0:T(8,128)(2,1)S(1)} %get-tuple-element.58), channel_id=1, source_target_pairs={{0,8},{4,12},{8,0},{12,4},{16,24},{20,28},{24,16},{28,20},{1,9},{5... | collective-permute-start | bytes 196616 | tf_op jit(solution)/shard_map/ppermute | solution.py:426
  148.5 3.3 %collective-permute-done.33.refs_1_ = bf16[128,256]{1,0:T(8,128)(2,1)S(1)} collective-permute-done((bf16[128,256]{1,0:T(8,128)(2,1)S(1)}, bf16[128,256]{1,0:T(8,128)(2,1)S(1)}, u32[]{:S(2)}, u32[]{:S(2)}) %collective-permute-start.33) | collective-permute-done | bytes 65568 | tf_op jit(solution)/shard_map/ppermute | solution.py:426
  153.1 3.6 %collective-permute-start.34 = (bf16[7,16,512]{2,1,0:T(8,128)(2,1)S(1)}, bf16[7,16,512]{2,1,0:T(8,128)(2,1)S(1)}, u32[]{:S(2)}, u32[]{:S(2)}) collective-permute-start(bf16[7,16,512]{2,1,0:T(8,128)(2,1)S(1)} %get-tuple-element.61), channel_id=1, source_target_pairs={{0,32},{1,33},{2,34},{3,35},{32,0},{33,1},{34,2},{35,3},{64,96},{6... | collective-permute-start | bytes 344072 | tf_op jit(solution)/shard_map/ppermute | solution.py:40
  156.7 2.3 %shard_map.86 = (bf16[512,3584]{1,0:T(8,128)(2,1)}, f32[8,128]{1,0:T(8,128)S(1)}) custom-call(s32[14]{0:T(128)S(1)} %stack.59.at_ref, bf16[128,1792]{1,0:T(8,128)(2,1)S(1)} %shard_map.82.refs_2_.refs_0_, bf16[128,1792]{1,0:T(8,128)(2,1)S(1)} %collective-permute-done.28.refs_1_, bf16[128,1792]{1,0:T(8,128)(2,1)S(1)} %collective-permute-done.24.refs_3_.refs_2_, ...), custom_call_target="tpu_custom_call" | custom-call | flops 1 | bytes 1 | tf_op jit(solution)/shard_map/pallas_call | solution.py:56
  159.1 1.6 collective-permute-done.35.refs_1_
  160.6 1.2 shard_map.92
  162.8 2.4 %shard_map.93 = (bf16[512,3584]{1,0:T(8,128)(2,1)}, f32[8,128]{1,0:T(8,128)}) custom-call(s32[14]{0:T(128)S(1)} %stack.59.at_ref, bf16[128,1792]{1,0:T(8,128)(2,1)S(1)} %shard_map.85.refs_4_.refs_0_, bf16[128,1792]{1,0:T(8,128)(2,1)S(1)} %collective-permute-done.25.refs_1_, ...), custom_call_target="tpu_custom_call", output_to_operand_aliasing={{0}: (5, {})} | custom-call | flops 1 | bytes 1 | tf_op jit(solution)/shard_map/pallas_call | solution.py:56
  (66 shorter events, 22.9 us)
Async XLA Ops:
  0.6 8.6 %collective-permute-start.3 = (bf16[512,3584]{1,0:T(8,128)(2,1)}, bf16[512,3584]{1,0:T(8,128)(2,1)}, u32[]{:S(2)}, u32[]{:S(2)}) collective-permute-start(bf16[512,3584]{1,0:T(8,128)(2,1)} %refs_0_.9), channel_id=1, source_target_pairs={{0,1},{1,0},{2,3},{3,2},{32,33},{33,32},{34,35},{35,34},{64,65},{6... | collective-permute-start | bytes 11010056 | tf_op jit(solution)/shard_map/ppermute | solution.py:40
  0.7 8.5 %collective-permute-start.4 = (bf16[512,1024]{1,0:T(8,128)(2,1)}, bf16[512,1024]{1,0:T(8,128)(2,1)S(1)}, u32[]{:S(2)}, u32[]{:S(2)}) collective-permute-start(bf16[512,1024]{1,0:T(8,128)(2,1)} %refs_2_.3), channel_id=1, source_target_pairs={{0,1},{1,0},{2,3},{3,2},{32,33},{33,32},{34,35},{35,34},{64,65},{6... | collective-permute-start | bytes 3145736 | tf_op jit(solution)/shard_map/ppermute | solution.py:40
  1.3 2.0 %copy-start = (bf16[512,3584]{1,0:T(8,128)(2,1)S(1)}, bf16[512,3584]{1,0:T(8,128)(2,1)}, u32[]{:S(2)}) copy-start(bf16[512,3584]{1,0:T(8,128)(2,1)} %refs_0_.9) | copy-start | bytes 11010052
  3.4 3.5 %copy-start.2 = (bf16[3584,256]{1,0:T(8,128)(2,1)S(1)}, bf16[3584,256]{1,0:T(8,128)(2,1)}, u32[]{:S(2)}) copy-start(bf16[3584,256]{1,0:T(8,128)(2,1)} %refs_1_.5) | copy-start | bytes 5505028
  4.0 26.5 %collective-permute-start.5 = (bf16[512,1024]{1,0:T(8,128)(2,1)S(1)}, bf16[512,1024]{1,0:T(8,128)(2,1)S(1)}, u32[]{:S(2)}, u32[]{:S(2)}) collective-permute-start(bf16[512,1024]{1,0:T(8,128)(2,1)S(1)} %shard_map.66.refs_2_), channel_id=1, source_target_pairs={{0,34},{1,35},{2,32},{3,33},{32,2},{33,3},{34,0},{35,1},{64,98},{6... | collective-permute-start | bytes 3145736 | tf_op jit(solution)/shard_map/ppermute | solution.py:40
  6.9 1.4 copy-start.3
  7.0 2.4 %copy-start.1 = (bf16[512,3584]{1,0:T(8,128)(2,1)S(1)}, bf16[512,3584]{1,0:T(8,128)(2,1)}, u32[]{:S(2)}) copy-start(bf16[512,3584]{1,0:T(8,128)(2,1)} %refs_0_.9) | copy-start | bytes 11010052
  7.0 22.2 %collective-permute-start.2 = (bf16[1792,256]{1,0:T(8,128)(2,1)S(1)}, bf16[1792,256]{1,0:T(8,128)(2,1)S(1)}, u32[]{:S(2)}, u32[]{:S(2)}) collective-permute-start(bf16[1792,256]{1,0:T(8,128)(2,1)S(1)} %slice.3), channel_id=1, source_target_pairs={{0,2},{1,3},{2,0},{3,1},{32,34},{33,35},{34,32},{35,33},{64,66},{6... | collective-permute-start | bytes 2752520 | tf_op jit(solution)/shard_map/ppermute | solution.py:40
  7.3 24.0 %collective-permute-start = (bf16[3584,256]{1,0:T(8,128)(2,1)S(1)}, bf16[3584,256]{1,0:T(8,128)(2,1)S(1)}, u32[]{:S(2)}, u32[]{:S(2)}) collective-permute-start(bf16[3584,256]{1,0:T(8,128)(2,1)S(1)} %copy-done.2), channel_id=1, source_target_pairs={{0,1},{1,0},{2,3},{3,2},{32,33},{33,32},{34,35},{35,34},{64,65},{6... | collective-permute-start | bytes 5505032 | tf_op jit(solution)/shard_map/ppermute | solution.py:40
  31.1 2.6 %collective-permute-start.6 = (bf16[1792,256]{1,0:T(8,128)(2,1)S(1)}, bf16[1792,256]{1,0:T(8,128)(2,1)S(1)}, u32[]{:S(2)}, u32[]{:S(2)}) collective-permute-start(bf16[1792,256]{1,0:T(8,128)(2,1)S(1)} %shard_map.71.refs_5_), channel_id=1, source_target_pairs={{0,1},{1,0},{2,3},{3,2},{32,33},{33,32},{34,35},{35,34},{64,65},{6... | collective-permute-start | bytes 2752520 | tf_op jit(solution)/shard_map/ppermute | solution.py:40
  37.0 8.6 %collective-permute-start.8 = (bf16[128,1792]{1,0:T(8,128)(2,1)S(1)}, bf16[128,1792]{1,0:T(8,128)(2,1)S(1)}, u32[]{:S(2)}, u32[]{:S(2)}) collective-permute-start(bf16[128,1792]{1,0:T(8,128)(2,1)S(1)} %get-tuple-element.39), channel_id=1, source_target_pairs={{0,64},{1,193},{2,66},{3,195},{32,96},{33,225},{34,98},{35,227},{6... | collective-permute-start | bytes 1376264 | tf_op jit(solution)/shard_map/ppermute | solution.py:40
  38.6 22.9 %collective-permute-start.1 = (bf16[1792,256]{1,0:T(8,128)(2,1)S(1)}, bf16[1792,256]{1,0:T(8,128)(2,1)S(1)}, u32[]{:S(2)}, u32[]{:S(2)}) collective-permute-start(bf16[1792,256]{1,0:T(8,128)(2,1)S(1)} %get-tuple-element.35.refs_1_), channel_id=1, source_target_pairs={{0,2},{1,3},{2,0},{3,1},{32,34},{33,35},{34,32},{35,33},{64,66},{6... | collective-permute-start | bytes 2752520 | tf_op jit(solution)/shard_map/ppermute | solution.py:40
  38.9 20.7 %collective-permute-start.10 = (bf16[512,768]{1,0:T(8,128)(2,1)S(1)}, bf16[512,768]{1,0:T(8,128)(2,1)S(1)}, u32[]{:S(2)}, u32[]{:S(2)}) collective-permute-start(bf16[512,768]{1,0:T(8,128)(2,1)S(1)} %get-tuple-element.40), channel_id=1, source_target_pairs={{0,35},{1,34},{2,33},{3,32},{32,3},{33,2},{34,1},{35,0},{64,99},{6... | collective-permute-start | bytes 2359304 | tf_op jit(solution)/shard_map/ppermute | solution.py:40
  42.3 9.6 %collective-permute-start.7 = (bf16[128,1792]{1,0:T(8,128)(2,1)S(1)}, bf16[128,1792]{1,0:T(8,128)(2,1)S(1)}, u32[]{:S(2)}, u32[]{:S(2)}) collective-permute-start(bf16[128,1792]{1,0:T(8,128)(2,1)S(1)} %get-tuple-element.37), channel_id=1, source_target_pairs={{0,64},{1,193},{2,66},{3,195},{32,96},{33,225},{34,98},{35,227},{6... | collective-permute-start | bytes 1376264 | tf_op jit(solution)/shard_map/ppermute | solution.py:40
  46.4 9.8 %collective-permute-start.9 = (bf16[128,1792]{1,0:T(8,128)(2,1)S(1)}, bf16[128,1792]{1,0:T(8,128)(2,1)S(1)}, u32[]{:S(2)}, u32[]{:S(2)}) collective-permute-start(bf16[128,1792]{1,0:T(8,128)(2,1)S(1)} %shard_map.73), channel_id=1, source_target_pairs={{0,192},{1,65},{2,194},{3,67},{32,224},{33,97},{34,226},{35,99},{6... | collective-permute-start | bytes 1376264 | tf_op jit(solution)/shard_map/ppermute | solution.py:40
  62.2 2.6 %collective-permute-start.11 = (bf16[1792,256]{1,0:T(8,128)(2,1)S(1)}, bf16[1792,256]{1,0:T(8,128)(2,1)S(1)}, u32[]{:S(2)}, u32[]{:S(2)}) collective-permute-start(bf16[1792,256]{1,0:T(8,128)(2,1)S(1)} %shard_map.75.refs_5_), channel_id=1, source_target_pairs={{0,1},{1,0},{2,3},{3,2},{32,33},{33,32},{34,35},{35,34},{64,65},{6... | collective-permute-start | bytes 2752520 | tf_op jit(solution)/shard_map/ppermute | solution.py:40
  62.4 27.5 %collective-permute-start.18 = (bf16[1024,512]{1,0:T(8,128)(2,1)S(1)}, bf16[1024,512]{1,0:T(8,128)(2,1)S(1)}, u32[]{:S(2)}, u32[]{:S(2)}) collective-permute-start(bf16[1024,512]{1,0:T(8,128)(2,1)S(1)} %shard_map.70.refs_1_), channel_id=1, source_target_pairs={{0,2},{1,3},{2,0},{3,1},{32,34},{33,35},{34,32},{35,33},{64,66},{6... | collective-permute-start | bytes 3145736 | tf_op jit(solution)/shard_map/ppermute | solution.py:40
  68.0 8.6 %collective-permute-start.13 = (bf16[128,1792]{1,0:T(8,128)(2,1)S(1)}, bf16[128,1792]{1,0:T(8,128)(2,1)S(1)}, u32[]{:S(2)}, u32[]{:S(2)}) collective-permute-start(bf16[128,1792]{1,0:T(8,128)(2,1)S(1)} %get-tuple-element.44), channel_id=1, source_target_pairs={{0,64},{1,193},{2,66},{3,195},{32,96},{33,225},{34,98},{35,227},{6... | collective-permute-start | bytes 1376264 | tf_op jit(solution)/shard_map/ppermute | solution.py:40
  68.9 21.1 %collective-permute-start.17 = (bf16[512,512]{1,0:T(8,128)(2,1)S(1)}, bf16[512,512]{1,0:T(8,128)(2,1)S(1)}, u32[]{:S(2)}, u32[]{:S(2)}) collective-permute-start(bf16[512,512]{1,0:T(8,128)(2,1)S(1)} %get-tuple-element.46), channel_id=1, source_target_pairs={{0,35},{1,34},{2,33},{3,32},{32,3},{33,2},{34,1},{35,0},{64,99},{6... | collective-permute-start | bytes 1572872 | tf_op jit(solution)/shard_map/ppermute | solution.py:40
  71.4 11.0 %collective-permute-start.12 = (bf16[128,1792]{1,0:T(8,128)(2,1)S(1)}, bf16[128,1792]{1,0:T(8,128)(2,1)S(1)}, u32[]{:S(2)}, u32[]{:S(2)}) collective-permute-start(bf16[128,1792]{1,0:T(8,128)(2,1)S(1)} %get-tuple-element.42), channel_id=1, source_target_pairs={{0,64},{1,193},{2,66},{3,195},{32,96},{33,225},{34,98},{35,227},{6... | collective-permute-start | bytes 1376264 | tf_op jit(solution)/shard_map/ppermute | solution.py:40
  77.4 9.8 %collective-permute-start.14 = (bf16[128,1792]{1,0:T(8,128)(2,1)S(1)}, bf16[128,1792]{1,0:T(8,128)(2,1)S(1)}, u32[]{:S(2)}, u32[]{:S(2)}) collective-permute-start(bf16[128,1792]{1,0:T(8,128)(2,1)S(1)} %shard_map.77), channel_id=1, source_target_pairs={{0,192},{1,65},{2,194},{3,67},{32,224},{33,97},{34,226},{35,99},{6... | collective-permute-start | bytes 1376264 | tf_op jit(solution)/shard_map/ppermute | solution.py:40
  78.6 11.4 %collective-permute-start.16 = (bf16[512,256]{1,0:T(8,128)(2,1)S(1)}, bf16[512,256]{1,0:T(8,128)(2,1)S(1)}, u32[]{:S(2)}, u32[]{:S(2)}) collective-permute-start(bf16[512,256]{1,0:T(8,128)(2,1)S(1)} %get-tuple-element.45), channel_id=1, source_target_pairs={{0,34},{1,35},{2,32},{3,33},{32,2},{33,3},{34,0},{35,1},{64,98},{6... | collective-permute-start | bytes 786440 | tf_op jit(solution)/shard_map/ppermute | solution.py:40
  90.6 2.0 %collective-permute-start.19 = (bf16[512,512]{1,0:T(8,128)(2,1)S(1)}, bf16[512,512]{1,0:T(8,128)(2,1)S(1)}, u32[]{:S(2)}, u32[]{:S(2)}) collective-permute-start(bf16[512,512]{1,0:T(8,128)(2,1)S(1)} %shard_map.79), channel_id=1, source_target_pairs={{0,1},{1,0},{2,3},{3,2},{32,33},{33,32},{34,35},{35,34},{64,65},{6... | collective-permute-start | bytes 1572872 | tf_op jit(solution)/shard_map/ppermute | solution.py:40
  96.2 3.9 %collective-permute-start.20 = (bf16[1792,512]{1,0:T(8,128)(2,1)S(1)}, bf16[1792,512]{1,0:T(8,128)(2,1)S(1)}, u32[]{:S(2)}, u32[]{:S(2)}) collective-permute-start(bf16[1792,512]{1,0:T(8,128)(2,1)S(1)} %shard_map.80.refs_0_.refs_1_.refs_4_.refs_2_), channel_id=1, source_target_pairs={{0,1},{1,0},{2,3},{3,2},{32,33},{33,32},{34,35},{35,34},{64,65},{6... | collective-permute-start | bytes 5505032 | tf_op jit(solution)/shard_map/ppermute | solution.py:40
  96.4 14.9 %collective-permute-start.22 = (bf16[128,1792]{1,0:T(8,128)(2,1)S(1)}, bf16[128,1792]{1,0:T(8,128)(2,1)S(1)}, u32[]{:S(2)}, u32[]{:S(2)}) collective-permute-start(bf16[128,1792]{1,0:T(8,128)(2,1)S(1)} %shard_map.74.refs_1_.refs_8_.refs_0_), channel_id=1, source_target_pairs={{0,32},{1,33},{2,34},{3,35},{32,0},{33,1},{34,2},{35,3},{64,96},{6... | collective-permute-start | bytes 1376264 | tf_op jit(solution)/shard_map/ppermute | solution.py:40
  103.5 8.6 %collective-permute-start.21 = (bf16[7,64,512]{2,1,0:T(8,128)(2,1)S(1)}, bf16[7,64,512]{2,1,0:T(8,128)(2,1)S(1)}, u32[]{:S(2)}, u32[]{:S(2)}) collective-permute-start(bf16[7,64,512]{2,1,0:T(8,128)(2,1)S(1)} %get-tuple-element.48), channel_id=1, source_target_pairs={{0,64},{1,193},{2,66},{3,195},{32,96},{33,225},{34,98},{35,227},{6... | collective-permute-start | bytes 1376264 | tf_op jit(solution)/shard_map/ppermute | solution.py:40
  104.8 15.7 %collective-permute-start.15 = (bf16[128,1792]{1,0:T(8,128)(2,1)S(1)}, bf16[128,1792]{1,0:T(8,128)(2,1)S(1)}, u32[]{:S(2)}, u32[]{:S(2)}) collective-permute-start(bf16[128,1792]{1,0:T(8,128)(2,1)S(1)} %shard_map.78.refs_1_.refs_9_.refs_0_), channel_id=1, source_target_pairs={{0,32},{1,33},{2,34},{3,35},{32,0},{33,1},{34,2},{35,3},{64,96},{6... | collective-permute-start | bytes 1376264 | tf_op jit(solution)/shard_map/ppermute | solution.py:40
  105.1 15.4 %collective-permute-start.23 = (bf16[7,64,512]{2,1,0:T(8,128)(2,1)S(1)}, bf16[7,64,512]{2,1,0:T(8,128)(2,1)S(1)}, u32[]{:S(2)}, u32[]{:S(2)}) collective-permute-start(bf16[7,64,512]{2,1,0:T(8,128)(2,1)S(1)} %get-tuple-element.50), channel_id=1, source_target_pairs={{0,64},{1,193},{2,66},{3,195},{32,96},{33,225},{34,98},{35,227},{6... | collective-permute-start | bytes 1376264 | tf_op jit(solution)/shard_map/ppermute | solution.py:40
  112.9 13.3 %collective-permute-start.24 = (bf16[128,1792]{1,0:T(8,128)(2,1)S(1)}, bf16[128,1792]{1,0:T(8,128)(2,1)S(1)}, u32[]{:S(2)}, u32[]{:S(2)}) collective-permute-start(bf16[128,1792]{1,0:T(8,128)(2,1)S(1)} %shard_map.82.refs_2_.refs_0_), channel_id=1, source_target_pairs={{0,64},{1,193},{2,66},{3,195},{32,96},{33,225},{34,98},{35,227},{6... | collective-permute-start | bytes 1376264 | tf_op jit(solution)/shard_map/ppermute | solution.py:40
  114.2 23.9 %collective-permute-start.28 = (bf16[128,1792]{1,0:T(8,128)(2,1)S(1)}, bf16[128,1792]{1,0:T(8,128)(2,1)S(1)}, u32[]{:S(2)}, u32[]{:S(2)}) collective-permute-start(bf16[128,1792]{1,0:T(8,128)(2,1)S(1)} %shard_map.82.refs_2_.refs_0_), channel_id=1, source_target_pairs={{0,192},{1,65},{2,194},{3,67},{32,224},{33,97},{34,226},{35,99},{6... | collective-permute-start | bytes 1376264 | tf_op jit(solution)/shard_map/ppermute | solution.py:40
  121.4 23.3 %collective-permute-start.30 = (bf16[7,64,512]{2,1,0:T(8,128)(2,1)S(1)}, bf16[7,64,512]{2,1,0:T(8,128)(2,1)S(1)}, u32[]{:S(2)}, u32[]{:S(2)}) collective-permute-start(bf16[7,64,512]{2,1,0:T(8,128)(2,1)S(1)} %bitcast.19), channel_id=1, source_target_pairs={{0,192},{1,65},{2,194},{3,67},{32,224},{33,97},{34,226},{35,99},{6... | collective-permute-start | bytes 1376264 | tf_op jit(solution)/shard_map/ppermute | solution.py:40
  127.0 18.5 %collective-permute-start.25 = (bf16[128,1792]{1,0:T(8,128)(2,1)S(1)}, bf16[128,1792]{1,0:T(8,128)(2,1)S(1)}, u32[]{:S(2)}, u32[]{:S(2)}) collective-permute-start(bf16[128,1792]{1,0:T(8,128)(2,1)S(1)} %shard_map.85.refs_4_.refs_0_), channel_id=1, source_target_pairs={{0,192},{1,65},{2,194},{3,67},{32,224},{33,97},{34,226},{35,99},{6... | collective-permute-start | bytes 1376264 | tf_op jit(solution)/shard_map/ppermute | solution.py:40
  129.1 23.3 %collective-permute-start.26 = (bf16[128,1792]{1,0:T(8,128)(2,1)S(1)}, bf16[128,1792]{1,0:T(8,128)(2,1)S(1)}, u32[]{:S(2)}, u32[]{:S(2)}) collective-permute-start(bf16[128,1792]{1,0:T(8,128)(2,1)S(1)} %shard_map.85.refs_4_.refs_0_), channel_id=1, source_target_pairs={{0,64},{1,193},{2,66},{3,195},{32,96},{33,225},{34,98},{35,227},{6... | collective-permute-start | bytes 1376264 | tf_op jit(solution)/shard_map/ppermute | solution.py:40
  131.8 12.3 %collective-permute-start.31 = (bf16[256,256]{1,0:T(8,128)(2,1)S(1)}, bf16[256,256]{1,0:T(8,128)(2,1)S(1)}, u32[]{:S(2)}, u32[]{:S(2)}) collective-permute-start(bf16[256,256]{1,0:T(8,128)(2,1)S(1)} %get-tuple-element.54), channel_id=1, source_target_pairs={{0,16},{4,20},{8,24},{12,28},{16,0},{20,4},{24,8},{28,12},{1,17},{... | collective-permute-start | bytes 393224 | tf_op jit(solution)/shard_map/ppermute | solution.py:426
  138.2 18.6 %collective-permute-start.29 = (bf16[128,1792]{1,0:T(8,128)(2,1)S(1)}, bf16[128,1792]{1,0:T(8,128)(2,1)S(1)}, u32[]{:S(2)}, u32[]{:S(2)}) collective-permute-start(bf16[128,1792]{1,0:T(8,128)(2,1)S(1)} %collective-permute-done.28.refs_1_), channel_id=1, source_target_pairs={{0,64},{1,193},{2,66},{3,195},{32,96},{33,225},{34,98},{35,227},{6... | collective-permute-start | bytes 1376264 | tf_op jit(solution)/shard_map/ppermute | solution.py:40
  145.4 7.1 %collective-permute-start.32 = (bf16[7,32,512]{2,1,0:T(8,128)(2,1)S(1)}, bf16[7,32,512]{2,1,0:T(8,128)(2,1)S(1)}, u32[]{:S(2)}, u32[]{:S(2)}) collective-permute-start(bf16[7,32,512]{2,1,0:T(8,128)(2,1)S(1)} %get-tuple-element.57), channel_id=1, source_target_pairs={{0,2},{1,3},{2,0},{3,1},{32,34},{33,35},{34,32},{35,33},{64,66},{6... | collective-permute-start | bytes 688136 | tf_op jit(solution)/shard_map/ppermute | solution.py:40
  145.5 17.3 %collective-permute-start.27 = (bf16[128,1792]{1,0:T(8,128)(2,1)S(1)}, bf16[128,1792]{1,0:T(8,128)(2,1)S(1)}, u32[]{:S(2)}, u32[]{:S(2)}) collective-permute-start(bf16[128,1792]{1,0:T(8,128)(2,1)S(1)} %collective-permute-done.25.refs_1_), channel_id=1, source_target_pairs={{0,64},{1,193},{2,66},{3,195},{32,96},{33,225},{34,98},{35,227},{6... | collective-permute-start | bytes 1376264 | tf_op jit(solution)/shard_map/ppermute | solution.py:40
  146.7 5.2 %collective-permute-start.33 = (bf16[128,256]{1,0:T(8,128)(2,1)S(1)}, bf16[128,256]{1,0:T(8,128)(2,1)S(1)}, u32[]{:S(2)}, u32[]{:S(2)}) collective-permute-start(bf16[128,256]{1,0:T(8,128)(2,1)S(1)} %get-tuple-element.58), channel_id=1, source_target_pairs={{0,8},{4,12},{8,0},{12,4},{16,24},{20,28},{24,16},{28,20},{1,9},{5... | collective-permute-start | bytes 196616 | tf_op jit(solution)/shard_map/ppermute | solution.py:426
  153.1 9.7 %collective-permute-start.34 = (bf16[7,16,512]{2,1,0:T(8,128)(2,1)S(1)}, bf16[7,16,512]{2,1,0:T(8,128)(2,1)S(1)}, u32[]{:S(2)}, u32[]{:S(2)}) collective-permute-start(bf16[7,16,512]{2,1,0:T(8,128)(2,1)S(1)} %get-tuple-element.61), channel_id=1, source_target_pairs={{0,32},{1,33},{2,34},{3,35},{32,0},{33,1},{34,2},{35,3},{64,96},{6... | collective-permute-start | bytes 344072 | tf_op jit(solution)/shard_map/ppermute | solution.py:40
  156.7 3.9 %collective-permute-start.35 = (bf16[64,256]{1,0:T(8,128)(2,1)S(1)}, bf16[64,256]{1,0:T(8,128)(2,1)S(1)}, u32[]{:S(2)}, u32[]{:S(2)}) collective-permute-start(bf16[64,256]{1,0:T(8,128)(2,1)S(1)} %get-tuple-element.62), channel_id=1, source_target_pairs={{0,4},{4,0},{8,12},{12,8},{16,20},{20,16},{24,28},{28,24},{1,5},{5... | collective-permute-start | bytes 98312 | tf_op jit(solution)/shard_map/ppermute | solution.py:426
  162.8 2.4 %copy-start.4 = (f32[7,16,512]{2,1,0:T(8,128)}, f32[7,16,512]{2,1,0:T(8,128)S(1)}, u32[]{:S(2)}) copy-start(f32[7,16,512]{2,1,0:T(8,128)S(1)} %convert_add_fusion.refs_5_) | copy-start | bytes 688132

commit v4 on v3

--- a/solution.py
+++ b/solution.py
@@ -368,11 +368,6 @@
             (N_Y,), aliases={N_Y + 1: 0} if k > 0 else None, after=after,
         )
 
-    blocks = (num * mine_rows, BLK)
-    near = add(at, [near.reshape(blocks), came_near.reshape(blocks)], after=[slab_done, came_own, beside[1]])
-    totals.append(add(at, [mine[1], beside[1]], after=[near, rounds[0][2]]))
-    rounds.append(go_round(totals[1]))
-    grad_hidden, placed = place(0, rounds[0], None, [totals[1]])
     upper = pair // 2
 
     def right_kernel(at, own_ref, other_ref, own_slab_ref, other_slab_ref, keep_ref, send_ref, total_ref):
@@ -403,9 +398,14 @@
         right_kernel, at, [own_half, other_half, own_half, other_half],
         [rows_spec, rows_spec, slab_spec, slab_spec],
         [shape((upper, slab), F32), shape((upper, slab))], [upper_spec] * 2, (steps,),
-        scratch=[pltpu.VMEM((pair, slab), F32)], after=totals[1:],
-    )
-
+        scratch=[pltpu.VMEM((pair, slab), F32)], after=[slab_done],
+    )
+
+    blocks = (num * mine_rows, BLK)
+    near = add(at, [near.reshape(blocks), came_near.reshape(blocks)], after=[stay, came_own, beside[1]])
+    totals.append(add(at, [mine[1], beside[1]], after=[near, rounds[0][2]]))
+    rounds.append(go_round(totals[1]))
+    grad_hidden, placed = place(0, rounds[0], None, [totals[1]])
     def right_sum(stay, came, bit):
         rows = stay.shape[0] // 2
 

time: 166 us -> 163 us (0.982)
  waiting for transfers between devices: 68.9 us -> 66.3 us
    ppermute x33, waiting for transfers between devices: 59.8 us -> 57.8 us  [send(): return lax.ppermute(x, ('row', 'rep'), perm)]
  transfers between devices with their start and end apart: 36 -> 36, of which waited for: 22 -> 23; matrix products, arithmetic and copies ran while one was open for 1% -> 1% of each run, Pallas kernels for 22% -> 22%
where the time goes in v4:
time: 163 us
  waiting for transfers between devices  66.3 us (41%)
  Pallas kernels  46.3 us (28%)
  starting transfers between devices  46 us (28%)
  local copies, waits for them, and re-layouts  3.17 us (2%)
    ppermute x33, waiting for transfers between devices, send(): return lax.ppermute(x, ('row', 'rep'), perm)  57.8 us
    pallas_call x28, Pallas kernels, call(): pl.pallas_call(run, grid_spec=pltpu.PrefetchScalarGridSpec(num_scalar_pre...  46.3 us
    ppermute x33, starting transfers between devices, send(): return lax.ppermute(x, ('row', 'rep'), perm)  37.3 us
    ppermute x3, starting transfers between devices, body(): came_z = lax.ppermute(go, 'col', [(j, j ^ bit) for j in range(cols)])  8.69 us
    ppermute x3, waiting for transfers between devices, body(): came_z = lax.ppermute(go, 'col', [(j, j ^ bit) for j in range(cols)])  8.45 us
  transfers between devices with their start and end apart: 36, of which 23 were waited for; matrix products, arithmetic and copies ran while one was open for 1% of the time, Pallas kernels for 22%

profile of v4, /device:TPU:32, one launch (start us, length us, event | category | flops | bytes accessed | tf_op | source)
XLA Modules:
  0.0 162.7 jit_solution(5430398745253952617)
XLA Ops:
  1.3 2.0 %copy-done = bf16[512,3584]{1,0:T(8,128)(2,1)S(1)} copy-done((bf16[512,3584]{1,0:T(8,128)(2,1)S(1)}, bf16[512,3584]{1,0:T(8,128)(2,1)}, u32[]{:S(2)}) %copy-start) | copy-done | bytes 3670040
  4.0 2.8 %collective-permute-start.5 = (bf16[512,1024]{1,0:T(8,128)(2,1)S(1)}, bf16[512,1024]{1,0:T(8,128)(2,1)S(1)}, u32[]{:S(2)}, u32[]{:S(2)}) collective-permute-start(bf16[512,1024]{1,0:T(8,128)(2,1)S(1)} %shard_map.66.refs_2_), channel_id=1, source_target_pairs={{0,34},{1,35},{2,32},{3,33},{32,2},{33,3},{34,0},{35,1},{64,98},{6... | collective-permute-start | bytes 3145736 | tf_op jit(solution)/shard_map/ppermute | solution.py:40
  7.3 1.0 shard_map.67
  9.3 6.4 %shard_map.69.refs_4_.refs_0_ = f32[1792,512]{1,0:T(8,128)S(1)} custom-call(s32[14]{0:T(128)S(1)} %stack.59.at_ref, bf16[512,3584]{1,0:T(8,128)(2,1)S(1)} %copy-done.1, bf16[512,3584]{1,0:T(8,128)(2,1)} %collective-permute-done.3.refs_1_, bf16[512,1024]{1,0:T(8,128)(2,1)S(1)} %copy-done.3, bf16[512,1024]{1,0:T(8,128)(2,1)S(1)} %collective-permute-done.4.refs_3_, ...), custom_call_target="tpu_custom_call" | custom-call | flops 1 | bytes 1 | tf_op jit(solution)/shard_map/pallas_call | solution.py:56
  15.7 3.1 %shard_map.70.refs_1_ = bf16[1024,512]{1,0:T(8,128)(2,1)S(1)} custom-call(s32[14]{0:T(128)S(1)} %stack.59.at_ref, bf16[512,3584]{1,0:T(8,128)(2,1)S(1)} %copy-done.1, bf16[512,3584]{1,0:T(8,128)(2,1)} %collective-permute-done.3.refs_1_, bf16[512,1024]{1,0:T(8,128)(2,1)S(1)} %copy-done.3, bf16[512,1024]{1,0:T(8,128)(2,1)S(1)} %collective-permute-done.4.refs_3_, ...), custom_call_target="tpu_custom_call" | custom-call | flops 1 | bytes 1 | tf_op jit(solution)/shard_map/pallas_call | solution.py:56
  18.9 10.3 %collective-permute-done.2.refs_0_.refs_3_ = bf16[1792,256]{1,0:T(8,128)(2,1)S(1)} collective-permute-done((bf16[1792,256]{1,0:T(8,128)(2,1)S(1)}, bf16[1792,256]{1,0:T(8,128)(2,1)S(1)}, u32[]{:S(2)}, u32[]{:S(2)}) %collective-permute-start.2) | collective-permute-done | bytes 917536 | tf_op jit(solution)/shard_map/ppermute | solution.py:40
  29.1 1.4 collective-permute-done.5.refs_2_.refs_1_
  31.3 2.4 %collective-permute-done.6.refs_4_ = bf16[1792,256]{1,0:T(8,128)(2,1)S(1)} collective-permute-done((bf16[1792,256]{1,0:T(8,128)(2,1)S(1)}, bf16[1792,256]{1,0:T(8,128)(2,1)S(1)}, u32[]{:S(2)}, u32[]{:S(2)}) %collective-permute-start.6) | collective-permute-done | bytes 917536 | tf_op jit(solution)/shard_map/ppermute | solution.py:40
  33.7 3.3 %shard_map.72 = (bf16[128,1792]{1,0:T(8,128)(2,1)S(1)}, bf16[128,1792]{1,0:T(8,128)(2,1)S(1)}, bf16[128,1792]{1,0:T(8,128)(2,1)S(1)}, bf16[128,1792]{1,0:T(8,128)(2,1)S(1)}) custom-call(s32[14]{0:T(128)S(1)} %stack.59.at_ref, bf16[512,1024]{1,0:T(8,128)(2,1)S(1)} %shard_map.68.refs_4_.refs_0_, bf16[3584,256]{1,0:T(8,128)(2,1)S(1)} %copy-done.2, ...), custom_call_target="tpu_custom_call" | custom-call | flops 1 | bytes 1 | tf_op jit(solution)/shard_map/pallas_call | solution.py:56
  37.0 1.7 %collective-permute-start.8 = (bf16[128,1792]{1,0:T(8,128)(2,1)S(1)}, bf16[128,1792]{1,0:T(8,128)(2,1)S(1)}, u32[]{:S(2)}, u32[]{:S(2)}) collective-permute-start(bf16[128,1792]{1,0:T(8,128)(2,1)S(1)} %get-tuple-element.39), channel_id=1, source_target_pairs={{0,64},{1,193},{2,66},{3,195},{32,96},{33,225},{34,98},{35,227},{6... | collective-permute-start | bytes 1376264 | tf_op jit(solution)/shard_map/ppermute | solution.py:40
  38.9 3.4 %collective-permute-start.10 = (bf16[512,768]{1,0:T(8,128)(2,1)S(1)}, bf16[512,768]{1,0:T(8,128)(2,1)S(1)}, u32[]{:S(2)}, u32[]{:S(2)}) collective-permute-start(bf16[512,768]{1,0:T(8,128)(2,1)S(1)} %get-tuple-element.40), channel_id=1, source_target_pairs={{0,35},{1,34},{2,33},{3,32},{32,3},{33,2},{34,1},{35,0},{64,99},{6... | collective-permute-start | bytes 2359304 | tf_op jit(solution)/shard_map/ppermute | solution.py:40
  42.4 3.1 %collective-permute-done.8.refs_1_ = bf16[128,1792]{1,0:T(8,128)(2,1)S(1)} collective-permute-done((bf16[128,1792]{1,0:T(8,128)(2,1)S(1)}, bf16[128,1792]{1,0:T(8,128)(2,1)S(1)}, u32[]{:S(2)}, u32[]{:S(2)}) %collective-permute-start.8) | collective-permute-done | bytes 458784 | tf_op jit(solution)/shard_map/ppermute | solution.py:40
  46.4 3.1 %collective-permute-start.9 = (bf16[128,1792]{1,0:T(8,128)(2,1)S(1)}, bf16[128,1792]{1,0:T(8,128)(2,1)S(1)}, u32[]{:S(2)}, u32[]{:S(2)}) collective-permute-start(bf16[128,1792]{1,0:T(8,128)(2,1)S(1)} %shard_map.73), channel_id=1, source_target_pairs={{0,192},{1,65},{2,194},{3,67},{32,224},{33,97},{34,226},{35,99},{6... | collective-permute-start | bytes 1376264 | tf_op jit(solution)/shard_map/ppermute | solution.py:40
  49.5 2.4 %collective-permute-done.7.refs_1_ = bf16[128,1792]{1,0:T(8,128)(2,1)S(1)} collective-permute-done((bf16[128,1792]{1,0:T(8,128)(2,1)S(1)}, bf16[128,1792]{1,0:T(8,128)(2,1)S(1)}, u32[]{:S(2)}, u32[]{:S(2)}) %collective-permute-start.7) | collective-permute-done | bytes 458784 | tf_op jit(solution)/shard_map/ppermute | solution.py:40
  51.9 4.3 %collective-permute-done.9.refs_2_ = bf16[128,1792]{1,0:T(8,128)(2,1)S(1)} collective-permute-done((bf16[128,1792]{1,0:T(8,128)(2,1)S(1)}, bf16[128,1792]{1,0:T(8,128)(2,1)S(1)}, u32[]{:S(2)}, u32[]{:S(2)}) %collective-permute-start.9) | collective-permute-done | bytes 458784 | tf_op jit(solution)/shard_map/ppermute | solution.py:40
  57.1 2.6 %collective-permute-done.10.refs_2_.refs_3_ = bf16[512,768]{1,0:T(8,128)(2,1)S(1)} collective-permute-done((bf16[512,768]{1,0:T(8,128)(2,1)S(1)}, bf16[512,768]{1,0:T(8,128)(2,1)S(1)}, u32[]{:S(2)}, u32[]{:S(2)}) %collective-permute-start.10) | collective-permute-done | bytes 786464 | tf_op jit(solution)/shard_map/ppermute | solution.py:40
  59.7 1.9 %collective-permute-done.1.refs_0_.refs_3_ = bf16[1792,256]{1,0:T(8,128)(2,1)S(1)} collective-permute-done((bf16[1792,256]{1,0:T(8,128)(2,1)S(1)}, bf16[1792,256]{1,0:T(8,128)(2,1)S(1)}, u32[]{:S(2)}, u32[]{:S(2)}) %collective-permute-start.1) | collective-permute-done | bytes 917536 | tf_op jit(solution)/shard_map/ppermute | solution.py:40
  62.7 2.0 %collective-permute-done.11.refs_4_ = bf16[1792,256]{1,0:T(8,128)(2,1)S(1)} collective-permute-done((bf16[1792,256]{1,0:T(8,128)(2,1)S(1)}, bf16[1792,256]{1,0:T(8,128)(2,1)S(1)}, u32[]{:S(2)}, u32[]{:S(2)}) %collective-permute-start.11) | collective-permute-done | bytes 917536 | tf_op jit(solution)/shard_map/ppermute | solution.py:40
  64.8 3.3 %shard_map.76 = (bf16[128,1792]{1,0:T(8,128)(2,1)S(1)}, bf16[128,1792]{1,0:T(8,128)(2,1)S(1)}, bf16[128,1792]{1,0:T(8,128)(2,1)S(1)}, bf16[128,1792]{1,0:T(8,128)(2,1)S(1)}) custom-call(s32[14]{0:T(128)S(1)} %stack.59.at_ref, bf16[512,1024]{1,0:T(8,128)(2,1)S(1)} %shard_map.68.refs_4_.refs_0_, bf16[3584,256]{1,0:T(8,128)(2,1)S(1)} %copy-done.2, ...), custom_call_target="tpu_custom_call" | custom-call | flops 1 | bytes 1 | tf_op jit(solution)/shard_map/pallas_call | solution.py:56
  68.9 2.5 %collective-permute-start.17 = (bf16[512,512]{1,0:T(8,128)(2,1)S(1)}, bf16[512,512]{1,0:T(8,128)(2,1)S(1)}, u32[]{:S(2)}, u32[]{:S(2)}) collective-permute-start(bf16[512,512]{1,0:T(8,128)(2,1)S(1)} %get-tuple-element.46), channel_id=1, source_target_pairs={{0,35},{1,34},{2,33},{3,32},{32,3},{33,2},{34,1},{35,0},{64,99},{6... | collective-permute-start | bytes 1572872 | tf_op jit(solution)/shard_map/ppermute | solution.py:40
  71.7 4.9 %collective-permute-done.13.refs_1_ = bf16[128,1792]{1,0:T(8,128)(2,1)S(1)} collective-permute-done((bf16[128,1792]{1,0:T(8,128)(2,1)S(1)}, bf16[128,1792]{1,0:T(8,128)(2,1)S(1)}, u32[]{:S(2)}, u32[]{:S(2)}) %collective-permute-start.13) | collective-permute-done | bytes 458784 | tf_op jit(solution)/shard_map/ppermute | solution.py:40
  77.4 1.1 collective-permute-start.14
  78.6 2.8 %collective-permute-start.16 = (bf16[512,256]{1,0:T(8,128)(2,1)S(1)}, bf16[512,256]{1,0:T(8,128)(2,1)S(1)}, u32[]{:S(2)}, u32[]{:S(2)}) collective-permute-start(bf16[512,256]{1,0:T(8,128)(2,1)S(1)} %get-tuple-element.45), channel_id=1, source_target_pairs={{0,34},{1,35},{2,32},{3,33},{32,2},{33,3},{34,0},{35,1},{64,98},{6... | collective-permute-start | bytes 786440 | tf_op jit(solution)/shard_map/ppermute | solution.py:40
  82.3 4.9 %collective-permute-done.14.refs_2_ = bf16[128,1792]{1,0:T(8,128)(2,1)S(1)} collective-permute-done((bf16[128,1792]{1,0:T(8,128)(2,1)S(1)}, bf16[128,1792]{1,0:T(8,128)(2,1)S(1)}, u32[]{:S(2)}, u32[]{:S(2)}) %collective-permute-start.14) | collective-permute-done | bytes 458784 | tf_op jit(solution)/shard_map/ppermute | solution.py:40
  88.1 1.8 %collective-permute-done.16.refs_2_ = bf16[512,256]{1,0:T(8,128)(2,1)S(1)} collective-permute-done((bf16[512,256]{1,0:T(8,128)(2,1)S(1)}, bf16[512,256]{1,0:T(8,128)(2,1)S(1)}, u32[]{:S(2)}, u32[]{:S(2)}) %collective-permute-start.16) | collective-permute-done | bytes 262176 | tf_op jit(solution)/shard_map/ppermute | solution.py:40
  90.7 1.9 %collective-permute-done.19.refs_6_ = bf16[512,512]{1,0:T(8,128)(2,1)S(1)} collective-permute-done((bf16[512,512]{1,0:T(8,128)(2,1)S(1)}, bf16[512,512]{1,0:T(8,128)(2,1)S(1)}, u32[]{:S(2)}, u32[]{:S(2)}) %collective-permute-start.19) | collective-permute-done | bytes 524320 | tf_op jit(solution)/shard_map/ppermute | solution.py:40
  92.6 3.6 %shard_map.80.refs_0_.refs_1_.refs_4_.refs_2_ = bf16[1792,512]{1,0:T(8,128)(2,1)S(1)} custom-call(s32[14]{0:T(128)S(1)} %stack.59.at_ref, f32[1792,512]{1,0:T(8,128)S(1)} %shard_map.69.refs_4_.refs_0_, bf16[512,1024]{1,0:T(8,128)(2,1)S(1)} %collective-permute-done.5.refs_2_.refs_1_, bf16[512,256]{1,0:T(8,128)(2,1)S(1)} %collective-permute-done.16.refs_2_, ...), custom_call_target="tpu_custom_call" | custom-call | flops 1 | bytes 1 | tf_op jit(solution)/shard_map/pallas_call | solution.py:56
  97.1 2.9 %collective-permute-done.20.refs_2_.refs_3_.refs_1_ = bf16[1792,512]{1,0:T(8,128)(2,1)S(1)} collective-permute-done((bf16[1792,512]{1,0:T(8,128)(2,1)S(1)}, bf16[1792,512]{1,0:T(8,128)(2,1)S(1)}, u32[]{:S(2)}, u32[]{:S(2)}) %collective-permute-start.20) | collective-permute-done | bytes 1835040 | tf_op jit(solution)/shard_map/ppermute | solution.py:40
  100.1 3.4 %shard_map.81 = (bf16[7,64,512]{2,1,0:T(8,128)(2,1)S(1)}, bf16[7,64,512]{2,1,0:T(8,128)(2,1)S(1)}, bf16[7,64,512]{2,1,0:T(8,128)(2,1)S(1)}, bf16[7,64,512]{2,1,0:T(8,128)(2,1)S(1)}) custom-call(s32[14]{0:T(128)S(1)} %stack.59.at_ref, bf16[1792,512]{1,0:T(8,128)(2,1)S(1)} %shard_map.80.refs_0_.refs_1_.refs_4_.refs_2_, ...), custom_call_target="tpu_custom_call" | custom-call | flops 1 | bytes 1 | tf_op jit(solution)/shard_map/pallas_call | solution.py:56
  103.5 1.3 collective-permute-start.21
  105.1 1.2 collective-permute-start.23
  106.3 5.0 %collective-permute-done.22.refs_1_ = bf16[128,1792]{1,0:T(8,128)(2,1)S(1)} collective-permute-done((bf16[128,1792]{1,0:T(8,128)(2,1)S(1)}, bf16[128,1792]{1,0:T(8,128)(2,1)S(1)}, u32[]{:S(2)}, u32[]{:S(2)}) %collective-permute-start.22) | collective-permute-done | bytes 458784 | tf_op jit(solution)/shard_map/ppermute | solution.py:40
  112.9 1.3 collective-permute-start.24
  115.3 2.0 %shard_map.83 = (bf16[3584,256]{1,0:T(8,128)(2,1)}, f32[8,128]{1,0:T(8,128)S(1)}) custom-call(s32[14]{0:T(128)S(1)} %stack.59.at_ref, bf16[1792,512]{1,0:T(8,128)(2,1)S(1)} %shard_map.80.refs_0_.refs_1_.refs_4_.refs_2_, bf16[1792,512]{1,0:T(8,128)(2,1)S(1)} %collective-permute-done.20.refs_2_.refs_3_.refs_1_, bf16[128,1792]{1,0:T(8,128)(2,1)S(1)} %shard_map.82.refs_2_.refs_0_), custom_call_target="tpu_custom_call" | custom-call | flops 1 | bytes 1 | tf_op jit(solution)/shard_map/pallas_call | solution.py:56
  117.3 2.4 %shard_map.84 = (f32[256,256]{1,0:T(8,128)S(1)}, bf16[256,256]{1,0:T(8,128)(2,1)S(1)}) custom-call(s32[14]{0:T(128)S(1)} %stack.59.at_ref, bf16[1792,512]{1,0:T(8,128)(2,1)S(1)} %shard_map.80.refs_0_.refs_1_.refs_4_.refs_2_, bf16[1792,512]{1,0:T(8,128)(2,1)S(1)} %collective-permute-done.20.refs_2_.refs_3_.refs_1_, ...), custom_call_target="tpu_custom_call" | custom-call | flops 1 | bytes 1 | tf_op jit(solution)/shard_map/pallas_call | solution.py:56
  121.4 1.8 %collective-permute-start.30 = (bf16[7,64,512]{2,1,0:T(8,128)(2,1)S(1)}, bf16[7,64,512]{2,1,0:T(8,128)(2,1)S(1)}, u32[]{:S(2)}, u32[]{:S(2)}) collective-permute-start(bf16[7,64,512]{2,1,0:T(8,128)(2,1)S(1)} %bitcast.19), channel_id=1, source_target_pairs={{0,192},{1,65},{2,194},{3,67},{32,224},{33,97},{34,226},{35,99},{6... | collective-permute-start | bytes 1376264 | tf_op jit(solution)/shard_map/ppermute | solution.py:40
  123.2 3.0 %collective-permute-done.24.refs_3_.refs_2_ = bf16[128,1792]{1,0:T(8,128)(2,1)S(1)} collective-permute-done((bf16[128,1792]{1,0:T(8,128)(2,1)S(1)}, bf16[128,1792]{1,0:T(8,128)(2,1)S(1)}, u32[]{:S(2)}, u32[]{:S(2)}) %collective-permute-start.24) | collective-permute-done | bytes 458784 | tf_op jit(solution)/shard_map/ppermute | solution.py:40
  127.0 2.1 %collective-permute-start.25 = (bf16[128,1792]{1,0:T(8,128)(2,1)S(1)}, bf16[128,1792]{1,0:T(8,128)(2,1)S(1)}, u32[]{:S(2)}, u32[]{:S(2)}) collective-permute-start(bf16[128,1792]{1,0:T(8,128)(2,1)S(1)} %shard_map.86.refs_4_.refs_0_), channel_id=1, source_target_pairs={{0,192},{1,65},{2,194},{3,67},{32,224},{33,97},{34,226},{35,99},{6... | collective-permute-start | bytes 1376264 | tf_op jit(solution)/shard_map/ppermute | solution.py:40
  129.4 6.3 %collective-permute-start.31 = (bf16[256,256]{1,0:T(8,128)(2,1)S(1)}, bf16[256,256]{1,0:T(8,128)(2,1)S(1)}, u32[]{:S(2)}, u32[]{:S(2)}) collective-permute-start(bf16[256,256]{1,0:T(8,128)(2,1)S(1)} %get-tuple-element.54), channel_id=1, source_target_pairs={{0,16},{4,20},{8,24},{12,28},{16,0},{20,4},{24,8},{28,12},{1,17},{... | collective-permute-start | bytes 393224 | tf_op jit(solution)/shard_map/ppermute | solution.py:426
  135.7 1.8 %collective-permute-start.29 = (bf16[128,1792]{1,0:T(8,128)(2,1)S(1)}, bf16[128,1792]{1,0:T(8,128)(2,1)S(1)}, u32[]{:S(2)}, u32[]{:S(2)}) collective-permute-start(bf16[128,1792]{1,0:T(8,128)(2,1)S(1)} %collective-permute-done.28.refs_1_), channel_id=1, source_target_pairs={{0,64},{1,193},{2,66},{3,195},{32,96},{33,225},{34,98},{35,227},{6... | collective-permute-start | bytes 1376264 | tf_op jit(solution)/shard_map/ppermute | solution.py:40
  137.5 4.1 %collective-permute-done.31.refs_1_ = bf16[256,256]{1,0:T(8,128)(2,1)S(1)} collective-permute-done((bf16[256,256]{1,0:T(8,128)(2,1)S(1)}, bf16[256,256]{1,0:T(8,128)(2,1)S(1)}, u32[]{:S(2)}, u32[]{:S(2)}) %collective-permute-start.31) | collective-permute-done | bytes 131104 | tf_op jit(solution)/shard_map/ppermute | solution.py:426
  144.3 2.4 %collective-permute-start.33 = (bf16[128,256]{1,0:T(8,128)(2,1)S(1)}, bf16[128,256]{1,0:T(8,128)(2,1)S(1)}, u32[]{:S(2)}, u32[]{:S(2)}) collective-permute-start(bf16[128,256]{1,0:T(8,128)(2,1)S(1)} %get-tuple-element.58), channel_id=1, source_target_pairs={{0,8},{4,12},{8,0},{12,4},{16,24},{20,28},{24,16},{28,20},{1,9},{5... | collective-permute-start | bytes 196616 | tf_op jit(solution)/shard_map/ppermute | solution.py:426
  146.7 2.8 %collective-permute-done.33.refs_1_ = bf16[128,256]{1,0:T(8,128)(2,1)S(1)} collective-permute-done((bf16[128,256]{1,0:T(8,128)(2,1)S(1)}, bf16[128,256]{1,0:T(8,128)(2,1)S(1)}, u32[]{:S(2)}, u32[]{:S(2)}) %collective-permute-start.33) | collective-permute-done | bytes 65568 | tf_op jit(solution)/shard_map/ppermute | solution.py:426
  150.6 3.7 %collective-permute-start.34 = (bf16[7,16,512]{2,1,0:T(8,128)(2,1)S(1)}, bf16[7,16,512]{2,1,0:T(8,128)(2,1)S(1)}, u32[]{:S(2)}, u32[]{:S(2)}) collective-permute-start(bf16[7,16,512]{2,1,0:T(8,128)(2,1)S(1)} %get-tuple-element.61), channel_id=1, source_target_pairs={{0,32},{1,33},{2,34},{3,35},{32,0},{33,1},{34,2},{35,3},{64,96},{6... | collective-permute-start | bytes 344072 | tf_op jit(solution)/shard_map/ppermute | solution.py:40
  154.3 2.3 %shard_map.87 = (bf16[512,3584]{1,0:T(8,128)(2,1)}, f32[8,128]{1,0:T(8,128)S(1)}) custom-call(s32[14]{0:T(128)S(1)} %stack.59.at_ref, bf16[128,1792]{1,0:T(8,128)(2,1)S(1)} %shard_map.82.refs_2_.refs_0_, bf16[128,1792]{1,0:T(8,128)(2,1)S(1)} %collective-permute-done.28.refs_1_, bf16[128,1792]{1,0:T(8,128)(2,1)S(1)} %collective-permute-done.24.refs_3_.refs_2_, ...), custom_call_target="tpu_custom_call" | custom-call | flops 1 | bytes 1 | tf_op jit(solution)/shard_map/pallas_call | solution.py:56
  156.6 1.6 collective-permute-done.35.refs_1_
  158.2 1.2 shard_map.92
  160.4 2.4 %shard_map.93 = (bf16[512,3584]{1,0:T(8,128)(2,1)}, f32[8,128]{1,0:T(8,128)}) custom-call(s32[14]{0:T(128)S(1)} %stack.59.at_ref, bf16[128,1792]{1,0:T(8,128)(2,1)S(1)} %shard_map.86.refs_4_.refs_0_, bf16[128,1792]{1,0:T(8,128)(2,1)S(1)} %collective-permute-done.25.refs_1_, ...), custom_call_target="tpu_custom_call", output_to_operand_aliasing={{0}: (5, {})} | custom-call | flops 1 | bytes 1 | tf_op jit(solution)/shard_map/pallas_call | solution.py:56
  (66 shorter events, 22.8 us)
Async XLA Ops:
  0.6 8.6 %collective-permute-start.3 = (bf16[512,3584]{1,0:T(8,128)(2,1)}, bf16[512,3584]{1,0:T(8,128)(2,1)}, u32[]{:S(2)}, u32[]{:S(2)}) collective-permute-start(bf16[512,3584]{1,0:T(8,128)(2,1)} %refs_0_.9), channel_id=1, source_target_pairs={{0,1},{1,0},{2,3},{3,2},{32,33},{33,32},{34,35},{35,34},{64,65},{6... | collective-permute-start | bytes 11010056 | tf_op jit(solution)/shard_map/ppermute | solution.py:40
  0.7 8.5 %collective-permute-start.4 = (bf16[512,1024]{1,0:T(8,128)(2,1)}, bf16[512,1024]{1,0:T(8,128)(2,1)S(1)}, u32[]{:S(2)}, u32[]{:S(2)}) collective-permute-start(bf16[512,1024]{1,0:T(8,128)(2,1)} %refs_2_.3), channel_id=1, source_target_pairs={{0,1},{1,0},{2,3},{3,2},{32,33},{33,32},{34,35},{35,34},{64,65},{6... | collective-permute-start | bytes 3145736 | tf_op jit(solution)/shard_map/ppermute | solution.py:40
  1.3 2.0 %copy-start = (bf16[512,3584]{1,0:T(8,128)(2,1)S(1)}, bf16[512,3584]{1,0:T(8,128)(2,1)}, u32[]{:S(2)}) copy-start(bf16[512,3584]{1,0:T(8,128)(2,1)} %refs_0_.9) | copy-start | bytes 11010052
  3.4 3.5 %copy-start.2 = (bf16[3584,256]{1,0:T(8,128)(2,1)S(1)}, bf16[3584,256]{1,0:T(8,128)(2,1)}, u32[]{:S(2)}) copy-start(bf16[3584,256]{1,0:T(8,128)(2,1)} %refs_1_.5) | copy-start | bytes 5505028
  4.0 26.5 %collective-permute-start.5 = (bf16[512,1024]{1,0:T(8,128)(2,1)S(1)}, bf16[512,1024]{1,0:T(8,128)(2,1)S(1)}, u32[]{:S(2)}, u32[]{:S(2)}) collective-permute-start(bf16[512,1024]{1,0:T(8,128)(2,1)S(1)} %shard_map.66.refs_2_), channel_id=1, source_target_pairs={{0,34},{1,35},{2,32},{3,33},{32,2},{33,3},{34,0},{35,1},{64,98},{6... | collective-permute-start | bytes 3145736 | tf_op jit(solution)/shard_map/ppermute | solution.py:40
  6.9 1.4 copy-start.3
  7.0 2.4 %copy-start.1 = (bf16[512,3584]{1,0:T(8,128)(2,1)S(1)}, bf16[512,3584]{1,0:T(8,128)(2,1)}, u32[]{:S(2)}) copy-start(bf16[512,3584]{1,0:T(8,128)(2,1)} %refs_0_.9) | copy-start | bytes 11010052
  7.0 22.2 %collective-permute-start.2 = (bf16[1792,256]{1,0:T(8,128)(2,1)S(1)}, bf16[1792,256]{1,0:T(8,128)(2,1)S(1)}, u32[]{:S(2)}, u32[]{:S(2)}) collective-permute-start(bf16[1792,256]{1,0:T(8,128)(2,1)S(1)} %slice.3), channel_id=1, source_target_pairs={{0,2},{1,3},{2,0},{3,1},{32,34},{33,35},{34,32},{35,33},{64,66},{6... | collective-permute-start | bytes 2752520 | tf_op jit(solution)/shard_map/ppermute | solution.py:40
  7.3 24.0 %collective-permute-start = (bf16[3584,256]{1,0:T(8,128)(2,1)S(1)}, bf16[3584,256]{1,0:T(8,128)(2,1)S(1)}, u32[]{:S(2)}, u32[]{:S(2)}) collective-permute-start(bf16[3584,256]{1,0:T(8,128)(2,1)S(1)} %copy-done.2), channel_id=1, source_target_pairs={{0,1},{1,0},{2,3},{3,2},{32,33},{33,32},{34,35},{35,34},{64,65},{6... | collective-permute-start | bytes 5505032 | tf_op jit(solution)/shard_map/ppermute | solution.py:40
  31.1 2.6 %collective-permute-start.6 = (bf16[1792,256]{1,0:T(8,128)(2,1)S(1)}, bf16[1792,256]{1,0:T(8,128)(2,1)S(1)}, u32[]{:S(2)}, u32[]{:S(2)}) collective-permute-start(bf16[1792,256]{1,0:T(8,128)(2,1)S(1)} %shard_map.71.refs_5_), channel_id=1, source_target_pairs={{0,1},{1,0},{2,3},{3,2},{32,33},{33,32},{34,35},{35,34},{64,65},{6... | collective-permute-start | bytes 2752520 | tf_op jit(solution)/shard_map/ppermute | solution.py:40
  37.0 8.6 %collective-permute-start.8 = (bf16[128,1792]{1,0:T(8,128)(2,1)S(1)}, bf16[128,1792]{1,0:T(8,128)(2,1)S(1)}, u32[]{:S(2)}, u32[]{:S(2)}) collective-permute-start(bf16[128,1792]{1,0:T(8,128)(2,1)S(1)} %get-tuple-element.39), channel_id=1, source_target_pairs={{0,64},{1,193},{2,66},{3,195},{32,96},{33,225},{34,98},{35,227},{6... | collective-permute-start | bytes 1376264 | tf_op jit(solution)/shard_map/ppermute | solution.py:40
  38.6 22.9 %collective-permute-start.1 = (bf16[1792,256]{1,0:T(8,128)(2,1)S(1)}, bf16[1792,256]{1,0:T(8,128)(2,1)S(1)}, u32[]{:S(2)}, u32[]{:S(2)}) collective-permute-start(bf16[1792,256]{1,0:T(8,128)(2,1)S(1)} %get-tuple-element.35.refs_1_), channel_id=1, source_target_pairs={{0,2},{1,3},{2,0},{3,1},{32,34},{33,35},{34,32},{35,33},{64,66},{6... | collective-permute-start | bytes 2752520 | tf_op jit(solution)/shard_map/ppermute | solution.py:40
  38.9 20.7 %collective-permute-start.10 = (bf16[512,768]{1,0:T(8,128)(2,1)S(1)}, bf16[512,768]{1,0:T(8,128)(2,1)S(1)}, u32[]{:S(2)}, u32[]{:S(2)}) collective-permute-start(bf16[512,768]{1,0:T(8,128)(2,1)S(1)} %get-tuple-element.40), channel_id=1, source_target_pairs={{0,35},{1,34},{2,33},{3,32},{32,3},{33,2},{34,1},{35,0},{64,99},{6... | collective-permute-start | bytes 2359304 | tf_op jit(solution)/shard_map/ppermute | solution.py:40
  42.3 9.6 %collective-permute-start.7 = (bf16[128,1792]{1,0:T(8,128)(2,1)S(1)}, bf16[128,1792]{1,0:T(8,128)(2,1)S(1)}, u32[]{:S(2)}, u32[]{:S(2)}) collective-permute-start(bf16[128,1792]{1,0:T(8,128)(2,1)S(1)} %get-tuple-element.37), channel_id=1, source_target_pairs={{0,64},{1,193},{2,66},{3,195},{32,96},{33,225},{34,98},{35,227},{6... | collective-permute-start | bytes 1376264 | tf_op jit(solution)/shard_map/ppermute | solution.py:40
  46.4 9.8 %collective-permute-start.9 = (bf16[128,1792]{1,0:T(8,128)(2,1)S(1)}, bf16[128,1792]{1,0:T(8,128)(2,1)S(1)}, u32[]{:S(2)}, u32[]{:S(2)}) collective-permute-start(bf16[128,1792]{1,0:T(8,128)(2,1)S(1)} %shard_map.73), channel_id=1, source_target_pairs={{0,192},{1,65},{2,194},{3,67},{32,224},{33,97},{34,226},{35,99},{6... | collective-permute-start | bytes 1376264 | tf_op jit(solution)/shard_map/ppermute | solution.py:40
  62.2 2.6 %collective-permute-start.11 = (bf16[1792,256]{1,0:T(8,128)(2,1)S(1)}, bf16[1792,256]{1,0:T(8,128)(2,1)S(1)}, u32[]{:S(2)}, u32[]{:S(2)}) collective-permute-start(bf16[1792,256]{1,0:T(8,128)(2,1)S(1)} %shard_map.75.refs_5_), channel_id=1, source_target_pairs={{0,1},{1,0},{2,3},{3,2},{32,33},{33,32},{34,35},{35,34},{64,65},{6... | collective-permute-start | bytes 2752520 | tf_op jit(solution)/shard_map/ppermute | solution.py:40
  62.4 27.5 %collective-permute-start.18 = (bf16[1024,512]{1,0:T(8,128)(2,1)S(1)}, bf16[1024,512]{1,0:T(8,128)(2,1)S(1)}, u32[]{:S(2)}, u32[]{:S(2)}) collective-permute-start(bf16[1024,512]{1,0:T(8,128)(2,1)S(1)} %shard_map.70.refs_1_), channel_id=1, source_target_pairs={{0,2},{1,3},{2,0},{3,1},{32,34},{33,35},{34,32},{35,33},{64,66},{6... | collective-permute-start | bytes 3145736 | tf_op jit(solution)/shard_map/ppermute | solution.py:40
  68.0 8.6 %collective-permute-start.13 = (bf16[128,1792]{1,0:T(8,128)(2,1)S(1)}, bf16[128,1792]{1,0:T(8,128)(2,1)S(1)}, u32[]{:S(2)}, u32[]{:S(2)}) collective-permute-start(bf16[128,1792]{1,0:T(8,128)(2,1)S(1)} %get-tuple-element.44), channel_id=1, source_target_pairs={{0,64},{1,193},{2,66},{3,195},{32,96},{33,225},{34,98},{35,227},{6... | collective-permute-start | bytes 1376264 | tf_op jit(solution)/shard_map/ppermute | solution.py:40
  68.9 21.1 %collective-permute-start.17 = (bf16[512,512]{1,0:T(8,128)(2,1)S(1)}, bf16[512,512]{1,0:T(8,128)(2,1)S(1)}, u32[]{:S(2)}, u32[]{:S(2)}) collective-permute-start(bf16[512,512]{1,0:T(8,128)(2,1)S(1)} %get-tuple-element.46), channel_id=1, source_target_pairs={{0,35},{1,34},{2,33},{3,32},{32,3},{33,2},{34,1},{35,0},{64,99},{6... | collective-permute-start | bytes 1572872 | tf_op jit(solution)/shard_map/ppermute | solution.py:40
  71.4 11.0 %collective-permute-start.12 = (bf16[128,1792]{1,0:T(8,128)(2,1)S(1)}, bf16[128,1792]{1,0:T(8,128)(2,1)S(1)}, u32[]{:S(2)}, u32[]{:S(2)}) collective-permute-start(bf16[128,1792]{1,0:T(8,128)(2,1)S(1)} %get-tuple-element.42), channel_id=1, source_target_pairs={{0,64},{1,193},{2,66},{3,195},{32,96},{33,225},{34,98},{35,227},{6... | collective-permute-start | bytes 1376264 | tf_op jit(solution)/shard_map/ppermute | solution.py:40
  77.4 9.8 %collective-permute-start.14 = (bf16[128,1792]{1,0:T(8,128)(2,1)S(1)}, bf16[128,1792]{1,0:T(8,128)(2,1)S(1)}, u32[]{:S(2)}, u32[]{:S(2)}) collective-permute-start(bf16[128,1792]{1,0:T(8,128)(2,1)S(1)} %shard_map.77), channel_id=1, source_target_pairs={{0,192},{1,65},{2,194},{3,67},{32,224},{33,97},{34,226},{35,99},{6... | collective-permute-start | bytes 1376264 | tf_op jit(solution)/shard_map/ppermute | solution.py:40
  78.6 11.4 %collective-permute-start.16 = (bf16[512,256]{1,0:T(8,128)(2,1)S(1)}, bf16[512,256]{1,0:T(8,128)(2,1)S(1)}, u32[]{:S(2)}, u32[]{:S(2)}) collective-permute-start(bf16[512,256]{1,0:T(8,128)(2,1)S(1)} %get-tuple-element.45), channel_id=1, source_target_pairs={{0,34},{1,35},{2,32},{3,33},{32,2},{33,3},{34,0},{35,1},{64,98},{6... | collective-permute-start | bytes 786440 | tf_op jit(solution)/shard_map/ppermute | solution.py:40
  90.6 2.0 %collective-permute-start.19 = (bf16[512,512]{1,0:T(8,128)(2,1)S(1)}, bf16[512,512]{1,0:T(8,128)(2,1)S(1)}, u32[]{:S(2)}, u32[]{:S(2)}) collective-permute-start(bf16[512,512]{1,0:T(8,128)(2,1)S(1)} %shard_map.79), channel_id=1, source_target_pairs={{0,1},{1,0},{2,3},{3,2},{32,33},{33,32},{34,35},{35,34},{64,65},{6... | collective-permute-start | bytes 1572872 | tf_op jit(solution)/shard_map/ppermute | solution.py:40
  96.2 3.9 %collective-permute-start.20 = (bf16[1792,512]{1,0:T(8,128)(2,1)S(1)}, bf16[1792,512]{1,0:T(8,128)(2,1)S(1)}, u32[]{:S(2)}, u32[]{:S(2)}) collective-permute-start(bf16[1792,512]{1,0:T(8,128)(2,1)S(1)} %shard_map.80.refs_0_.refs_1_.refs_4_.refs_2_), channel_id=1, source_target_pairs={{0,1},{1,0},{2,3},{3,2},{32,33},{33,32},{34,35},{35,34},{64,65},{6... | collective-permute-start | bytes 5505032 | tf_op jit(solution)/shard_map/ppermute | solution.py:40
  96.4 14.9 %collective-permute-start.22 = (bf16[128,1792]{1,0:T(8,128)(2,1)S(1)}, bf16[128,1792]{1,0:T(8,128)(2,1)S(1)}, u32[]{:S(2)}, u32[]{:S(2)}) collective-permute-start(bf16[128,1792]{1,0:T(8,128)(2,1)S(1)} %shard_map.74.refs_1_.refs_8_.refs_0_), channel_id=1, source_target_pairs={{0,32},{1,33},{2,34},{3,35},{32,0},{33,1},{34,2},{35,3},{64,96},{6... | collective-permute-start | bytes 1376264 | tf_op jit(solution)/shard_map/ppermute | solution.py:40
  103.5 8.6 %collective-permute-start.21 = (bf16[7,64,512]{2,1,0:T(8,128)(2,1)S(1)}, bf16[7,64,512]{2,1,0:T(8,128)(2,1)S(1)}, u32[]{:S(2)}, u32[]{:S(2)}) collective-permute-start(bf16[7,64,512]{2,1,0:T(8,128)(2,1)S(1)} %get-tuple-element.48), channel_id=1, source_target_pairs={{0,64},{1,193},{2,66},{3,195},{32,96},{33,225},{34,98},{35,227},{6... | collective-permute-start | bytes 1376264 | tf_op jit(solution)/shard_map/ppermute | solution.py:40
  104.8 15.7 %collective-permute-start.15 = (bf16[128,1792]{1,0:T(8,128)(2,1)S(1)}, bf16[128,1792]{1,0:T(8,128)(2,1)S(1)}, u32[]{:S(2)}, u32[]{:S(2)}) collective-permute-start(bf16[128,1792]{1,0:T(8,128)(2,1)S(1)} %shard_map.78.refs_1_.refs_9_.refs_0_), channel_id=1, source_target_pairs={{0,32},{1,33},{2,34},{3,35},{32,0},{33,1},{34,2},{35,3},{64,96},{6... | collective-permute-start | bytes 1376264 | tf_op jit(solution)/shard_map/ppermute | solution.py:40
  105.1 15.4 %collective-permute-start.23 = (bf16[7,64,512]{2,1,0:T(8,128)(2,1)S(1)}, bf16[7,64,512]{2,1,0:T(8,128)(2,1)S(1)}, u32[]{:S(2)}, u32[]{:S(2)}) collective-permute-start(bf16[7,64,512]{2,1,0:T(8,128)(2,1)S(1)} %get-tuple-element.51), channel_id=1, source_target_pairs={{0,64},{1,193},{2,66},{3,195},{32,96},{33,225},{34,98},{35,227},{6... | collective-permute-start | bytes 1376264 | tf_op jit(solution)/shard_map/ppermute | solution.py:40
  112.9 13.3 %collective-permute-start.24 = (bf16[128,1792]{1,0:T(8,128)(2,1)S(1)}, bf16[128,1792]{1,0:T(8,128)(2,1)S(1)}, u32[]{:S(2)}, u32[]{:S(2)}) collective-permute-start(bf16[128,1792]{1,0:T(8,128)(2,1)S(1)} %shard_map.82.refs_2_.refs_0_), channel_id=1, source_target_pairs={{0,64},{1,193},{2,66},{3,195},{32,96},{33,225},{34,98},{35,227},{6... | collective-permute-start | bytes 1376264 | tf_op jit(solution)/shard_map/ppermute | solution.py:40
  114.2 21.5 %collective-permute-start.28 = (bf16[128,1792]{1,0:T(8,128)(2,1)S(1)}, bf16[128,1792]{1,0:T(8,128)(2,1)S(1)}, u32[]{:S(2)}, u32[]{:S(2)}) collective-permute-start(bf16[128,1792]{1,0:T(8,128)(2,1)S(1)} %shard_map.82.refs_2_.refs_0_), channel_id=1, source_target_pairs={{0,192},{1,65},{2,194},{3,67},{32,224},{33,97},{34,226},{35,99},{6... | collective-permute-start | bytes 1376264 | tf_op jit(solution)/shard_map/ppermute | solution.py:40
  121.4 20.8 %collective-permute-start.30 = (bf16[7,64,512]{2,1,0:T(8,128)(2,1)S(1)}, bf16[7,64,512]{2,1,0:T(8,128)(2,1)S(1)}, u32[]{:S(2)}, u32[]{:S(2)}) collective-permute-start(bf16[7,64,512]{2,1,0:T(8,128)(2,1)S(1)} %bitcast.19), channel_id=1, source_target_pairs={{0,192},{1,65},{2,194},{3,67},{32,224},{33,97},{34,226},{35,99},{6... | collective-permute-start | bytes 1376264 | tf_op jit(solution)/shard_map/ppermute | solution.py:40
  127.0 16.4 %collective-permute-start.25 = (bf16[128,1792]{1,0:T(8,128)(2,1)S(1)}, bf16[128,1792]{1,0:T(8,128)(2,1)S(1)}, u32[]{:S(2)}, u32[]{:S(2)}) collective-permute-start(bf16[128,1792]{1,0:T(8,128)(2,1)S(1)} %shard_map.86.refs_4_.refs_0_), channel_id=1, source_target_pairs={{0,192},{1,65},{2,194},{3,67},{32,224},{33,97},{34,226},{35,99},{6... | collective-permute-start | bytes 1376264 | tf_op jit(solution)/shard_map/ppermute | solution.py:40
  129.1 20.9 %collective-permute-start.26 = (bf16[128,1792]{1,0:T(8,128)(2,1)S(1)}, bf16[128,1792]{1,0:T(8,128)(2,1)S(1)}, u32[]{:S(2)}, u32[]{:S(2)}) collective-permute-start(bf16[128,1792]{1,0:T(8,128)(2,1)S(1)} %shard_map.86.refs_4_.refs_0_), channel_id=1, source_target_pairs={{0,64},{1,193},{2,66},{3,195},{32,96},{33,225},{34,98},{35,227},{6... | collective-permute-start | bytes 1376264 | tf_op jit(solution)/shard_map/ppermute | solution.py:40
  129.4 12.2 %collective-permute-start.31 = (bf16[256,256]{1,0:T(8,128)(2,1)S(1)}, bf16[256,256]{1,0:T(8,128)(2,1)S(1)}, u32[]{:S(2)}, u32[]{:S(2)}) collective-permute-start(bf16[256,256]{1,0:T(8,128)(2,1)S(1)} %get-tuple-element.54), channel_id=1, source_target_pairs={{0,16},{4,20},{8,24},{12,28},{16,0},{20,4},{24,8},{28,12},{1,17},{... | collective-permute-start | bytes 393224 | tf_op jit(solution)/shard_map/ppermute | solution.py:426
  135.7 18.6 %collective-permute-start.29 = (bf16[128,1792]{1,0:T(8,128)(2,1)S(1)}, bf16[128,1792]{1,0:T(8,128)(2,1)S(1)}, u32[]{:S(2)}, u32[]{:S(2)}) collective-permute-start(bf16[128,1792]{1,0:T(8,128)(2,1)S(1)} %collective-permute-done.28.refs_1_), channel_id=1, source_target_pairs={{0,64},{1,193},{2,66},{3,195},{32,96},{33,225},{34,98},{35,227},{6... | collective-permute-start | bytes 1376264 | tf_op jit(solution)/shard_map/ppermute | solution.py:40
  142.9 7.1 %collective-permute-start.32 = (bf16[7,32,512]{2,1,0:T(8,128)(2,1)S(1)}, bf16[7,32,512]{2,1,0:T(8,128)(2,1)S(1)}, u32[]{:S(2)}, u32[]{:S(2)}) collective-permute-start(bf16[7,32,512]{2,1,0:T(8,128)(2,1)S(1)} %get-tuple-element.57), channel_id=1, source_target_pairs={{0,2},{1,3},{2,0},{3,1},{32,34},{33,35},{34,32},{35,33},{64,66},{6... | collective-permute-start | bytes 688136 | tf_op jit(solution)/shard_map/ppermute | solution.py:40
  143.4 17.0 %collective-permute-start.27 = (bf16[128,1792]{1,0:T(8,128)(2,1)S(1)}, bf16[128,1792]{1,0:T(8,128)(2,1)S(1)}, u32[]{:S(2)}, u32[]{:S(2)}) collective-permute-start(bf16[128,1792]{1,0:T(8,128)(2,1)S(1)} %collective-permute-done.25.refs_1_), channel_id=1, source_target_pairs={{0,64},{1,193},{2,66},{3,195},{32,96},{33,225},{34,98},{35,227},{6... | collective-permute-start | bytes 1376264 | tf_op jit(solution)/shard_map/ppermute | solution.py:40
  144.3 5.2 %collective-permute-start.33 = (bf16[128,256]{1,0:T(8,128)(2,1)S(1)}, bf16[128,256]{1,0:T(8,128)(2,1)S(1)}, u32[]{:S(2)}, u32[]{:S(2)}) collective-permute-start(bf16[128,256]{1,0:T(8,128)(2,1)S(1)} %get-tuple-element.58), channel_id=1, source_target_pairs={{0,8},{4,12},{8,0},{12,4},{16,24},{20,28},{24,16},{28,20},{1,9},{5... | collective-permute-start | bytes 196616 | tf_op jit(solution)/shard_map/ppermute | solution.py:426
  150.6 9.7 %collective-permute-start.34 = (bf16[7,16,512]{2,1,0:T(8,128)(2,1)S(1)}, bf16[7,16,512]{2,1,0:T(8,128)(2,1)S(1)}, u32[]{:S(2)}, u32[]{:S(2)}) collective-permute-start(bf16[7,16,512]{2,1,0:T(8,128)(2,1)S(1)} %get-tuple-element.61), channel_id=1, source_target_pairs={{0,32},{1,33},{2,34},{3,35},{32,0},{33,1},{34,2},{35,3},{64,96},{6... | collective-permute-start | bytes 344072 | tf_op jit(solution)/shard_map/ppermute | solution.py:40
  154.3 3.9 %collective-permute-start.35 = (bf16[64,256]{1,0:T(8,128)(2,1)S(1)}, bf16[64,256]{1,0:T(8,128)(2,1)S(1)}, u32[]{:S(2)}, u32[]{:S(2)}) collective-permute-start(bf16[64,256]{1,0:T(8,128)(2,1)S(1)} %get-tuple-element.62), channel_id=1, source_target_pairs={{0,4},{4,0},{8,12},{12,8},{16,20},{20,16},{24,28},{28,24},{1,5},{5... | collective-permute-start | bytes 98312 | tf_op jit(solution)/shard_map/ppermute | solution.py:426
  160.3 2.4 %copy-start.4 = (f32[7,16,512]{2,1,0:T(8,128)}, f32[7,16,512]{2,1,0:T(8,128)S(1)}, u32[]{:S(2)}) copy-start(f32[7,16,512]{2,1,0:T(8,128)S(1)} %convert_add_fusion.refs_5_) | copy-start | bytes 688132

commit v5 on v4

--- a/solution.py
+++ b/solution.py
@@ -328,11 +328,11 @@
     own, near, came_near, came_own = scatter_sends(*left)
     def go_round(total):
         near = send(total, Y_SECOND)
-        off = send(total, Y_FIRST)
-        return [total, near, off, send(near, Y_FIRST)]
+        return [total, near, send(total, Y_FIRST)]
 
     totals = [add(at, [mine[0], beside[0]], after=[came_near])]
     rounds = [go_round(totals[0])]
+    rounds[0].append(send(rounds[0][1], Y_FIRST))
     def slab_kernel(at, own_ref, other_ref, result_ref, token_ref):
         token_ref[...] = jnp.zeros_like(token_ref)
         held = pl.program_id(0) == at[CORE_AT]
@@ -405,8 +405,9 @@
     near = add(at, [near.reshape(blocks), came_near.reshape(blocks)], after=[stay, came_own, beside[1]])
     totals.append(add(at, [mine[1], beside[1]], after=[near, rounds[0][2]]))
     rounds.append(go_round(totals[1]))
-    grad_hidden, placed = place(0, rounds[0], None, [totals[1]])
-    def right_sum(stay, came, bit):
+    grad_hidden, placed = place(0, rounds[0], None, [near])
+
+    def right_sum(stay, came, bit, after):
         rows = stay.shape[0] // 2
 
         def kernel(at_ref, stay_ref, came_ref, keep_ref, send_ref):
@@ -418,14 +419,15 @@
         whole = pl.BlockSpec(stay.shape, lambda i, at: (0, 0))
         half_of = pl.BlockSpec((rows, slab), lambda i, at: (0, 0))
         return call(
-            kernel, at, [stay, came], [whole] * 2, [shape((rows, slab), F32), shape((rows, slab))], [half_of] * 2
+            kernel, at, [stay, came], [whole] * 2, [shape((rows, slab), F32), shape((rows, slab))], [half_of] * 2,
+            after=after,
         )
 
     right_steps = []
     for i, bit in enumerate(bits):
         came_z = lax.ppermute(go, "col", [(j, j ^ bit) for j in range(cols)])
         if i < len(bits) - 1:
-            stay, go = right_sum(stay, came_z, Z_HIGH + 1 + i)
+            stay, go = right_sum(stay, came_z, Z_HIGH + 1 + i, [placed] if i else [])
             right_steps.append(stay)
 
     near = near.reshape(own.shape)
@@ -448,8 +450,12 @@
         )
 
     stays, goes = left_sum([own, came_own, send(near, Y_SECOND)], 4, X_LO_AT, right_steps[:1])
+    passed = copy_of(at, rounds[1][1], after=[goes])
     stays, goes = left_sum([stays, send(goes, X_LO)], 2, X_HI_AT, [*right_steps[1:], rounds[1][2]])
-    left_stats = stays + send(goes, X_HI).astype(F32)
+    came = send(goes, X_HI)
+
+    rounds[1].append(send(passed, Y_FIRST))
+    grad_hidden, placed = place(1, rounds[1], grad_hidden, [goes, right_steps[-1]])
 
     def last_kernel(at, mine_ref, came_ref, result_ref):
         result_ref[...] = mine_ref[...] + came_ref[...].astype(F32)
@@ -458,8 +464,9 @@
     right_stats = call(
         last_kernel, at, [stay, came_z], [spec] * 2, [shape(stay.shape, F32)], [spec], after=[placed]
     )[0].T
-
-    grad_hidden, _ = place(1, rounds[1], grad_hidden, [left_stats, right_stats])
+    spec = pl.BlockSpec(stays.shape, lambda i, at: (0, 0, 0))
+    left_stats = call(last_kernel, at, [stays, came], [spec] * 2, [shape(stays.shape, F32)], [spec], after=[placed])[0]
+
     return grad_hidden, grad_slab, left_stats, right_stats
 
 

time: 163 us -> 162 us (level)
  waiting for transfers between devices: 66.3 us -> 62.3 us
  Pallas kernels: 46.3 us -> 48.2 us
    ppermute x3, waiting for transfers between devices: 8.45 us -> 4.81 us  [body(): came_z = lax.ppermute(go, 'col', [(j, j ^ bit) for j in range(cols)])]
    ppermute x33, starting transfers between devices: 37.3 us -> 40.3 us  [send(): return lax.ppermute(x, ('row', 'rep'), perm)]
    pallas_call x28 -> x30, Pallas kernels: 46.3 us -> 48.2 us  [call(): pl.pallas_call(run, grid_spec=pltpu.PrefetchScalarGridSpec(num_scalar_pre...]
  transfers between devices with their start and end apart: 36 -> 36, of which waited for: 23 -> 22; matrix products, arithmetic and copies ran while one was open for 1% -> 0% of each run, Pallas kernels for 22% -> 24%
where the time goes in v5:
time: 162 us; the launch traced here: 161 us
  waiting for transfers between devices  62.3 us (38%)
  Pallas kernels  48.2 us (30%)
  starting transfers between devices  47.6 us (29%)
  local copies, waits for them, and re-layouts  2.24 us (1%)
    ppermute x33, waiting for transfers between devices, send(): return lax.ppermute(x, ('row', 'rep'), perm)  57.5 us
    pallas_call x30, Pallas kernels, call(): pl.pallas_call(run, grid_spec=pltpu.PrefetchScalarGridSpec(num_scalar_pre...  48.2 us
    ppermute x33, starting transfers between devices, send(): return lax.ppermute(x, ('row', 'rep'), perm)  40.3 us
    ppermute x3, starting transfers between devices, body(): came_z = lax.ppermute(go, 'col', [(j, j ^ bit) for j in range(cols)])  7.3 us
    ppermute x3, waiting for transfers between devices, body(): came_z = lax.ppermute(go, 'col', [(j, j ^ bit) for j in range(cols)])  4.81 us
  transfers between devices with their start and end apart: 36, of which 22 were waited for; matrix products, arithmetic and copies ran while one was open for 0% of the time, Pallas kernels for 24%

profile of v5, /device:TPU:32, one launch (start us, length us, event | category | flops | bytes accessed | tf_op | source)
XLA Modules:
  0.0 161.3 jit_solution(14777099255418393269)
XLA Ops:
  1.3 2.0 %copy-done = bf16[512,3584]{1,0:T(8,128)(2,1)S(1)} copy-done((bf16[512,3584]{1,0:T(8,128)(2,1)S(1)}, bf16[512,3584]{1,0:T(8,128)(2,1)}, u32[]{:S(2)}) %copy-start) | copy-done | bytes 3670040
  4.0 2.8 %collective-permute-start.5 = (bf16[512,1024]{1,0:T(8,128)(2,1)S(1)}, bf16[512,1024]{1,0:T(8,128)(2,1)S(1)}, u32[]{:S(2)}, u32[]{:S(2)}) collective-permute-start(bf16[512,1024]{1,0:T(8,128)(2,1)S(1)} %shard_map.66.refs_2_), channel_id=1, source_target_pairs={{0,34},{1,35},{2,32},{3,33},{32,2},{33,3},{34,0},{35,1},{64,98},{6... | collective-permute-start | bytes 3145736 | tf_op jit(solution)/shard_map/ppermute | solution.py:40
  9.3 6.4 %shard_map.69.refs_4_.refs_0_ = f32[1792,512]{1,0:T(8,128)S(1)} custom-call(s32[14]{0:T(128)S(1)} %stack.59.at_ref, bf16[512,3584]{1,0:T(8,128)(2,1)S(1)} %copy-done.1, bf16[512,3584]{1,0:T(8,128)(2,1)} %collective-permute-done.3.refs_1_, bf16[512,1024]{1,0:T(8,128)(2,1)S(1)} %copy-done.3, bf16[512,1024]{1,0:T(8,128)(2,1)S(1)} %collective-permute-done.4.refs_3_, ...), custom_call_target="tpu_custom_call" | custom-call | flops 1 | bytes 1 | tf_op jit(solution)/shard_map/pallas_call | solution.py:56
  15.7 3.1 %shard_map.70.refs_1_ = bf16[1024,512]{1,0:T(8,128)(2,1)S(1)} custom-call(s32[14]{0:T(128)S(1)} %stack.59.at_ref, bf16[512,3584]{1,0:T(8,128)(2,1)S(1)} %copy-done.1, bf16[512,3584]{1,0:T(8,128)(2,1)} %collective-permute-done.3.refs_1_, bf16[512,1024]{1,0:T(8,128)(2,1)S(1)} %copy-done.3, bf16[512,1024]{1,0:T(8,128)(2,1)S(1)} %collective-permute-done.4.refs_3_, ...), custom_call_target="tpu_custom_call" | custom-call | flops 1 | bytes 1 | tf_op jit(solution)/shard_map/pallas_call | solution.py:56
  18.9 10.3 %collective-permute-done.2.refs_0_.refs_3_ = bf16[1792,256]{1,0:T(8,128)(2,1)S(1)} collective-permute-done((bf16[1792,256]{1,0:T(8,128)(2,1)S(1)}, bf16[1792,256]{1,0:T(8,128)(2,1)S(1)}, u32[]{:S(2)}, u32[]{:S(2)}) %collective-permute-start.2) | collective-permute-done | bytes 917536 | tf_op jit(solution)/shard_map/ppermute | solution.py:40
  29.1 1.4 collective-permute-done.5.refs_2_.refs_1_
  31.3 2.4 %collective-permute-done.6.refs_4_ = bf16[1792,256]{1,0:T(8,128)(2,1)S(1)} collective-permute-done((bf16[1792,256]{1,0:T(8,128)(2,1)S(1)}, bf16[1792,256]{1,0:T(8,128)(2,1)S(1)}, u32[]{:S(2)}, u32[]{:S(2)}) %collective-permute-start.6) | collective-permute-done | bytes 917536 | tf_op jit(solution)/shard_map/ppermute | solution.py:40
  33.7 3.3 %shard_map.72 = (bf16[128,1792]{1,0:T(8,128)(2,1)S(1)}, bf16[128,1792]{1,0:T(8,128)(2,1)S(1)}, bf16[128,1792]{1,0:T(8,128)(2,1)S(1)}, bf16[128,1792]{1,0:T(8,128)(2,1)S(1)}) custom-call(s32[14]{0:T(128)S(1)} %stack.59.at_ref, bf16[512,1024]{1,0:T(8,128)(2,1)S(1)} %shard_map.68.refs_4_.refs_0_, bf16[3584,256]{1,0:T(8,128)(2,1)S(1)} %copy-done.2, ...), custom_call_target="tpu_custom_call" | custom-call | flops 1 | bytes 1 | tf_op jit(solution)/shard_map/pallas_call | solution.py:56
  37.0 1.7 %collective-permute-start.8 = (bf16[128,1792]{1,0:T(8,128)(2,1)S(1)}, bf16[128,1792]{1,0:T(8,128)(2,1)S(1)}, u32[]{:S(2)}, u32[]{:S(2)}) collective-permute-start(bf16[128,1792]{1,0:T(8,128)(2,1)S(1)} %get-tuple-element.40), channel_id=1, source_target_pairs={{0,64},{1,193},{2,66},{3,195},{32,96},{33,225},{34,98},{35,227},{6... | collective-permute-start | bytes 1376264 | tf_op jit(solution)/shard_map/ppermute | solution.py:40
  38.9 3.4 %collective-permute-start.10 = (bf16[512,768]{1,0:T(8,128)(2,1)S(1)}, bf16[512,768]{1,0:T(8,128)(2,1)S(1)}, u32[]{:S(2)}, u32[]{:S(2)}) collective-permute-start(bf16[512,768]{1,0:T(8,128)(2,1)S(1)} %get-tuple-element.41), channel_id=1, source_target_pairs={{0,35},{1,34},{2,33},{3,32},{32,3},{33,2},{34,1},{35,0},{64,99},{6... | collective-permute-start | bytes 2359304 | tf_op jit(solution)/shard_map/ppermute | solution.py:40
  42.4 3.1 %collective-permute-done.8.refs_1_ = bf16[128,1792]{1,0:T(8,128)(2,1)S(1)} collective-permute-done((bf16[128,1792]{1,0:T(8,128)(2,1)S(1)}, bf16[128,1792]{1,0:T(8,128)(2,1)S(1)}, u32[]{:S(2)}, u32[]{:S(2)}) %collective-permute-start.8) | collective-permute-done | bytes 458784 | tf_op jit(solution)/shard_map/ppermute | solution.py:40
  46.4 3.1 %collective-permute-start.9 = (bf16[128,1792]{1,0:T(8,128)(2,1)S(1)}, bf16[128,1792]{1,0:T(8,128)(2,1)S(1)}, u32[]{:S(2)}, u32[]{:S(2)}) collective-permute-start(bf16[128,1792]{1,0:T(8,128)(2,1)S(1)} %shard_map.73), channel_id=1, source_target_pairs={{0,192},{1,65},{2,194},{3,67},{32,224},{33,97},{34,226},{35,99},{6... | collective-permute-start | bytes 1376264 | tf_op jit(solution)/shard_map/ppermute | solution.py:40
  49.5 2.4 %collective-permute-done.7.refs_1_ = bf16[128,1792]{1,0:T(8,128)(2,1)S(1)} collective-permute-done((bf16[128,1792]{1,0:T(8,128)(2,1)S(1)}, bf16[128,1792]{1,0:T(8,128)(2,1)S(1)}, u32[]{:S(2)}, u32[]{:S(2)}) %collective-permute-start.7) | collective-permute-done | bytes 458784 | tf_op jit(solution)/shard_map/ppermute | solution.py:40
  51.9 4.3 %collective-permute-done.9.refs_2_ = bf16[128,1792]{1,0:T(8,128)(2,1)S(1)} collective-permute-done((bf16[128,1792]{1,0:T(8,128)(2,1)S(1)}, bf16[128,1792]{1,0:T(8,128)(2,1)S(1)}, u32[]{:S(2)}, u32[]{:S(2)}) %collective-permute-start.9) | collective-permute-done | bytes 458784 | tf_op jit(solution)/shard_map/ppermute | solution.py:40
  57.1 2.6 %collective-permute-done.10.refs_2_.refs_3_ = bf16[512,768]{1,0:T(8,128)(2,1)S(1)} collective-permute-done((bf16[512,768]{1,0:T(8,128)(2,1)S(1)}, bf16[512,768]{1,0:T(8,128)(2,1)S(1)}, u32[]{:S(2)}, u32[]{:S(2)}) %collective-permute-start.10) | collective-permute-done | bytes 786464 | tf_op jit(solution)/shard_map/ppermute | solution.py:40
  59.7 1.9 %collective-permute-done.1.refs_0_.refs_3_ = bf16[1792,256]{1,0:T(8,128)(2,1)S(1)} collective-permute-done((bf16[1792,256]{1,0:T(8,128)(2,1)S(1)}, bf16[1792,256]{1,0:T(8,128)(2,1)S(1)}, u32[]{:S(2)}, u32[]{:S(2)}) %collective-permute-start.1) | collective-permute-done | bytes 917536 | tf_op jit(solution)/shard_map/ppermute | solution.py:40
  62.7 2.0 %collective-permute-done.11.refs_4_ = bf16[1792,256]{1,0:T(8,128)(2,1)S(1)} collective-permute-done((bf16[1792,256]{1,0:T(8,128)(2,1)S(1)}, bf16[1792,256]{1,0:T(8,128)(2,1)S(1)}, u32[]{:S(2)}, u32[]{:S(2)}) %collective-permute-start.11) | collective-permute-done | bytes 917536 | tf_op jit(solution)/shard_map/ppermute | solution.py:40
  64.8 3.3 %shard_map.76 = (bf16[128,1792]{1,0:T(8,128)(2,1)S(1)}, bf16[128,1792]{1,0:T(8,128)(2,1)S(1)}, bf16[128,1792]{1,0:T(8,128)(2,1)S(1)}, bf16[128,1792]{1,0:T(8,128)(2,1)S(1)}) custom-call(s32[14]{0:T(128)S(1)} %stack.59.at_ref, bf16[512,1024]{1,0:T(8,128)(2,1)S(1)} %shard_map.68.refs_4_.refs_0_, bf16[3584,256]{1,0:T(8,128)(2,1)S(1)} %copy-done.2, ...), custom_call_target="tpu_custom_call" | custom-call | flops 1 | bytes 1 | tf_op jit(solution)/shard_map/pallas_call | solution.py:56
  68.9 2.5 %collective-permute-start.17 = (bf16[512,512]{1,0:T(8,128)(2,1)S(1)}, bf16[512,512]{1,0:T(8,128)(2,1)S(1)}, u32[]{:S(2)}, u32[]{:S(2)}) collective-permute-start(bf16[512,512]{1,0:T(8,128)(2,1)S(1)} %get-tuple-element.47), channel_id=1, source_target_pairs={{0,35},{1,34},{2,33},{3,32},{32,3},{33,2},{34,1},{35,0},{64,99},{6... | collective-permute-start | bytes 1572872 | tf_op jit(solution)/shard_map/ppermute | solution.py:40
  71.7 4.9 %collective-permute-done.13.refs_1_ = bf16[128,1792]{1,0:T(8,128)(2,1)S(1)} collective-permute-done((bf16[128,1792]{1,0:T(8,128)(2,1)S(1)}, bf16[128,1792]{1,0:T(8,128)(2,1)S(1)}, u32[]{:S(2)}, u32[]{:S(2)}) %collective-permute-start.13) | collective-permute-done | bytes 458784 | tf_op jit(solution)/shard_map/ppermute | solution.py:40
  77.4 1.1 collective-permute-start.14
  78.6 2.8 %collective-permute-start.16 = (bf16[512,256]{1,0:T(8,128)(2,1)S(1)}, bf16[512,256]{1,0:T(8,128)(2,1)S(1)}, u32[]{:S(2)}, u32[]{:S(2)}) collective-permute-start(bf16[512,256]{1,0:T(8,128)(2,1)S(1)} %get-tuple-element.46), channel_id=1, source_target_pairs={{0,34},{1,35},{2,32},{3,33},{32,2},{33,3},{34,0},{35,1},{64,98},{6... | collective-permute-start | bytes 786440 | tf_op jit(solution)/shard_map/ppermute | solution.py:40
  82.3 4.9 %collective-permute-done.14.refs_2_ = bf16[128,1792]{1,0:T(8,128)(2,1)S(1)} collective-permute-done((bf16[128,1792]{1,0:T(8,128)(2,1)S(1)}, bf16[128,1792]{1,0:T(8,128)(2,1)S(1)}, u32[]{:S(2)}, u32[]{:S(2)}) %collective-permute-start.14) | collective-permute-done | bytes 458784 | tf_op jit(solution)/shard_map/ppermute | solution.py:40
  88.1 1.8 %collective-permute-done.16.refs_2_ = bf16[512,256]{1,0:T(8,128)(2,1)S(1)} collective-permute-done((bf16[512,256]{1,0:T(8,128)(2,1)S(1)}, bf16[512,256]{1,0:T(8,128)(2,1)S(1)}, u32[]{:S(2)}, u32[]{:S(2)}) %collective-permute-start.16) | collective-permute-done | bytes 262176 | tf_op jit(solution)/shard_map/ppermute | solution.py:40
  90.7 1.9 %collective-permute-done.19.refs_6_ = bf16[512,512]{1,0:T(8,128)(2,1)S(1)} collective-permute-done((bf16[512,512]{1,0:T(8,128)(2,1)S(1)}, bf16[512,512]{1,0:T(8,128)(2,1)S(1)}, u32[]{:S(2)}, u32[]{:S(2)}) %collective-permute-start.19) | collective-permute-done | bytes 524320 | tf_op jit(solution)/shard_map/ppermute | solution.py:40
  92.6 3.6 %shard_map.80.refs_0_.refs_1_.refs_4_.refs_2_ = bf16[1792,512]{1,0:T(8,128)(2,1)S(1)} custom-call(s32[14]{0:T(128)S(1)} %stack.59.at_ref, f32[1792,512]{1,0:T(8,128)S(1)} %shard_map.69.refs_4_.refs_0_, bf16[512,1024]{1,0:T(8,128)(2,1)S(1)} %collective-permute-done.5.refs_2_.refs_1_, bf16[512,256]{1,0:T(8,128)(2,1)S(1)} %collective-permute-done.16.refs_2_, ...), custom_call_target="tpu_custom_call" | custom-call | flops 1 | bytes 1 | tf_op jit(solution)/shard_map/pallas_call | solution.py:56
  97.1 2.9 %collective-permute-done.20.refs_2_.refs_3_.refs_1_ = bf16[1792,512]{1,0:T(8,128)(2,1)S(1)} collective-permute-done((bf16[1792,512]{1,0:T(8,128)(2,1)S(1)}, bf16[1792,512]{1,0:T(8,128)(2,1)S(1)}, u32[]{:S(2)}, u32[]{:S(2)}) %collective-permute-start.20) | collective-permute-done | bytes 1835040 | tf_op jit(solution)/shard_map/ppermute | solution.py:40
  100.1 3.4 %shard_map.81 = (bf16[7,64,512]{2,1,0:T(8,128)(2,1)S(1)}, bf16[7,64,512]{2,1,0:T(8,128)(2,1)S(1)}, bf16[7,64,512]{2,1,0:T(8,128)(2,1)S(1)}, bf16[7,64,512]{2,1,0:T(8,128)(2,1)S(1)}) custom-call(s32[14]{0:T(128)S(1)} %stack.59.at_ref, bf16[1792,512]{1,0:T(8,128)(2,1)S(1)} %shard_map.80.refs_0_.refs_1_.refs_4_.refs_2_, ...), custom_call_target="tpu_custom_call" | custom-call | flops 1 | bytes 1 | tf_op jit(solution)/shard_map/pallas_call | solution.py:56
  103.5 1.3 collective-permute-start.21
  105.2 1.2 collective-permute-start.23
  106.3 4.9 %collective-permute-done.22.refs_1_ = bf16[128,1792]{1,0:T(8,128)(2,1)S(1)} collective-permute-done((bf16[128,1792]{1,0:T(8,128)(2,1)S(1)}, bf16[128,1792]{1,0:T(8,128)(2,1)S(1)}, u32[]{:S(2)}, u32[]{:S(2)}) %collective-permute-start.22) | collective-permute-done | bytes 458784 | tf_op jit(solution)/shard_map/ppermute | solution.py:40
  112.9 1.3 collective-permute-start.24
  115.3 2.0 %shard_map.83 = (bf16[3584,256]{1,0:T(8,128)(2,1)}, f32[8,128]{1,0:T(8,128)S(1)}) custom-call(s32[14]{0:T(128)S(1)} %stack.59.at_ref, bf16[1792,512]{1,0:T(8,128)(2,1)S(1)} %shard_map.80.refs_0_.refs_1_.refs_4_.refs_2_, bf16[1792,512]{1,0:T(8,128)(2,1)S(1)} %collective-permute-done.20.refs_2_.refs_3_.refs_1_, bf16[128,1792]{1,0:T(8,128)(2,1)S(1)} %shard_map.82.refs_2_.refs_0_), custom_call_target="tpu_custom_call" | custom-call | flops 1 | bytes 1 | tf_op jit(solution)/shard_map/pallas_call | solution.py:56
  117.3 2.4 %shard_map.84 = (f32[256,256]{1,0:T(8,128)S(1)}, bf16[256,256]{1,0:T(8,128)(2,1)S(1)}) custom-call(s32[14]{0:T(128)S(1)} %stack.59.at_ref, bf16[1792,512]{1,0:T(8,128)(2,1)S(1)} %shard_map.80.refs_0_.refs_1_.refs_4_.refs_2_, bf16[1792,512]{1,0:T(8,128)(2,1)S(1)} %collective-permute-done.20.refs_2_.refs_3_.refs_1_, ...), custom_call_target="tpu_custom_call" | custom-call | flops 1 | bytes 1 | tf_op jit(solution)/shard_map/pallas_call | solution.py:56
  121.4 1.8 %collective-permute-start.27 = (bf16[7,64,512]{2,1,0:T(8,128)(2,1)S(1)}, bf16[7,64,512]{2,1,0:T(8,128)(2,1)S(1)}, u32[]{:S(2)}, u32[]{:S(2)}) collective-permute-start(bf16[7,64,512]{2,1,0:T(8,128)(2,1)S(1)} %bitcast.18), channel_id=1, source_target_pairs={{0,192},{1,65},{2,194},{3,67},{32,224},{33,97},{34,226},{35,99},{6... | collective-permute-start | bytes 1376264 | tf_op jit(solution)/shard_map/ppermute | solution.py:40
  123.2 3.0 %collective-permute-done.24.refs_3_.refs_2_ = bf16[128,1792]{1,0:T(8,128)(2,1)S(1)} collective-permute-done((bf16[128,1792]{1,0:T(8,128)(2,1)S(1)}, bf16[128,1792]{1,0:T(8,128)(2,1)S(1)}, u32[]{:S(2)}, u32[]{:S(2)}) %collective-permute-start.24) | collective-permute-done | bytes 458784 | tf_op jit(solution)/shard_map/ppermute | solution.py:40
  127.0 2.1 %collective-permute-start.25 = (bf16[128,1792]{1,0:T(8,128)(2,1)S(1)}, bf16[128,1792]{1,0:T(8,128)(2,1)S(1)}, u32[]{:S(2)}, u32[]{:S(2)}) collective-permute-start(bf16[128,1792]{1,0:T(8,128)(2,1)S(1)} %shard_map.86.refs_0_), channel_id=1, source_target_pairs={{0,192},{1,65},{2,194},{3,67},{32,224},{33,97},{34,226},{35,99},{6... | collective-permute-start | bytes 1376264 | tf_op jit(solution)/shard_map/ppermute | solution.py:40
  129.1 6.3 %collective-permute-start.28 = (bf16[256,256]{1,0:T(8,128)(2,1)S(1)}, bf16[256,256]{1,0:T(8,128)(2,1)S(1)}, u32[]{:S(2)}, u32[]{:S(2)}) collective-permute-start(bf16[256,256]{1,0:T(8,128)(2,1)S(1)} %get-tuple-element.54), channel_id=1, source_target_pairs={{0,16},{4,20},{8,24},{12,28},{16,0},{20,4},{24,8},{28,12},{1,17},{... | collective-permute-start | bytes 393224 | tf_op jit(solution)/shard_map/ppermute | solution.py:428
  135.8 1.7 %collective-permute-start.26 = (bf16[128,1792]{1,0:T(8,128)(2,1)S(1)}, bf16[128,1792]{1,0:T(8,128)(2,1)S(1)}, u32[]{:S(2)}, u32[]{:S(2)}) collective-permute-start(bf16[128,1792]{1,0:T(8,128)(2,1)S(1)} %shard_map.86.refs_0_), channel_id=1, source_target_pairs={{0,64},{1,193},{2,66},{3,195},{32,96},{33,225},{34,98},{35,227},{6... | collective-permute-start | bytes 1376264 | tf_op jit(solution)/shard_map/ppermute | solution.py:40
  137.4 1.4 collective-permute-done.28.refs_1_
  140.8 2.4 %collective-permute-start.29 = (bf16[128,1792]{1,0:T(8,128)(2,1)S(1)}, bf16[128,1792]{1,0:T(8,128)(2,1)S(1)}, u32[]{:S(2)}, u32[]{:S(2)}) collective-permute-start(bf16[128,1792]{1,0:T(8,128)(2,1)S(1)} %shard_map.89), channel_id=1, source_target_pairs={{0,64},{1,193},{2,66},{3,195},{32,96},{33,225},{34,98},{35,227},{6... | collective-permute-start | bytes 1376264 | tf_op jit(solution)/shard_map/ppermute | solution.py:40
  144.9 2.3 %shard_map.90 = (bf16[512,3584]{1,0:T(8,128)(2,1)}, f32[8,128]{1,0:T(8,128)S(1)}) custom-call(s32[14]{0:T(128)S(1)} %stack.59.at_ref, bf16[128,1792]{1,0:T(8,128)(2,1)S(1)} %shard_map.82.refs_2_.refs_0_, bf16[128,1792]{1,0:T(8,128)(2,1)S(1)} %collective-permute-done.30.refs_1_, bf16[128,1792]{1,0:T(8,128)(2,1)S(1)} %collective-permute-done.24.refs_3_.refs_2_, ...), custom_call_target="tpu_custom_call" | custom-call | flops 1 | bytes 1 | tf_op jit(solution)/shard_map/pallas_call | solution.py:56
  147.3 1.8 %collective-permute-done.33.refs_1_ = bf16[128,256]{1,0:T(8,128)(2,1)S(1)} collective-permute-done((bf16[128,256]{1,0:T(8,128)(2,1)S(1)}, bf16[128,256]{1,0:T(8,128)(2,1)S(1)}, u32[]{:S(2)}, u32[]{:S(2)}) %collective-permute-start.33) | collective-permute-done | bytes 65568 | tf_op jit(solution)/shard_map/ppermute | solution.py:428
  150.3 4.7 %collective-permute-start.34 = (bf16[7,16,512]{2,1,0:T(8,128)(2,1)S(1)}, bf16[7,16,512]{2,1,0:T(8,128)(2,1)S(1)}, u32[]{:S(2)}, u32[]{:S(2)}) collective-permute-start(bf16[7,16,512]{2,1,0:T(8,128)(2,1)S(1)} %get-tuple-element.62.refs_5_), channel_id=1, source_target_pairs={{0,32},{1,33},{2,34},{3,35},{32,0},{33,1},{34,2},{35,3},{64,96},{6... | collective-permute-start | bytes 344072 | tf_op jit(solution)/shard_map/ppermute | solution.py:40
  155.0 2.3 %shard_map.93 = (bf16[512,3584]{1,0:T(8,128)(2,1)}, f32[8,128]{1,0:T(8,128)S(1)}) custom-call(s32[14]{0:T(128)S(1)} %stack.59.at_ref, bf16[128,1792]{1,0:T(8,128)(2,1)S(1)} %shard_map.86.refs_0_, bf16[128,1792]{1,0:T(8,128)(2,1)S(1)} %collective-permute-done.25.refs_0_.refs_1_, ...), custom_call_target="tpu_custom_call", output_to_operand_aliasing={{0}: (5, {})} | custom-call | flops 1 | bytes 1 | tf_op jit(solution)/shard_map/pallas_call | solution.py:56
  157.3 1.6 collective-permute-done.35.refs_1_
  158.9 1.2 shard_map.95
  160.0 1.2 shard_map.94
  (64 shorter events, 24.0 us)
Async XLA Ops:
  0.6 8.6 %collective-permute-start.3 = (bf16[512,3584]{1,0:T(8,128)(2,1)}, bf16[512,3584]{1,0:T(8,128)(2,1)}, u32[]{:S(2)}, u32[]{:S(2)}) collective-permute-start(bf16[512,3584]{1,0:T(8,128)(2,1)} %refs_0_.9), channel_id=1, source_target_pairs={{0,1},{1,0},{2,3},{3,2},{32,33},{33,32},{34,35},{35,34},{64,65},{6... | collective-permute-start | bytes 11010056 | tf_op jit(solution)/shard_map/ppermute | solution.py:40
  0.7 8.5 %collective-permute-start.4 = (bf16[512,1024]{1,0:T(8,128)(2,1)}, bf16[512,1024]{1,0:T(8,128)(2,1)S(1)}, u32[]{:S(2)}, u32[]{:S(2)}) collective-permute-start(bf16[512,1024]{1,0:T(8,128)(2,1)} %refs_2_.3), channel_id=1, source_target_pairs={{0,1},{1,0},{2,3},{3,2},{32,33},{33,32},{34,35},{35,34},{64,65},{6... | collective-permute-start | bytes 3145736 | tf_op jit(solution)/shard_map/ppermute | solution.py:40
  1.3 2.0 %copy-start = (bf16[512,3584]{1,0:T(8,128)(2,1)S(1)}, bf16[512,3584]{1,0:T(8,128)(2,1)}, u32[]{:S(2)}) copy-start(bf16[512,3584]{1,0:T(8,128)(2,1)} %refs_0_.9) | copy-start | bytes 11010052
  3.4 3.5 %copy-start.2 = (bf16[3584,256]{1,0:T(8,128)(2,1)S(1)}, bf16[3584,256]{1,0:T(8,128)(2,1)}, u32[]{:S(2)}) copy-start(bf16[3584,256]{1,0:T(8,128)(2,1)} %refs_1_.5) | copy-start | bytes 5505028
  4.0 26.5 %collective-permute-start.5 = (bf16[512,1024]{1,0:T(8,128)(2,1)S(1)}, bf16[512,1024]{1,0:T(8,128)(2,1)S(1)}, u32[]{:S(2)}, u32[]{:S(2)}) collective-permute-start(bf16[512,1024]{1,0:T(8,128)(2,1)S(1)} %shard_map.66.refs_2_), channel_id=1, source_target_pairs={{0,34},{1,35},{2,32},{3,33},{32,2},{33,3},{34,0},{35,1},{64,98},{6... | collective-permute-start | bytes 3145736 | tf_op jit(solution)/shard_map/ppermute | solution.py:40
  6.9 1.4 copy-start.3
  7.0 2.4 %copy-start.1 = (bf16[512,3584]{1,0:T(8,128)(2,1)S(1)}, bf16[512,3584]{1,0:T(8,128)(2,1)}, u32[]{:S(2)}) copy-start(bf16[512,3584]{1,0:T(8,128)(2,1)} %refs_0_.9) | copy-start | bytes 11010052
  7.0 22.2 %collective-permute-start.2 = (bf16[1792,256]{1,0:T(8,128)(2,1)S(1)}, bf16[1792,256]{1,0:T(8,128)(2,1)S(1)}, u32[]{:S(2)}, u32[]{:S(2)}) collective-permute-start(bf16[1792,256]{1,0:T(8,128)(2,1)S(1)} %slice.3), channel_id=1, source_target_pairs={{0,2},{1,3},{2,0},{3,1},{32,34},{33,35},{34,32},{35,33},{64,66},{6... | collective-permute-start | bytes 2752520 | tf_op jit(solution)/shard_map/ppermute | solution.py:40
  7.3 24.0 %collective-permute-start = (bf16[3584,256]{1,0:T(8,128)(2,1)S(1)}, bf16[3584,256]{1,0:T(8,128)(2,1)S(1)}, u32[]{:S(2)}, u32[]{:S(2)}) collective-permute-start(bf16[3584,256]{1,0:T(8,128)(2,1)S(1)} %copy-done.2), channel_id=1, source_target_pairs={{0,1},{1,0},{2,3},{3,2},{32,33},{33,32},{34,35},{35,34},{64,65},{6... | collective-permute-start | bytes 5505032 | tf_op jit(solution)/shard_map/ppermute | solution.py:40
  31.1 2.6 %collective-permute-start.6 = (bf16[1792,256]{1,0:T(8,128)(2,1)S(1)}, bf16[1792,256]{1,0:T(8,128)(2,1)S(1)}, u32[]{:S(2)}, u32[]{:S(2)}) collective-permute-start(bf16[1792,256]{1,0:T(8,128)(2,1)S(1)} %shard_map.71.refs_5_), channel_id=1, source_target_pairs={{0,1},{1,0},{2,3},{3,2},{32,33},{33,32},{34,35},{35,34},{64,65},{6... | collective-permute-start | bytes 2752520 | tf_op jit(solution)/shard_map/ppermute | solution.py:40
  37.0 8.6 %collective-permute-start.8 = (bf16[128,1792]{1,0:T(8,128)(2,1)S(1)}, bf16[128,1792]{1,0:T(8,128)(2,1)S(1)}, u32[]{:S(2)}, u32[]{:S(2)}) collective-permute-start(bf16[128,1792]{1,0:T(8,128)(2,1)S(1)} %get-tuple-element.40), channel_id=1, source_target_pairs={{0,64},{1,193},{2,66},{3,195},{32,96},{33,225},{34,98},{35,227},{6... | collective-permute-start | bytes 1376264 | tf_op jit(solution)/shard_map/ppermute | solution.py:40
  38.6 22.9 %collective-permute-start.1 = (bf16[1792,256]{1,0:T(8,128)(2,1)S(1)}, bf16[1792,256]{1,0:T(8,128)(2,1)S(1)}, u32[]{:S(2)}, u32[]{:S(2)}) collective-permute-start(bf16[1792,256]{1,0:T(8,128)(2,1)S(1)} %get-tuple-element.36.refs_1_), channel_id=1, source_target_pairs={{0,2},{1,3},{2,0},{3,1},{32,34},{33,35},{34,32},{35,33},{64,66},{6... | collective-permute-start | bytes 2752520 | tf_op jit(solution)/shard_map/ppermute | solution.py:40
  38.9 20.7 %collective-permute-start.10 = (bf16[512,768]{1,0:T(8,128)(2,1)S(1)}, bf16[512,768]{1,0:T(8,128)(2,1)S(1)}, u32[]{:S(2)}, u32[]{:S(2)}) collective-permute-start(bf16[512,768]{1,0:T(8,128)(2,1)S(1)} %get-tuple-element.41), channel_id=1, source_target_pairs={{0,35},{1,34},{2,33},{3,32},{32,3},{33,2},{34,1},{35,0},{64,99},{6... | collective-permute-start | bytes 2359304 | tf_op jit(solution)/shard_map/ppermute | solution.py:40
  42.3 9.6 %collective-permute-start.7 = (bf16[128,1792]{1,0:T(8,128)(2,1)S(1)}, bf16[128,1792]{1,0:T(8,128)(2,1)S(1)}, u32[]{:S(2)}, u32[]{:S(2)}) collective-permute-start(bf16[128,1792]{1,0:T(8,128)(2,1)S(1)} %get-tuple-element.38), channel_id=1, source_target_pairs={{0,64},{1,193},{2,66},{3,195},{32,96},{33,225},{34,98},{35,227},{6... | collective-permute-start | bytes 1376264 | tf_op jit(solution)/shard_map/ppermute | solution.py:40
  46.4 9.8 %collective-permute-start.9 = (bf16[128,1792]{1,0:T(8,128)(2,1)S(1)}, bf16[128,1792]{1,0:T(8,128)(2,1)S(1)}, u32[]{:S(2)}, u32[]{:S(2)}) collective-permute-start(bf16[128,1792]{1,0:T(8,128)(2,1)S(1)} %shard_map.73), channel_id=1, source_target_pairs={{0,192},{1,65},{2,194},{3,67},{32,224},{33,97},{34,226},{35,99},{6... | collective-permute-start | bytes 1376264 | tf_op jit(solution)/shard_map/ppermute | solution.py:40
  62.2 2.6 %collective-permute-start.11 = (bf16[1792,256]{1,0:T(8,128)(2,1)S(1)}, bf16[1792,256]{1,0:T(8,128)(2,1)S(1)}, u32[]{:S(2)}, u32[]{:S(2)}) collective-permute-start(bf16[1792,256]{1,0:T(8,128)(2,1)S(1)} %shard_map.75.refs_5_), channel_id=1, source_target_pairs={{0,1},{1,0},{2,3},{3,2},{32,33},{33,32},{34,35},{35,34},{64,65},{6... | collective-permute-start | bytes 2752520 | tf_op jit(solution)/shard_map/ppermute | solution.py:40
  62.4 27.5 %collective-permute-start.18 = (bf16[1024,512]{1,0:T(8,128)(2,1)S(1)}, bf16[1024,512]{1,0:T(8,128)(2,1)S(1)}, u32[]{:S(2)}, u32[]{:S(2)}) collective-permute-start(bf16[1024,512]{1,0:T(8,128)(2,1)S(1)} %shard_map.70.refs_1_), channel_id=1, source_target_pairs={{0,2},{1,3},{2,0},{3,1},{32,34},{33,35},{34,32},{35,33},{64,66},{6... | collective-permute-start | bytes 3145736 | tf_op jit(solution)/shard_map/ppermute | solution.py:40
  68.0 8.6 %collective-permute-start.13 = (bf16[128,1792]{1,0:T(8,128)(2,1)S(1)}, bf16[128,1792]{1,0:T(8,128)(2,1)S(1)}, u32[]{:S(2)}, u32[]{:S(2)}) collective-permute-start(bf16[128,1792]{1,0:T(8,128)(2,1)S(1)} %get-tuple-element.45), channel_id=1, source_target_pairs={{0,64},{1,193},{2,66},{3,195},{32,96},{33,225},{34,98},{35,227},{6... | collective-permute-start | bytes 1376264 | tf_op jit(solution)/shard_map/ppermute | solution.py:40
  68.9 21.1 %collective-permute-start.17 = (bf16[512,512]{1,0:T(8,128)(2,1)S(1)}, bf16[512,512]{1,0:T(8,128)(2,1)S(1)}, u32[]{:S(2)}, u32[]{:S(2)}) collective-permute-start(bf16[512,512]{1,0:T(8,128)(2,1)S(1)} %get-tuple-element.47), channel_id=1, source_target_pairs={{0,35},{1,34},{2,33},{3,32},{32,3},{33,2},{34,1},{35,0},{64,99},{6... | collective-permute-start | bytes 1572872 | tf_op jit(solution)/shard_map/ppermute | solution.py:40
  71.4 11.0 %collective-permute-start.12 = (bf16[128,1792]{1,0:T(8,128)(2,1)S(1)}, bf16[128,1792]{1,0:T(8,128)(2,1)S(1)}, u32[]{:S(2)}, u32[]{:S(2)}) collective-permute-start(bf16[128,1792]{1,0:T(8,128)(2,1)S(1)} %get-tuple-element.43), channel_id=1, source_target_pairs={{0,64},{1,193},{2,66},{3,195},{32,96},{33,225},{34,98},{35,227},{6... | collective-permute-start | bytes 1376264 | tf_op jit(solution)/shard_map/ppermute | solution.py:40
  77.4 9.8 %collective-permute-start.14 = (bf16[128,1792]{1,0:T(8,128)(2,1)S(1)}, bf16[128,1792]{1,0:T(8,128)(2,1)S(1)}, u32[]{:S(2)}, u32[]{:S(2)}) collective-permute-start(bf16[128,1792]{1,0:T(8,128)(2,1)S(1)} %shard_map.77), channel_id=1, source_target_pairs={{0,192},{1,65},{2,194},{3,67},{32,224},{33,97},{34,226},{35,99},{6... | collective-permute-start | bytes 1376264 | tf_op jit(solution)/shard_map/ppermute | solution.py:40
  78.6 11.4 %collective-permute-start.16 = (bf16[512,256]{1,0:T(8,128)(2,1)S(1)}, bf16[512,256]{1,0:T(8,128)(2,1)S(1)}, u32[]{:S(2)}, u32[]{:S(2)}) collective-permute-start(bf16[512,256]{1,0:T(8,128)(2,1)S(1)} %get-tuple-element.46), channel_id=1, source_target_pairs={{0,34},{1,35},{2,32},{3,33},{32,2},{33,3},{34,0},{35,1},{64,98},{6... | collective-permute-start | bytes 786440 | tf_op jit(solution)/shard_map/ppermute | solution.py:40
  90.6 2.0 %collective-permute-start.19 = (bf16[512,512]{1,0:T(8,128)(2,1)S(1)}, bf16[512,512]{1,0:T(8,128)(2,1)S(1)}, u32[]{:S(2)}, u32[]{:S(2)}) collective-permute-start(bf16[512,512]{1,0:T(8,128)(2,1)S(1)} %shard_map.79), channel_id=1, source_target_pairs={{0,1},{1,0},{2,3},{3,2},{32,33},{33,32},{34,35},{35,34},{64,65},{6... | collective-permute-start | bytes 1572872 | tf_op jit(solution)/shard_map/ppermute | solution.py:40
  96.2 3.9 %collective-permute-start.20 = (bf16[1792,512]{1,0:T(8,128)(2,1)S(1)}, bf16[1792,512]{1,0:T(8,128)(2,1)S(1)}, u32[]{:S(2)}, u32[]{:S(2)}) collective-permute-start(bf16[1792,512]{1,0:T(8,128)(2,1)S(1)} %shard_map.80.refs_0_.refs_1_.refs_4_.refs_2_), channel_id=1, source_target_pairs={{0,1},{1,0},{2,3},{3,2},{32,33},{33,32},{34,35},{35,34},{64,65},{6... | collective-permute-start | bytes 5505032 | tf_op jit(solution)/shard_map/ppermute | solution.py:40
  96.4 14.9 %collective-permute-start.22 = (bf16[128,1792]{1,0:T(8,128)(2,1)S(1)}, bf16[128,1792]{1,0:T(8,128)(2,1)S(1)}, u32[]{:S(2)}, u32[]{:S(2)}) collective-permute-start(bf16[128,1792]{1,0:T(8,128)(2,1)S(1)} %shard_map.74.refs_1_.refs_8_.refs_0_), channel_id=1, source_target_pairs={{0,32},{1,33},{2,34},{3,35},{32,0},{33,1},{34,2},{35,3},{64,96},{6... | collective-permute-start | bytes 1376264 | tf_op jit(solution)/shard_map/ppermute | solution.py:40
  103.5 8.6 %collective-permute-start.21 = (bf16[7,64,512]{2,1,0:T(8,128)(2,1)S(1)}, bf16[7,64,512]{2,1,0:T(8,128)(2,1)S(1)}, u32[]{:S(2)}, u32[]{:S(2)}) collective-permute-start(bf16[7,64,512]{2,1,0:T(8,128)(2,1)S(1)} %get-tuple-element.49), channel_id=1, source_target_pairs={{0,64},{1,193},{2,66},{3,195},{32,96},{33,225},{34,98},{35,227},{6... | collective-permute-start | bytes 1376264 | tf_op jit(solution)/shard_map/ppermute | solution.py:40
  104.9 15.7 %collective-permute-start.15 = (bf16[128,1792]{1,0:T(8,128)(2,1)S(1)}, bf16[128,1792]{1,0:T(8,128)(2,1)S(1)}, u32[]{:S(2)}, u32[]{:S(2)}) collective-permute-start(bf16[128,1792]{1,0:T(8,128)(2,1)S(1)} %shard_map.78.refs_1_.refs_9_.refs_0_), channel_id=1, source_target_pairs={{0,32},{1,33},{2,34},{3,35},{32,0},{33,1},{34,2},{35,3},{64,96},{6... | collective-permute-start | bytes 1376264 | tf_op jit(solution)/shard_map/ppermute | solution.py:40
  105.2 15.4 %collective-permute-start.23 = (bf16[7,64,512]{2,1,0:T(8,128)(2,1)S(1)}, bf16[7,64,512]{2,1,0:T(8,128)(2,1)S(1)}, u32[]{:S(2)}, u32[]{:S(2)}) collective-permute-start(bf16[7,64,512]{2,1,0:T(8,128)(2,1)S(1)} %get-tuple-element.52), channel_id=1, source_target_pairs={{0,64},{1,193},{2,66},{3,195},{32,96},{33,225},{34,98},{35,227},{6... | collective-permute-start | bytes 1376264 | tf_op jit(solution)/shard_map/ppermute | solution.py:40
  112.9 13.3 %collective-permute-start.24 = (bf16[128,1792]{1,0:T(8,128)(2,1)S(1)}, bf16[128,1792]{1,0:T(8,128)(2,1)S(1)}, u32[]{:S(2)}, u32[]{:S(2)}) collective-permute-start(bf16[128,1792]{1,0:T(8,128)(2,1)S(1)} %shard_map.82.refs_2_.refs_0_), channel_id=1, source_target_pairs={{0,64},{1,193},{2,66},{3,195},{32,96},{33,225},{34,98},{35,227},{6... | collective-permute-start | bytes 1376264 | tf_op jit(solution)/shard_map/ppermute | solution.py:40
  114.3 21.2 %collective-permute-start.30 = (bf16[128,1792]{1,0:T(8,128)(2,1)S(1)}, bf16[128,1792]{1,0:T(8,128)(2,1)S(1)}, u32[]{:S(2)}, u32[]{:S(2)}) collective-permute-start(bf16[128,1792]{1,0:T(8,128)(2,1)S(1)} %shard_map.82.refs_2_.refs_0_), channel_id=1, source_target_pairs={{0,192},{1,65},{2,194},{3,67},{32,224},{33,97},{34,226},{35,99},{6... | collective-permute-start | bytes 1376264 | tf_op jit(solution)/shard_map/ppermute | solution.py:40
  121.4 18.1 %collective-permute-start.27 = (bf16[7,64,512]{2,1,0:T(8,128)(2,1)S(1)}, bf16[7,64,512]{2,1,0:T(8,128)(2,1)S(1)}, u32[]{:S(2)}, u32[]{:S(2)}) collective-permute-start(bf16[7,64,512]{2,1,0:T(8,128)(2,1)S(1)} %bitcast.18), channel_id=1, source_target_pairs={{0,192},{1,65},{2,194},{3,67},{32,224},{33,97},{34,226},{35,99},{6... | collective-permute-start | bytes 1376264 | tf_op jit(solution)/shard_map/ppermute | solution.py:40
  127.0 13.2 %collective-permute-start.25 = (bf16[128,1792]{1,0:T(8,128)(2,1)S(1)}, bf16[128,1792]{1,0:T(8,128)(2,1)S(1)}, u32[]{:S(2)}, u32[]{:S(2)}) collective-permute-start(bf16[128,1792]{1,0:T(8,128)(2,1)S(1)} %shard_map.86.refs_0_), channel_id=1, source_target_pairs={{0,192},{1,65},{2,194},{3,67},{32,224},{33,97},{34,226},{35,99},{6... | collective-permute-start | bytes 1376264 | tf_op jit(solution)/shard_map/ppermute | solution.py:40
  129.1 9.7 %collective-permute-start.28 = (bf16[256,256]{1,0:T(8,128)(2,1)S(1)}, bf16[256,256]{1,0:T(8,128)(2,1)S(1)}, u32[]{:S(2)}, u32[]{:S(2)}) collective-permute-start(bf16[256,256]{1,0:T(8,128)(2,1)S(1)} %get-tuple-element.54), channel_id=1, source_target_pairs={{0,16},{4,20},{8,24},{12,28},{16,0},{20,4},{24,8},{28,12},{1,17},{... | collective-permute-start | bytes 393224 | tf_op jit(solution)/shard_map/ppermute | solution.py:428
  135.4 9.5 %collective-permute-start.31 = (bf16[128,1792]{1,0:T(8,128)(2,1)S(1)}, bf16[128,1792]{1,0:T(8,128)(2,1)S(1)}, u32[]{:S(2)}, u32[]{:S(2)}) collective-permute-start(bf16[128,1792]{1,0:T(8,128)(2,1)S(1)} %collective-permute-done.30.refs_1_), channel_id=1, source_target_pairs={{0,64},{1,193},{2,66},{3,195},{32,96},{33,225},{34,98},{35,227},{6... | collective-permute-start | bytes 1376264 | tf_op jit(solution)/shard_map/ppermute | solution.py:40
  135.8 13.9 %collective-permute-start.26 = (bf16[128,1792]{1,0:T(8,128)(2,1)S(1)}, bf16[128,1792]{1,0:T(8,128)(2,1)S(1)}, u32[]{:S(2)}, u32[]{:S(2)}) collective-permute-start(bf16[128,1792]{1,0:T(8,128)(2,1)S(1)} %shard_map.86.refs_0_), channel_id=1, source_target_pairs={{0,64},{1,193},{2,66},{3,195},{32,96},{33,225},{34,98},{35,227},{6... | collective-permute-start | bytes 1376264 | tf_op jit(solution)/shard_map/ppermute | solution.py:40
  140.8 14.1 %collective-permute-start.29 = (bf16[128,1792]{1,0:T(8,128)(2,1)S(1)}, bf16[128,1792]{1,0:T(8,128)(2,1)S(1)}, u32[]{:S(2)}, u32[]{:S(2)}) collective-permute-start(bf16[128,1792]{1,0:T(8,128)(2,1)S(1)} %shard_map.89), channel_id=1, source_target_pairs={{0,64},{1,193},{2,66},{3,195},{32,96},{33,225},{34,98},{35,227},{6... | collective-permute-start | bytes 1376264 | tf_op jit(solution)/shard_map/ppermute | solution.py:40
  143.2 6.4 %collective-permute-start.32 = (bf16[7,32,512]{2,1,0:T(8,128)(2,1)S(1)}, bf16[7,32,512]{2,1,0:T(8,128)(2,1)S(1)}, u32[]{:S(2)}, u32[]{:S(2)}) collective-permute-start(bf16[7,32,512]{2,1,0:T(8,128)(2,1)S(1)} %get-tuple-element.56.refs_1_), channel_id=1, source_target_pairs={{0,2},{1,3},{2,0},{3,1},{32,34},{33,35},{34,32},{35,33},{64,66},{6... | collective-permute-start | bytes 688136 | tf_op jit(solution)/shard_map/ppermute | solution.py:40
  143.9 5.2 %collective-permute-start.33 = (bf16[128,256]{1,0:T(8,128)(2,1)S(1)}, bf16[128,256]{1,0:T(8,128)(2,1)S(1)}, u32[]{:S(2)}, u32[]{:S(2)}) collective-permute-start(bf16[128,256]{1,0:T(8,128)(2,1)S(1)} %get-tuple-element.59), channel_id=1, source_target_pairs={{0,8},{4,12},{8,0},{12,4},{16,24},{20,28},{24,16},{28,20},{1,9},{5... | collective-permute-start | bytes 196616 | tf_op jit(solution)/shard_map/ppermute | solution.py:428
  150.3 9.7 %collective-permute-start.34 = (bf16[7,16,512]{2,1,0:T(8,128)(2,1)S(1)}, bf16[7,16,512]{2,1,0:T(8,128)(2,1)S(1)}, u32[]{:S(2)}, u32[]{:S(2)}) collective-permute-start(bf16[7,16,512]{2,1,0:T(8,128)(2,1)S(1)} %get-tuple-element.62.refs_5_), channel_id=1, source_target_pairs={{0,32},{1,33},{2,34},{3,35},{32,0},{33,1},{34,2},{35,3},{64,96},{6... | collective-permute-start | bytes 344072 | tf_op jit(solution)/shard_map/ppermute | solution.py:40
  154.9 3.9 %collective-permute-start.35 = (bf16[64,256]{1,0:T(8,128)(2,1)S(1)}, bf16[64,256]{1,0:T(8,128)(2,1)S(1)}, u32[]{:S(2)}, u32[]{:S(2)}) collective-permute-start(bf16[64,256]{1,0:T(8,128)(2,1)S(1)} %get-tuple-element.67), channel_id=1, source_target_pairs={{0,4},{4,0},{8,12},{12,8},{16,20},{20,16},{24,28},{28,24},{1,5},{5... | collective-permute-start | bytes 98312 | tf_op jit(solution)/shard_map/ppermute | solution.py:428
